TPU v7x, 256 devices: a whole 4x4x8 slice. The times are simulated.
256 devices in a mesh: lat: 64 (over z, y, x_hi), lon: 4 (over x_lo, core).
Axes of the slice: x: 4 (x_hi: 2, x_lo: 2; x = x_hi * 2 + x_lo), y: 4, z: 8, core: 2. Of those that a mesh axis runs over, the one named last changes fastest.
Arguments:
- tokens: bfloat16 [192, 256, 512], P('lat', 'lon'), may hold values from -6 to 6
- ocean_count: int32 [192, 4], P('lat', 'lon'), may hold values from 1 to 64
- w_qkv: bfloat16 [512, 1536], replicated, may hold values from -0.25 to 0.25
- w_out: bfloat16 [512, 512], replicated, may hold values from -0.25 to 0.25
- w_up: bfloat16 [512, 1024], replicated, may hold values from -0.25 to 0.25
- w_down: bfloat16 [1024, 512], replicated, may hold values from -0.1875 to 0.1875
- cotangent: bfloat16 [192, 256, 512], P('lat', 'lon'), may hold values from -6 to 6
Outputs:
- block_out: bfloat16 [192, 256, 512], P('lat', 'lon')
- grad_tokens: bfloat16 [192, 256, 512], P('lat', 'lon')
- grad_qkv: float32 [512, 1536], P('lat')
- grad_out: float32 [512, 512], P('lat')
- grad_up: float32 [512, 1024], P('lat')
- grad_down: float32 [1024, 512], P('lat')
Inputs may be any that keep to these rules, and one draw needn't show every extreme that they name: The ocean patches of row r in sector s are that sector's first ocean_count[r, s] positions; the others are land.
All inputs are finite; a program needn't handle non-finite values.
Results may differ from a plain program's by a relative error of at most 0.023.
Values may be sent and summed in bfloat16 or wider, within the bound.
No kernel may reach another device: no remote copies, remote signals or barrier semaphores. Data moves between devices by JAX's collectives and lax.ppermute only.
A program may use at most 64 MiB of HBM per device.

v0:
```python
import math

import jax
import jax.numpy as jnp
from jax import lax
from jax.sharding import PartitionSpec as P

HEAD_DIM = 64


SOFTMAX_SCALE = 8.0


def widen(values):
    return lax.optimization_barrier(values).astype(jnp.float32)


def elementwise_product(pattern, left_side, right_side):
    return jnp.einsum(pattern, left_side, right_side, preferred_element_type=jnp.float32)


def flatten(values):
    return values.reshape(-1, values.shape[-1])


def layer_norm(values):
    average = jnp.mean(values, axis=-1, keepdims=True)
    centered = values - average
    variance = jnp.mean(centered * centered, axis=-1, keepdims=True)
    return centered * lax.rsqrt(variance + 1e-05)


def split_heads(values, head_count):
    return values.reshape(values.shape[:-1] + (head_count, values.shape[-1] // head_count))


def head_norm(values, head_count):
    shaped = split_heads(values, head_count)
    scaled = shaped * lax.rsqrt(jnp.mean(shaped * shaped, axis=-1, keepdims=True) + 1e-06)
    return scaled.reshape(values.shape)


def project_in(tokens, w_qkv, head_count):
    model_width = tokens.shape[-1]
    normed = layer_norm(tokens.astype(jnp.float32)).astype(jnp.bfloat16)
    projected = elementwise_product("...d,de->...e", normed, w_qkv)
    query_raw = projected[..., :model_width]
    key_raw = projected[..., model_width : 2 * model_width]
    query_b = head_norm(query_raw, head_count).astype(jnp.bfloat16)
    key_value = jnp.concatenate(
        [head_norm(key_raw, head_count), projected[..., 2 * model_width :]], axis=-1
    ).astype(jnp.bfloat16)
    return (normed, query_b, key_value, query_raw, key_raw)


def row_scores(query_b, key_value, key_land_mask, head_count):
    model_width = query_b.shape[-1]
    head_features = model_width // head_count
    query_per_head = split_heads(query_b, head_count)
    key_per_head = split_heads(key_value[:, :model_width], head_count)
    unmasked_logits = elementwise_product("mvp,lvp->vml", query_per_head, key_per_head) * (
        SOFTMAX_SCALE / head_features
    )
    return (
        jnp.exp(unmasked_logits - SOFTMAX_SCALE) * key_land_mask.astype(jnp.float32)[None, None, :]
    )


def attend_row(query_b, key_value, key_land_mask, head_count):
    model_width = query_b.shape[-1]
    expscore = row_scores(query_b, key_value, key_land_mask, head_count)
    value_heads = split_heads(key_value[:, model_width:], head_count)
    numerator = elementwise_product("hqk,khc->qhc", expscore.astype(jnp.bfloat16), value_heads)
    row_total = jnp.transpose(jnp.sum(expscore, axis=-1))
    return (numerator.reshape(numerator.shape[0], model_width), row_total)


def attend_row_back(
    query_b, key_value, key_land_mask, row_total, grad_b, gradient_correction, head_count
):
    model_width = query_b.shape[-1]
    head_features = model_width // head_count
    expscore = row_scores(query_b, key_value, key_land_mask, head_count)
    row_attention_weight = expscore / jnp.transpose(row_total)[:, :, None]
    query_per_head = split_heads(query_b, head_count)
    key_per_head = split_heads(key_value[:, :model_width], head_count)
    value_heads = split_heads(key_value[:, model_width:], head_count)
    grad_heads = split_heads(grad_b, head_count)
    gradient_weights = elementwise_product("mvp,lvp->vml", grad_heads, value_heads)
    gradient_logits = (
        row_attention_weight
        * (gradient_weights - jnp.transpose(gradient_correction)[:, :, None])
        * (SOFTMAX_SCALE / head_features)
    ).astype(jnp.bfloat16)
    grad_query = elementwise_product("hqk,khc->qhc", gradient_logits, key_per_head).reshape(
        -1, model_width
    )
    grad_key = elementwise_product("hqk,qhc->khc", gradient_logits, query_per_head).reshape(
        -1, model_width
    )
    grad_value = elementwise_product(
        "hqk,qhc->khc", row_attention_weight.astype(jnp.bfloat16), grad_heads
    ).reshape(-1, model_width)
    return (grad_query, jnp.concatenate([grad_key, grad_value], axis=-1))


def forward_tail(tokens, attended_b, ocean_mask, w_out, w_up, w_down):
    middle = tokens.astype(jnp.float32) + ocean_mask[..., None] * elementwise_product(
        "...d,de->...e", attended_b, w_out
    )
    normed_two = layer_norm(middle).astype(jnp.bfloat16)
    lifted = elementwise_product("...d,df->...f", normed_two, w_up)
    active = jax.nn.gelu(lifted).astype(jnp.bfloat16)
    block_out = (
        middle + ocean_mask[..., None] * elementwise_product("...f,fd->...d", active, w_down)
    ).astype(jnp.bfloat16)
    return (block_out, (middle, normed_two, lifted, active))


def backward_tail(cotangent, ocean_mask, attended_b, tail_saved, w_out, w_up, w_down):
    middle, normed_two, lifted, active = tail_saved
    upstream = cotangent.astype(jnp.float32)
    grad_branch = (ocean_mask[..., None] * upstream).astype(jnp.bfloat16)
    grad_active = elementwise_product("...d,fd->...f", grad_branch, w_down)
    grad_lifted = jax.vjp(jax.nn.gelu, lifted)[1](grad_active)[0].astype(jnp.bfloat16)
    grad_normed = elementwise_product("...f,df->...d", grad_lifted, w_up)
    grad_middle = upstream + jax.vjp(layer_norm, middle)[1](grad_normed)[0]
    grad_attn = (ocean_mask[..., None] * grad_middle).astype(jnp.bfloat16)
    grad_attended = elementwise_product("...e,de->...d", grad_attn, w_out).astype(jnp.bfloat16)
    term_out = elementwise_product("td,te->de", flatten(attended_b), flatten(grad_attn))
    term_up = elementwise_product("td,tf->df", flatten(normed_two), flatten(grad_lifted))
    term_down = elementwise_product("tf,td->fd", flatten(active), flatten(grad_branch))
    return (grad_middle, grad_attended, (term_out, term_up, term_down))


def backward_head(
    tokens, normed, query_raw, key_raw, grad_query, grad_kv, grad_middle, w_qkv, head_count
):
    model_width = tokens.shape[-1]
    grad_qraw = jax.vjp(lambda values: head_norm(values, head_count), query_raw)[1](grad_query)[0]
    grad_kraw = jax.vjp(lambda values: head_norm(values, head_count), key_raw)[1](
        grad_kv[..., :model_width]
    )[0]
    grad_projected = jnp.concatenate(
        [grad_qraw, grad_kraw, grad_kv[..., model_width:]], axis=-1
    ).astype(jnp.bfloat16)
    term_qkv = elementwise_product("td,te->de", flatten(normed), flatten(grad_projected))
    grad_normed = elementwise_product("...e,de->...d", grad_projected, w_qkv)
    grad_layer = jax.vjp(layer_norm, tokens.astype(jnp.float32))[1](grad_normed)[0]
    return ((grad_middle + grad_layer).astype(jnp.bfloat16), term_qkv)


def local(tokens, ocean_count, w_qkv, w_out, w_up, w_down, cotangent):
    band_rows, local_len, model_width = tokens.shape
    head_count = model_width // HEAD_DIM
    ocean_mask = (lax.broadcasted_iota(jnp.int32, (band_rows, local_len), 1) < ocean_count).astype(
        jnp.float32
    )
    key_land_mask = ocean_mask.astype(jnp.bfloat16)
    normed, query_b, key_value, query_raw, key_raw = project_in(tokens, w_qkv, head_count)
    part_numerator, part_total = lax.map(
        lambda row_items: attend_row(row_items[0], row_items[1], row_items[2], head_count),
        (
            query_b,
            lax.all_gather(key_value, "lon", axis=1, tiled=True),
            lax.all_gather(key_land_mask, "lon", axis=1, tiled=True),
        ),
    )
    attended = (split_heads(part_numerator, head_count) / part_total[..., None]).reshape(
        band_rows, local_len, model_width
    )
    attended_b = attended.astype(jnp.bfloat16)
    block_out, tail_saved = forward_tail(tokens, attended_b, ocean_mask, w_out, w_up, w_down)
    grad_middle, grad_attended, tail_terms = backward_tail(
        cotangent, ocean_mask, attended_b, tail_saved, w_out, w_up, w_down
    )
    gradient_correction = jnp.sum(split_heads(widen(grad_attended) * attended, head_count), axis=-1)
    keys_all, masks_all = (
        lax.all_gather(key_value, "lon", axis=1, tiled=True),
        lax.all_gather(key_land_mask, "lon", axis=1, tiled=True),
    )
    grad_query, kv_terms = lax.map(
        lambda row_items: attend_row_back(
            row_items[0],
            row_items[1],
            row_items[2],
            row_items[3],
            row_items[4],
            row_items[5],
            head_count,
        ),
        (query_b, keys_all, masks_all, part_total, grad_attended, gradient_correction),
    )
    grad_kv = lax.psum_scatter(
        kv_terms.astype(jnp.bfloat16), "lon", scatter_dimension=1, tiled=True
    ).astype(jnp.float32)
    grad_tokens, term_qkv = backward_head(
        tokens, normed, query_raw, key_raw, grad_query, grad_kv, grad_middle, w_qkv, head_count
    )
    grad_scale = 1.0 / math.sqrt(
        band_rows * lax.axis_size("lat") * local_len * lax.axis_size("lon")
    )
    grad_terms = (
        term_qkv * grad_scale,
        tail_terms[0] * grad_scale,
        tail_terms[1] * grad_scale,
        tail_terms[2] * grad_scale,
    )
    band_parts = (
        lax.psum_scatter(grad_terms[0], "lat", scatter_dimension=0, tiled=True),
        lax.psum_scatter(grad_terms[1], "lat", scatter_dimension=0, tiled=True),
        lax.psum_scatter(grad_terms[2], "lat", scatter_dimension=0, tiled=True),
        lax.psum_scatter(grad_terms[3], "lat", scatter_dimension=0, tiled=True),
    )
    summed = (
        lax.psum(band_parts[0].astype(jnp.bfloat16), "lon").astype(jnp.float32),
        lax.psum(band_parts[1].astype(jnp.bfloat16), "lon").astype(jnp.float32),
        lax.psum(band_parts[2].astype(jnp.bfloat16), "lon").astype(jnp.float32),
        lax.psum(band_parts[3].astype(jnp.bfloat16), "lon").astype(jnp.float32),
    )
    return (block_out, grad_tokens, summed[0], summed[1], summed[2], summed[3])


def solution(mesh):
    in_specs = (P("lat", "lon", None), P("lat", "lon"), P(), P(), P(), P(), P("lat", "lon", None))
    out_specs = (
        P("lat", "lon", None),
        P("lat", "lon", None),
        P("lat", None),
        P("lat", None),
        P("lat", None),
        P("lat", None),
    )
    return jax.shard_map(local, mesh=mesh, in_specs=in_specs, out_specs=out_specs, check_vma=False)
```

profile of v0, /device:TPU:1, one launch (start us, length us, event | category | flops | bytes accessed | tf_op | source)
XLA Modules:
  0.0 2079.0 jit_solution(15939667157180536637)
XLA Ops:
  10.1 1.5 fusion.20
  27.6 8.1 all-gather
  35.8 22.8 %all-gather.3.cloned.1.call-done = bf16[3,256,1024]{2,1,0:T(8,128)(2,1)} async-done(((bf16[3,64,1024]{2,1,0:T(8,128)(2,1)}), bf16[3,256,1024]{2,1,0:T(8,128)(2,1)}) %all-gather.3.cloned.1.call-update) | async-done | bytes 1572880 | tf_op jit(solution)/shard_map/all_gather | solution.py:165
  58.6 2.6 copy.91
  61.2 8.6 while.28
  84.0 18.4 while.29
  104.9 1.9 bitcast_multiply_fusion.1
  108.0 1.9 bitcast_multiply_fusion
  111.2 1.9 slice_multiply_fusion
  113.1 2.1 mul.368
  115.2 1.4 reduce_sum.143
  118.0 2.2 broadcast_in_dim.81
  120.1 9.7 reduce-scatter.6.cloned.1.call-done
  129.9 2.4 fusion.52
  132.3 2.1 mul.374
  137.2 2.2 broadcast_in_dim.83
  142.4 2.4 fusion.17
  145.9 2.3 fusion.25
  148.2 297.2 %reduce-scatter.10.cloned.1.call-done = f32[8,512]{1,0:T(8,128)} async-done(((f32[512,512]{1,0:T(8,128)}), f32[8,512]{1,0:T(8,128)}) %reduce-scatter.10.cloned.1.call-update) | async-done | bytes 16400 | tf_op jit(solution)/shard_map/reduce_scatter | solution.py:211
  446.8 1.8 fusion.51
  448.9 360.8 %reduce-scatter.12.cloned.1.call-done = f32[8,1024]{1,0:T(8,128)} async-done(((f32[512,1024]{1,0:T(8,128)}), f32[8,1024]{1,0:T(8,128)}) %reduce-scatter.12.cloned.1.call-update) | async-done | bytes 32784 | tf_op jit(solution)/shard_map/reduce_scatter | solution.py:212
  811.0 360.0 %reduce-scatter.14.cloned.1.call-done = f32[16,512]{1,0:T(8,128)} async-done(((f32[1024,512]{1,0:T(8,128)}), f32[16,512]{1,0:T(8,128)}) %reduce-scatter.14.cloned.1.call-update) | async-done | bytes 32784 | tf_op jit(solution)/shard_map/reduce_scatter | solution.py:213
  1172.3 847.9 %reduce-scatter.8.cloned.1.call-done = f32[8,1536]{1,0:T(8,128)} async-done(((f32[512,1536]{1,0:T(8,128)}), f32[8,1536]{1,0:T(8,128)}) %reduce-scatter.8.cloned.1.call-update) | async-done | bytes 49168 | tf_op jit(solution)/shard_map/reduce_scatter | solution.py:210
  2022.6 44.2 %all-reduce.3.cloned.1.call-done = (bf16[8,1536]{1,0:T(8,128)(2,1)}, bf16[8,512]{1,0:T(8,128)(2,1)}, bf16[8,1024]{1,0:T(8,128)(2,1)}, bf16[16,512]{1,0:T(8,128)(2,1)}) async-done(((bf16[8,1536]{1,0:T(8,128)(2,1)}, bf16[8,512]{1,0:T(8,128)(2,1)}, bf16[8,1024]{1,0:T(8,128)(2,1)}, bf16[16,512]{1,0:T(8,128)(2,1)}), (bf16[8,1536]{1,0:T(8,128)(2,1)}, bf16[8,512]{1,0:T(8,128)(2,1)}, bf16[8,1024]{1,0:T(8,128)(2,1)}, ...) | async-done | bytes 65552 | tf_op jit(solution)/shard_map/psum | solution.py:216
  (252 shorter events, 84.6 us)
Async XLA Ops:
  7.2 51.4 %all-gather.3.cloned.1.call-start = ((), (), s32[]{:S(2)}) async-start(), calls=%async_computation.5 | async-start | bytes 1966080 | tf_op jit(solution)/shard_map/all_gather | solution.py:165
  8.4 3.2 copy-start.33
  11.6 13.3 copy-start.1
  15.5 4.3 copy-start.16
  19.7 41.5 %copy-start.10 = (f32[3,64,512]{2,1,0:T(8,128)}, f32[3,64,512]{2,1,0:T(8,128)S(1)}, u32[]{:S(2)}) copy-start(f32[3,64,512]{2,1,0:T(8,128)S(1)} %mul.336) | copy-start | bytes 1179652
  24.9 36.3 %copy-start.9 = (f32[3,64,512]{2,1,0:T(8,128)}, f32[3,64,512]{2,1,0:T(8,128)S(1)}, u32[]{:S(2)}) copy-start(f32[3,64,512]{2,1,0:T(8,128)S(1)} %mul.331) | copy-start | bytes 1179652
  26.9 103.0 %reduce-scatter.6.cloned.1.call-start = ((), (), s32[]{:S(2)}) async-start(), calls=%async_computation.6 | async-start | bytes 1966080 | tf_op jit(solution)/shard_map/reduce_scatter | solution.py:194
  71.4 3.4 copy-start.3
  71.4 3.4 copy-start.11
  71.4 3.4 copy-start.37
  74.8 4.8 copy-start.4
  78.4 3.3 copy-start.7
  102.5 343.0 %reduce-scatter.10.cloned.1.call-start = ((), (), s32[]{:S(2)}) async-start(), calls=%async_computation.8 | async-start | bytes 1064960 | tf_op jit(solution)/shard_map/reduce_scatter | solution.py:211
  104.9 704.8 %reduce-scatter.12.cloned.1.call-start = ((), (), s32[]{:S(2)}) async-start(), calls=%async_computation.9 | async-start | bytes 2129920 | tf_op jit(solution)/shard_map/reduce_scatter | solution.py:212
  106.9 1064.1 %reduce-scatter.14.cloned.1.call-start = ((), (), s32[]{:S(2)}) async-start(), calls=%async_computation.10 | async-start | bytes 2129920 | tf_op jit(solution)/shard_map/reduce_scatter | solution.py:213
  109.9 1910.3 %reduce-scatter.8.cloned.1.call-start = ((), (), s32[]{:S(2)}) async-start(), calls=%async_computation.7 | async-start | bytes 3194880 | tf_op jit(solution)/shard_map/reduce_scatter | solution.py:210
  111.2 5.5 copy-start.31
  137.2 5.2 copy-start.34
  137.2 5.2 copy-start.36
  139.4 3.1 copy-start.29
  144.8 301.9 %copy-start.27 = (bf16[3,64,512]{2,1,0:T(8,128)(2,1)S(1)}, bf16[3,64,512]{2,1,0:T(8,128)(2,1)}, u32[]{:S(2)}) copy-start(bf16[3,64,512]{2,1,0:T(8,128)(2,1)} %copy-done.26) | copy-start | bytes 589828
  144.8 1922.0 %all-reduce.3.cloned.1.call-start = ((), (), s32[]{:S(2)}) async-start(), calls=%async_computation.11 | async-start | bytes 131072 | tf_op jit(solution)/shard_map/psum | solution.py:216
  446.8 1574.9 %copy-start.8 = (f32[3,64,512]{2,1,0:T(8,128)S(1)}, f32[3,64,512]{2,1,0:T(8,128)}, u32[]{:S(2)}) copy-start(f32[3,64,512]{2,1,0:T(8,128)} %copy-done.7) | copy-start | bytes 1179652
  446.8 1574.9 %copy-start.25 = (bf16[3,64,512]{2,1,0:T(8,128)(2,1)S(1)}, bf16[3,64,512]{2,1,0:T(8,128)(2,1)}, u32[]{:S(2)}) copy-start(bf16[3,64,512]{2,1,0:T(8,128)(2,1)} %param.17) | copy-start | bytes 589828
  (25 other events, 33.3 us)
Sparse Core Ops, SparseCore 0:
  27.0 31.5 all-gather.2
  102.6 27.2 reduce-scatter.5
  132.4 313.0 reduce-scatter.9
  447.9 361.6 reduce-scatter.11
  812.0 358.9 reduce-scatter.13
  1177.4 842.7 reduce-scatter.7
  2023.6 43.1 all-reduce.2
where the time goes:
time: 2080 us
  waiting for transfers between devices  1940 us (93%)
  local copies, waits for them, and re-layouts  58.3 us (3%)
  other arithmetic  32.6 us (2%)
  matrix products  21.7 us (1%)
    reduce_scatter x1, waiting for transfers between devices, local(): lax.psum_scatter(grad_terms[0], 'lat', scatter_dimension=0, tiled=True)  848 us
    reduce_scatter x1, waiting for transfers between devices, local(): lax.psum_scatter(grad_terms[2], 'lat', scatter_dimension=0, tiled=True)  361 us
    reduce_scatter x1, waiting for transfers between devices, local(): lax.psum_scatter(grad_terms[3], 'lat', scatter_dimension=0, tiled=True)  360 us
    reduce_scatter x1, waiting for transfers between devices, local(): lax.psum_scatter(grad_terms[1], 'lat', scatter_dimension=0, tiled=True)  297 us
    psum x1, waiting for transfers between devices, local(): lax.psum(band_parts[0].astype(jnp.bfloat16), 'lon').astype(jnp.float32)  44.2 us
  transfers between devices with their start and end apart: 7, of which 7 were waited for; matrix products, arithmetic and copies ran while one was open for 2% of the time, Pallas kernels for 0%

commit v1 on v0

v1 whole, which is shorter than its diff:
```python
import math

import jax
import jax.numpy as jnp
from jax import lax
from jax.sharding import PartitionSpec as P

HEAD_DIM = 64


SOFTMAX_SCALE = 8.0


def widen(values):
    return lax.optimization_barrier(values).astype(jnp.float32)


def elementwise_product(pattern, left_side, right_side):
    return jnp.einsum(pattern, left_side, right_side, preferred_element_type=jnp.float32)


def flatten(values):
    return values.reshape(-1, values.shape[-1])


def layer_norm(values):
    average = jnp.mean(values, axis=-1, keepdims=True)
    centered = values - average
    variance = jnp.mean(centered * centered, axis=-1, keepdims=True)
    return centered * lax.rsqrt(variance + 1e-05)


def split_heads(values, head_count):
    return values.reshape(values.shape[:-1] + (head_count, values.shape[-1] // head_count))


def head_norm(values, head_count):
    shaped = split_heads(values, head_count)
    scaled = shaped * lax.rsqrt(jnp.mean(shaped * shaped, axis=-1, keepdims=True) + 1e-06)
    return scaled.reshape(values.shape)


def project_in(tokens, w_qkv, head_count):
    model_width = tokens.shape[-1]
    normed = layer_norm(tokens.astype(jnp.float32)).astype(jnp.bfloat16)
    projected = elementwise_product("...d,de->...e", normed, w_qkv)
    query_raw = projected[..., :model_width]
    key_raw = projected[..., model_width : 2 * model_width]
    query_b = head_norm(query_raw, head_count).astype(jnp.bfloat16)
    key_value = jnp.concatenate(
        [head_norm(key_raw, head_count), projected[..., 2 * model_width :]], axis=-1
    ).astype(jnp.bfloat16)
    return (normed, query_b, key_value, query_raw, key_raw)


def forward_tail(tokens, attended_b, ocean_mask, w_out, w_up, w_down):
    middle = tokens.astype(jnp.float32) + ocean_mask[..., None] * elementwise_product(
        "...d,de->...e", attended_b, w_out
    )
    normed_two = layer_norm(middle).astype(jnp.bfloat16)
    lifted = elementwise_product("...d,df->...f", normed_two, w_up)
    active = jax.nn.gelu(lifted).astype(jnp.bfloat16)
    block_out = (
        middle + ocean_mask[..., None] * elementwise_product("...f,fd->...d", active, w_down)
    ).astype(jnp.bfloat16)
    return (block_out, (middle, normed_two, lifted, active))


def backward_tail(cotangent, ocean_mask, attended_b, tail_saved, w_out, w_up, w_down):
    middle, normed_two, lifted, active = tail_saved
    upstream = cotangent.astype(jnp.float32)
    grad_branch = (ocean_mask[..., None] * upstream).astype(jnp.bfloat16)
    grad_active = elementwise_product("...d,fd->...f", grad_branch, w_down)
    grad_lifted = jax.vjp(jax.nn.gelu, lifted)[1](grad_active)[0].astype(jnp.bfloat16)
    grad_normed = elementwise_product("...f,df->...d", grad_lifted, w_up)
    grad_middle = upstream + jax.vjp(layer_norm, middle)[1](grad_normed)[0]
    grad_attn = (ocean_mask[..., None] * grad_middle).astype(jnp.bfloat16)
    grad_attended = elementwise_product("...e,de->...d", grad_attn, w_out).astype(jnp.bfloat16)
    term_out = elementwise_product("td,te->de", flatten(attended_b), flatten(grad_attn))
    term_up = elementwise_product("td,tf->df", flatten(normed_two), flatten(grad_lifted))
    term_down = elementwise_product("tf,td->fd", flatten(active), flatten(grad_branch))
    return (grad_middle, grad_attended, (term_out, term_up, term_down))


def lat_index(z, y, x_hi):
    return (z * 4 + y) * 2 + x_hi


CORE = [(0, 1), (1, 0), (2, 3), (3, 2)]
X_LO = [(0, 2), (2, 0), (1, 3), (3, 1)]
Z_GROUPS = [[lat_index(z, y, x) for z in range(8)] for y in range(4) for x in range(2)]
PLANE_GROUPS = [
    [lat_index(z, y, x_hi) * 4 + x_lo * 2 + core for y in range(4) for x_hi in range(2) for x_lo in range(2)]
    for z in range(8)
    for core in range(2)
]


def gather_sectors(values):
    from_core = lax.ppermute(values, "lon", CORE)
    from_x = lax.ppermute(values, "lon", X_LO)
    return (values, from_core, from_x, lax.ppermute(from_x, "lon", CORE))


def scatter_sectors(own, parts):
    for_core = jnp.stack([parts[0], parts[2]])
    from_core = lax.ppermute(for_core, "lon", CORE).astype(jnp.float32)
    for_x = (parts[1].astype(jnp.float32) + from_core[1]).astype(jnp.bfloat16)
    return own + from_core[0] + lax.ppermute(for_x, "lon", X_LO).astype(jnp.float32)


def quarters(term):
    width = term.shape[1] // 4
    return term.reshape(8, 4, 2, 8, 2, 2, width).transpose(1, 2, 4, 0, 3, 5, 6)


def reduce_weights(terms):
    term_qkv, term_out, term_up, term_down = terms
    down_rows = term_down.reshape(64, 2, 8, 512).transpose(0, 2, 1, 3).reshape(512, 1024)
    stacked = jnp.concatenate(
        [quarters(term.astype(jnp.bfloat16)) for term in (term_qkv, term_out, term_up, down_rows)], axis=-1
    )
    core = lax.axis_index("lon") % 2
    keep = lax.dynamic_index_in_dim(stacked, core, 5, keepdims=False)
    send = lax.dynamic_index_in_dim(stacked, 1 - core, 5, keepdims=False)
    half = keep.astype(jnp.float32) + lax.ppermute(send, "lon", CORE).astype(jnp.float32)
    half = half.astype(jnp.bfloat16).reshape(16 * 64, 1024)
    plane = lax.all_to_all(half, ("lat", "lon"), 0, 0, axis_index_groups=PLANE_GROUPS, tiled=True)
    plane = jnp.sum(plane.reshape(16, 64, 1024).astype(jnp.float32), axis=0).astype(jnp.bfloat16)
    column = lax.all_to_all(plane, "lat", 0, 0, axis_index_groups=Z_GROUPS, tiled=True)
    column = jnp.sum(column.reshape(8, 8, 1024).astype(jnp.float32), axis=0).astype(jnp.bfloat16)
    whole = lax.all_gather(column, "lon", axis=0)
    scale = 1.0 / math.sqrt(64 * 4 * 192)
    whole = whole.astype(jnp.float32) * scale
    pick = lambda lo, hi: whole[:, :, lo:hi].transpose(1, 0, 2).reshape(8, -1)
    down = pick(768, 1024).reshape(8, 2, 512).transpose(1, 0, 2).reshape(16, 512)
    return (pick(0, 384), pick(384, 512), pick(512, 768), down)


def local(tokens, ocean_count, w_qkv, w_out, w_up, w_down, cotangent):
    band_rows, local_len, model_width = tokens.shape
    head_count = model_width // HEAD_DIM
    bf = jnp.bfloat16
    tokens_all = jnp.stack(gather_sectors(tokens))
    counts_all = jnp.stack(gather_sectors(ocean_count))
    masks_all = (
        lax.broadcasted_iota(jnp.int32, (4, band_rows, local_len), 2) < counts_all
    ).astype(jnp.float32)
    ocean_mask = masks_all[0]
    normed_all = layer_norm(tokens_all.astype(jnp.float32)).astype(bf)
    normed = normed_all[0]
    query_raw = elementwise_product("rpd,de->rpe", normed, w_qkv[:, :512])
    kv_raw = elementwise_product("srpd,de->srpe", normed_all, w_qkv[:, 512:])
    key_raw = kv_raw[..., :512]
    query_b = head_norm(query_raw, head_count).astype(bf)
    query_h = split_heads(query_b, head_count)
    key_h = split_heads(head_norm(key_raw, head_count).astype(bf), head_count)
    value_h = split_heads(kv_raw[..., 512:].astype(bf), head_count)
    logits = elementwise_product("rphc,srqhc->rhpsq", query_h, key_h) * (SOFTMAX_SCALE / HEAD_DIM)
    key_mask = masks_all.transpose(1, 0, 2)[:, None, None]
    expscore = jnp.exp(logits - SOFTMAX_SCALE) * key_mask
    row_total = jnp.sum(expscore, axis=(3, 4))
    numerator = elementwise_product("rhpsq,srqhc->rphc", expscore.astype(bf), value_h)
    attended_h = numerator / row_total.transpose(0, 2, 1)[..., None]
    attended = attended_h.reshape(tokens.shape)
    attended_b = attended.astype(bf)
    block_out, tail_saved = forward_tail(tokens, attended_b, ocean_mask, w_out, w_up, w_down)
    grad_middle, grad_attended, tail_terms = backward_tail(
        cotangent, ocean_mask, attended_b, tail_saved, w_out, w_up, w_down
    )
    grad_h = split_heads(grad_attended, head_count)
    delta = jnp.sum(grad_h.astype(jnp.float32) * attended_h, axis=-1).transpose(0, 2, 1)
    weight = expscore / row_total[..., None, None]
    grad_weight = elementwise_product("rphc,srqhc->rhpsq", grad_h, value_h)
    grad_logits = (weight * (grad_weight - delta[..., None, None]) * (SOFTMAX_SCALE / HEAD_DIM)).astype(bf)
    grad_query = elementwise_product("rhpsq,srqhc->rphc", grad_logits, key_h).reshape(tokens.shape)
    grad_key = elementwise_product("rhpsq,rphc->srqhc", grad_logits, query_h).reshape(key_raw.shape)
    grad_value = elementwise_product("rhpsq,rphc->srqhc", weight.astype(bf), grad_h).reshape(key_raw.shape)
    norm_back = lambda raw, grad: jax.vjp(lambda values: head_norm(values, head_count), raw)[1](grad)[0]
    grad_q = norm_back(query_raw, grad_query).astype(bf)
    grad_kv = jnp.concatenate([norm_back(key_raw, grad_key), grad_value], axis=-1).astype(bf)
    term_qkv = jnp.concatenate(
        [
            elementwise_product("rpd,rpe->de", normed, grad_q),
            elementwise_product("srpd,srpe->de", normed_all, grad_kv),
        ],
        axis=-1,
    )
    normed_parts = elementwise_product("srpe,de->srpd", grad_kv, w_qkv[:, 512:])
    grad_own = normed_parts[0] + elementwise_product("rpe,de->rpd", grad_q, w_qkv[:, :512])
    others = normed_parts[1:].astype(bf)
    grad_normed = scatter_sectors(grad_own, others)
    grad_layer = jax.vjp(layer_norm, tokens.astype(jnp.float32))[1](grad_normed)[0]
    grad_tokens = (grad_middle + grad_layer).astype(bf)
    return (block_out, grad_tokens) + reduce_weights((term_qkv,) + tail_terms)


def solution(mesh):
    in_specs = (P("lat", "lon", None), P("lat", "lon"), P(), P(), P(), P(), P("lat", "lon", None))
    out_specs = (
        P("lat", "lon", None),
        P("lat", "lon", None),
        P("lat", None),
        P("lat", None),
        P("lat", None),
        P("lat", None),
    )
    return jax.shard_map(local, mesh=mesh, in_specs=in_specs, out_specs=out_specs, check_vma=False)
```

time: 2080 us -> 170 us (0.08)
  waiting for transfers between devices: 1940 us -> 34.6 us
  starting transfers between devices: 0.47 us -> 24.4 us
    reduce_scatter x5 -> x0, waiting for transfers between devices: 1880 us -> none  [the longest x1 848 us: local(): lax.psum_scatter(grad_terms[0], 'lat', scatter_dimension=0, tiled=True)]
    psum x1 -> x0, waiting for transfers between devices: 44.2 us -> none  [local(): lax.psum(band_parts[0].astype(jnp.bfloat16), 'lon').astype(jnp.float32)]
    ppermute x0 -> x9, waiting for transfers between devices: none -> 28.7 us  [the longest x1 26.8 us: scatter_sectors(): lax.ppermute(for_x, 'lon', X_LO).astype(jnp.float32)]
    all_gather x1 -> x0, waiting for transfers between devices: 22.8 us -> none  [local(): lax.all_gather(key_value, 'lon', axis=1, tiled=True)]
  transfers between devices with their start and end apart: 7 -> 11, of which waited for: 7 -> 4; matrix products, arithmetic and copies ran while one was open for 2% -> 9% of each run, Pallas kernels for 0% -> 0%
where the time goes in v1:
time: 170 us; the launch traced here: 169 us
  local copies, waits for them, and re-layouts  48.9 us (29%)
  waiting for transfers between devices  34.6 us (20%)
  matrix products  30.8 us (18%)
  starting transfers between devices  24.4 us (14%)
  other arithmetic  20.7 us (12%)
  blocking collectives  7.83 us (5%)
    dot_general x21, matrix products, elementwise_product(): jnp.einsum(pattern, left_side, right_side, preferred_element_type=jnp.flo...  30.8 us
    ppermute x1, waiting for transfers between devices, scatter_sectors(): lax.ppermute(for_x, 'lon', X_LO).astype(jnp.float32)  26.8 us
    reshape x6, local copies, waits for them, and re-layouts, split_heads(): values.reshape(values.shape[:-1] + (head_count, values.shape[-1] // head_...  14.2 us
    unnamed x82, local copies, waits for them, and re-layouts  9.93 us
    all_to_all x1, starting transfers between devices, reduce_weights(): lax.all_to_all(plane, 'lat', 0, 0, axis_index_groups=Z_GROUPS, tiled=True)  8.2 us
    all_gather x1, blocking collectives, reduce_weights(): whole = lax.all_gather(column, 'lon', axis=0)  7.83 us
    all_to_all x1, starting transfers between devices, reduce_weights(): lax.all_to_all(half, ('lat', 'lon'), 0, 0, axis_index_groups=PLANE_GROUPS...  6.13 us
    all_to_all x1, waiting for transfers between devices, reduce_weights(): lax.all_to_all(plane, 'lat', 0, 0, axis_index_groups=Z_GROUPS, tiled=True)  5.92 us
  transfers between devices with their start and end apart: 11, of which 4 were waited for; matrix products, arithmetic and copies ran while one was open for 9% of the time, Pallas kernels for 0%

profile of v1, /device:TPU:1, one launch (start us, length us, event | category | flops | bytes accessed | tf_op | source)
XLA Modules:
  0.0 168.6 jit_solution(16991297618383409618)
XLA Ops:
  0.7 2.1 %collective-permute-start.4 = (bf16[3,64,512]{2,1,0:T(8,128)(2,1)}, bf16[3,64,512]{2,1,0:T(8,128)(2,1)S(1)}, u32[]{:S(2)}, u32[]{:S(2)}) collective-permute-start(bf16[3,64,512]{2,1,0:T(8,128)(2,1)} %param.7), channel_id=1, source_target_pairs={{0,2},{2,0},{1,3},{3,1},{4,6},{6,4},{5,7},{7,5},{8,10},{10,8},{9,1... | collective-permute-start | bytes 589832 | tf_op jit(solution)/shard_map/ppermute | solution.py:101
  8.1 1.8 %collective-permute-start.2 = (s32[3,1]{0,1:T(1,128)S(1)}, s32[3,1]{0,1:T(1,128)S(1)}, u32[]{:S(2)}, u32[]{:S(2)}) collective-permute-start(s32[3,1]{0,1:T(1,128)S(1)} %collective-permute-done.1), channel_id=1, source_target_pairs={{0,1},{1,0},{2,3},{3,2},{4,5},{5,4},{6,7},{7,6},{8,9},{9,8},{10,11... | collective-permute-start | bytes 44 | tf_op jit(solution)/shard_map/ppermute | solution.py:102
  18.3 2.0 %reshape.200 = f32[4,3,64,8,64]{4,3,2,1,0:T(8,128)} reshape(f32[4,3,64,512]{3,2,1,0:T(8,128)S(1)} %slice.76) | data formatting | bytes 3145728 | tf_op jit(solution)/shard_map/reshape | solution.py:34
  20.3 2.8 %multiply_reduce_fusion = f32[4,3,64,8]{3,2,1,0:T(8,128)S(1)} fusion(f32[4,3,64,8,64]{4,3,2,1,0:T(8,128)} %reshape.200), kind=kLoop, calls=%fused_computation.10 | loop fusion | flops 780288 | bytes 1597440 | tf_op jit(solution)/shard_map/reduce_sum | solution.py:39
  23.1 3.6 %copy.188 = f32[4,3,64,8,64]{2,4,0,3,1:T(8,128)} copy(f32[4,3,64,8,64]{4,3,2,1,0:T(8,128)} %reshape.200) | data formatting | bytes 3145728 | tf_op jit(solution)/shard_map/reshape | solution.py:34
  27.0 2.1 %mul.275.clone = f32[4,3,64,8,64]{4,3,2,1,0:T(8,128)} broadcast(f32[4,3,64,8]{3,2,1,0:T(8,128)S(1)} %copy.228), dimensions={0,1,2,3} | broadcast | bytes 1597440 | tf_op jit(solution)/shard_map/mul | solution.py:39
  29.2 2.8 %mul.276 = f32[4,3,64,512]{3,2,1,0:T(8,128)S(1)} reshape(f32[4,3,64,8,64]{4,3,2,1,0:T(8,128)} %mul.275.clone) | data formatting | bytes 3145728 | tf_op jit(solution)/shard_map/mul | solution.py:39
  35.4 2.1 %copy.192 = bf16[4,3,64,8,64]{2,4,0,3,1:T(8,128)(2,1)S(1)} copy(bf16[4,3,64,8,64]{4,3,2,1,0:T(8,128)(2,1)} %reshape.201) | data formatting | bytes 1572864 | tf_op jit(solution)/shard_map/reshape | solution.py:34
  39.1 3.2 %reshape.199 = bf16[4,3,64,8,64]{4,3,2,1,0:T(8,128)(2,1)} reshape(bf16[4,3,64,512]{3,2,1,0:T(8,128)(2,1)} %slice.125) | data formatting | bytes 1572864 | tf_op jit(solution)/shard_map/reshape | solution.py:34
  53.8 4.9 %fusion.11 = bf16[4,3,64,8,64]{2,4,0,3,1:T(8,128)(2,1)} fusion(bf16[3,64,8,64,1]{1,3,4,2,0:T(8,128)(2,1)S(1)} %bitcast.245, f32[3,8,64,4,64]{2,4,3,1,0:T(8,128)} %copy-done.6, f32[3,8,64]{2,1,0:T(8,128)S(1)} %get-tuple-element.19), kind=kOutput, calls=%fused_computation.30 | convolution fusion | flops 51511296 | bytes 2562048 | tf_op jit(solution)/shard_map/rhpsq,rphc->srqhc/dot_general | solution.py:19
  63.3 2.8 %copy.191 = bf16[4,3,64,8,64]{4,3,2,1,0:T(8,128)(2,1)} copy(bf16[4,3,64,8,64]{2,4,0,3,1:T(8,128)(2,1)} %fusion.11) | data formatting | bytes 1572864 | tf_op jit(solution)/shard_map/rhpsq,rphc->srqhc/transpose | solution.py:19
  66.1 3.6 %reshape.204 = bf16[4,3,64,512]{3,2,1,0:T(8,128)(2,1)} reshape(bf16[4,3,64,8,64]{4,3,2,1,0:T(8,128)(2,1)} %copy.191) | data formatting | bytes 1572864 | tf_op jit(solution)/shard_map/reshape | solution.py:178
  69.7 3.7 %fusion.2 = (f32[4,3,64,8]{2,0,3,1:T(4,128)S(1)}, f32[3,8,64,4,64]{4,2,3,1,0:T(8,128)S(1)}) fusion(f32[4,3,64,8,64]{2,4,0,3,1:T(8,128)} %copy.188, bf16[3,8,64,4,64]{2,4,3,1,0:T(8,128)(2,1)S(1)} %copy-done.14, f32[3,64,8,64]{1,3,2,0:T(8,128)S(1)} %get-tuple-element.18, f32[3,64,8]{1,2,0:T(8,128)S(1)} %fusion.81), kind=kOutput, calls=%fused_computation.7 | convolution fusion | flops 51308544 | bytes 4356096 | tf_op jit(solution)/shard_map/rhpsq,rphc->srqhc/dot_general | solution.py:19
  73.4 2.3 %fusion.1 = bf16[4,3,64,8,64]{2,4,0,3,1:T(8,128)(2,1)} fusion(f32[3,8,64,4,64]{4,2,3,1,0:T(8,128)S(1)} %get-tuple-element.30, f32[4,3,64,8,64]{2,4,0,3,1:T(8,128)S(1)} %copy-done.2, f32[4,3,64,8]{2,0,3,1:T(4,128)S(1)} %copy.187, f32[4,3,64,8]{2,0,3,1:T(4,128)S(1)} %copy.172), kind=kLoop, calls=%fused_computation.4 | loop fusion | flops 1966080 | bytes 3981312 | tf_op jit(solution)/shard_map/convert.12
  75.7 2.0 %copy.189 = bf16[4,3,64,8,64]{4,3,2,1,0:T(8,128)(2,1)S(1)} copy(bf16[4,3,64,8,64]{2,4,0,3,1:T(8,128)(2,1)} %fusion.1) | data formatting | bytes 1572864 | tf_op jit(solution)/shard_map/convert.12
  91.1 3.7 %fusion.92 = (bf16[4,3,64,512]{3,2,1,0:T(8,128)(2,1)S(1)}, f32[4,3,64,512]{3,2,1,0:T(8,128)}) fusion(bf16[4,3,64,1024]{3,2,1,0:T(8,128)(2,1)} %copy-done.38, bf16[512,1536]{1,0:T(8,128)(2,1)S(1)} %copy-done.25), kind=kOutput, calls=%fused_computation.154 | convolution fusion | flops 805699584 | bytes 4980736 | tf_op jit(solution)/shard_map/srpe,de->srpd/dot_general | solution.py:19
  95.7 3.9 %fusion = bf16[4,2,2,8,8,1024]{5,4,3,2,1,0:T(8,128)(2,1)} fusion(bf16[4,2,2,8,8,1024]{5,4,3,2,1,0:T(8,128)(2,1)} %collective-permute-done.8, bf16[4,2,2,8,8,2,1024]{6,4,3,2,1,0,5:T(8,128)(2,1)S(1)} %copy-done.4, s32[]{:T(128)S(6)} %select_n.15), kind=kLoop, calls=%fused_computation.3 | loop fusion | flops 4194304 | bytes 6291460 | tf_op jit(solution)/shard_map/convert_element_type | solution.py:127
  99.6 6.1 %all-to-all-start = ((bf16[16,64,1024]{2,1,0:T(8,128)(2,1)}), bf16[16,64,1024]{2,1,0:T(8,128)(2,1)S(1)}, u32[]{:S(2)}, u32[]{:S(2)}) async-start(bf16[16,64,1024]{2,1,0:T(8,128)(2,1)} %bitcast.69), calls=%async_computation | async-start | bytes 4194304 | tf_op jit(solution)/shard_map/all_to_all | solution.py:128
  106.4 2.5 %fusion.25 = bf16[3,64,512]{2,1,0:T(8,128)(2,1)} fusion(f32[3,64,512]{2,1,0:T(8,128)S(1)} %copy-done.12, bf16[3,64,1024]{2,1,0:T(8,128)(2,1)} %get-tuple-element.25, bf16[1024,512]{1,0:T(8,128)(2,1)} %param.12, f32[3,64]{1,0:T(4,128)S(1)} %convert_bitcast_fusion), kind=kOutput, calls=%fused_computation.46 | convolution fusion | flops 201621504 | bytes 2032384 | tf_op jit(solution)/shard_map/...f,fd->...d/dot_general | solution.py:19
  113.2 26.8 %collective-permute-done.7 = bf16[3,64,512]{2,1,0:T(8,128)(2,1)S(1)} collective-permute-done((bf16[3,64,512]{2,1,0:T(8,128)(2,1)S(1)}, bf16[3,64,512]{2,1,0:T(8,128)(2,1)S(1)}, u32[]{:S(2)}, u32[]{:S(2)}) %collective-permute-start.7) | collective-permute-done | bytes 196640 | tf_op jit(solution)/shard_map/ppermute | solution.py:109
  142.7 8.2 %all-to-all-start.1 = ((bf16[8,8,1024]{2,1,0:T(8,128)(2,1)}), bf16[8,8,1024]{2,1,0:T(8,128)(2,1)S(1)}, u32[]{:S(2)}, u32[]{:S(2)}) async-start(bf16[8,8,1024]{2,1,0:T(8,128)(2,1)} %bitcast.249), calls=%async_computation.1 | async-start | bytes 262144 | tf_op jit(solution)/shard_map/all_to_all | solution.py:130
  150.9 2.0 %add_convert_fusion = bf16[3,64,512]{2,1,0:T(8,128)(2,1)} fusion(f32[3,64,512]{2,1,0:T(8,128)} %copy-done.19, bf16[3,64,512]{2,1,0:T(8,128)(2,1)S(1)} %copy-done.32, f32[3,64]{1,0:T(4,128)} %negate_multiply_fusion, f32[3,64]{1,0:T(4,128)S(1)} %negate_multiply_fusion.1, f32[3,64]{1,0:T(4,128)S(1)} %get-tuple-element.16, ...), kind=kLoop, calls=%fused_computation.107 | loop fusion | flops 1179648 | bytes 1380096 | tf_op jit(solution)/shard_map/convert_element_type | solution.py:194
  152.9 5.9 %all-to-all-done.1 = bf16[8,8,1024]{2,1,0:T(8,128)(2,1)S(1)} async-done(((bf16[8,8,1024]{2,1,0:T(8,128)(2,1)}), bf16[8,8,1024]{2,1,0:T(8,128)(2,1)S(1)}, u32[]{:S(2)}, u32[]{:S(2)}) %all-to-all-start.1) | async-done | bytes 131104 | tf_op jit(solution)/shard_map/all_to_all | solution.py:130
  158.9 7.8 %all-gather = bf16[32,1024]{1,0:T(8,128)(2,1)S(1)} all-gather(bf16[8,1024]{1,0:T(8,128)(2,1)S(1)} %reduce_sum.225), channel_id=2, replica_groups=mesh['lat'=64,'lon'=4] {'lon'}, dimensions={0}, use_global_device_ids=true | all-gather | bytes 81920 | tf_op jit(solution)/shard_map/all_gather | solution.py:132
  (175 shorter events, 58.4 us)
Async XLA Ops:
  0.6 45.5 %copy-start = (bf16[512,1024]{1,0:T(8,128)(2,1)S(1)}, bf16[512,1024]{1,0:T(8,128)(2,1)}, u32[]{:S(2)}) copy-start(bf16[512,1024]{1,0:T(8,128)(2,1)} %param.11) | copy-start | bytes 3145732
  0.6 12.5 %copy-start.8 = (bf16[3,64,512]{2,1,0:T(8,128)(2,1)S(1)}, bf16[3,64,512]{2,1,0:T(8,128)(2,1)}, u32[]{:S(2)}) copy-start(bf16[3,64,512]{2,1,0:T(8,128)(2,1)} %param.7) | copy-start | bytes 589828
  0.7 10.1 %copy-start.39 = (s32[3,1]{0,1:T(1,128)S(1)}, s32[3,1]{0,1:T(1,128)}, u32[]{:S(2)}) copy-start(s32[3,1]{0,1:T(1,128)} %param.8) | copy-start | bytes 40
  0.7 10.3 %copy-start.30 = (bf16[3,64,512]{2,1,0:T(8,128)(2,1)S(1)}, bf16[3,64,512]{2,1,0:T(8,128)(2,1)}, u32[]{:S(2)}) copy-start(bf16[3,64,512]{2,1,0:T(8,128)(2,1)} %param.13) | copy-start | bytes 589828
  0.7 11.1 %collective-permute-start.4 = (bf16[3,64,512]{2,1,0:T(8,128)(2,1)}, bf16[3,64,512]{2,1,0:T(8,128)(2,1)S(1)}, u32[]{:S(2)}, u32[]{:S(2)}) collective-permute-start(bf16[3,64,512]{2,1,0:T(8,128)(2,1)} %param.7), channel_id=1, source_target_pairs={{0,2},{2,0},{1,3},{3,1},{4,6},{6,4},{5,7},{7,5},{8,10},{10,8},{9,1... | collective-permute-start | bytes 589832 | tf_op jit(solution)/shard_map/ppermute | solution.py:101
  2.8 9.3 %collective-permute-start.3 = (bf16[3,64,512]{2,1,0:T(8,128)(2,1)}, bf16[3,64,512]{2,1,0:T(8,128)(2,1)S(1)}, u32[]{:S(2)}, u32[]{:S(2)}) collective-permute-start(bf16[3,64,512]{2,1,0:T(8,128)(2,1)} %param.7), channel_id=1, source_target_pairs={{0,1},{1,0},{2,3},{3,2},{4,5},{5,4},{6,7},{7,6},{8,9},{9,8},{10,11... | collective-permute-start | bytes 589832 | tf_op jit(solution)/shard_map/ppermute | solution.py:100
  4.1 4.0 %collective-permute-start.1 = (s32[3,1]{0,1:T(1,128)}, s32[3,1]{0,1:T(1,128)S(1)}, u32[]{:S(2)}, u32[]{:S(2)}) collective-permute-start(s32[3,1]{0,1:T(1,128)} %param.8), channel_id=1, source_target_pairs={{0,2},{2,0},{1,3},{3,1},{4,6},{6,4},{5,7},{7,5},{8,10},{10,8},{9,1... | collective-permute-start | bytes 44 | tf_op jit(solution)/shard_map/ppermute | solution.py:101
  5.8 4.2 %collective-permute-start = (s32[3,1]{0,1:T(1,128)}, s32[3,1]{0,1:T(1,128)S(1)}, u32[]{:S(2)}, u32[]{:S(2)}) collective-permute-start(s32[3,1]{0,1:T(1,128)} %param.8), channel_id=1, source_target_pairs={{0,1},{1,0},{2,3},{3,2},{4,5},{5,4},{6,7},{7,6},{8,9},{9,8},{10,11... | collective-permute-start | bytes 44 | tf_op jit(solution)/shard_map/ppermute | solution.py:100
  8.1 2.6 %collective-permute-start.2 = (s32[3,1]{0,1:T(1,128)S(1)}, s32[3,1]{0,1:T(1,128)S(1)}, u32[]{:S(2)}, u32[]{:S(2)}) collective-permute-start(s32[3,1]{0,1:T(1,128)S(1)} %collective-permute-done.1), channel_id=1, source_target_pairs={{0,1},{1,0},{2,3},{3,2},{4,5},{5,4},{6,7},{7,6},{8,9},{9,8},{10,11... | collective-permute-start | bytes 44 | tf_op jit(solution)/shard_map/ppermute | solution.py:102
  11.7 1.4 collective-permute-start.5
  45.9 4.9 %copy-start.11 = (f32[3,64,512]{2,1,0:T(8,128)}, f32[3,64,512]{2,1,0:T(8,128)S(1)}, u32[]{:S(2)}) copy-start(f32[3,64,512]{2,1,0:T(8,128)S(1)} %get-tuple-element.24) | copy-start | bytes 1179652
  53.8 4.9 %copy-start.7 = (f32[3,8,64,4,64]{2,4,3,1,0:T(8,128)S(1)}, f32[3,8,64,4,64]{2,4,3,1,0:T(8,128)}, u32[]{:S(2)}) copy-start(f32[3,8,64,4,64]{2,4,3,1,0:T(8,128)} %copy-done.6) | copy-start | bytes 4718596
  53.8 4.9 %copy-start.16 = (bf16[4,3,64,8,64]{4,3,2,1,0:T(8,128)(2,1)S(1)}, bf16[4,3,64,8,64]{4,3,2,1,0:T(8,128)(2,1)}, u32[]{:S(2)}) copy-start(bf16[4,3,64,8,64]{4,3,2,1,0:T(8,128)(2,1)} %reshape.199) | copy-start | bytes 2359300
  69.7 3.8 %copy-start.2 = (f32[4,3,64,8,64]{2,4,0,3,1:T(8,128)S(1)}, f32[4,3,64,8,64]{2,4,0,3,1:T(8,128)}, u32[]{:S(2)}) copy-start(f32[4,3,64,8,64]{2,4,0,3,1:T(8,128)} %copy.188) | copy-start | bytes 4718596
  90.6 5.1 %collective-permute-start.8 = (bf16[4,2,2,8,8,1024]{5,4,3,2,1,0:T(8,128)(2,1)}, bf16[4,2,2,8,8,1024]{5,4,3,2,1,0:T(8,128)(2,1)}, u32[]{:S(2)}, u32[]{:S(2)}) collective-permute-start(bf16[4,2,2,8,8,1024]{5,4,3,2,1,0:T(8,128)(2,1)} %dynamic-slice_bitcast_fusion), channel_id=1, source_target_pairs={{0,1},{1,0},{2,3},{3,2},{4,5},{5,4},{6,7},{7,6},{8,9},{9,8},{10,11... | collective-permute-start | bytes 6291464 | tf_op jit(solution)/shard_map/ppermute | solution.py:126
  91.1 4.6 %copy-start.4 = (bf16[4,2,2,8,8,2,1024]{6,4,3,2,1,0,5:T(8,128)(2,1)S(1)}, bf16[4,2,2,8,8,2,1024]{6,4,3,2,1,0,5:T(8,128)(2,1)}, u32[]{:S(2)}) copy-start(bf16[4,2,2,8,8,2,1024]{6,4,3,2,1,0,5:T(8,128)(2,1)} %copy-done.3) | copy-start | bytes 12582916
  99.6 6.8 %copy-start.12 = (f32[3,64,512]{2,1,0:T(8,128)S(1)}, f32[3,64,512]{2,1,0:T(8,128)}, u32[]{:S(2)}) copy-start(f32[3,64,512]{2,1,0:T(8,128)} %copy-done.11) | copy-start | bytes 1179652
  99.6 42.0 %all-to-all-start = ((bf16[16,64,1024]{2,1,0:T(8,128)(2,1)}), bf16[16,64,1024]{2,1,0:T(8,128)(2,1)S(1)}, u32[]{:S(2)}, u32[]{:S(2)}) async-start(bf16[16,64,1024]{2,1,0:T(8,128)(2,1)} %bitcast.69), calls=%async_computation | async-start | bytes 4194304 | tf_op jit(solution)/shard_map/all_to_all | solution.py:128
  105.8 3.1 %collective-permute-start.6 = (bf16[2,3,64,512]{3,2,1,0:T(8,128)(2,1)S(1)}, bf16[2,3,64,512]{3,2,1,0:T(8,128)(2,1)S(1)}, u32[]{:S(2)}, u32[]{:S(2)}) collective-permute-start(bf16[2,3,64,512]{3,2,1,0:T(8,128)(2,1)S(1)} %pad_maximum_fusion.3), channel_id=1, source_target_pairs={{0,1},{1,0},{2,3},{3,2},{4,5},{5,4},{6,7},{7,6},{8,9},{9,8},{10,11... | collective-permute-start | bytes 1179656 | tf_op jit(solution)/shard_map/ppermute | solution.py:107
  106.4 5.2 %copy-start.22 = (bf16[3,64,8,64]{1,3,2,0:T(8,128)(2,1)S(1)}, bf16[3,64,8,64]{1,3,2,0:T(8,128)(2,1)}, u32[]{:S(2)}) copy-start(bf16[3,64,8,64]{1,3,2,0:T(8,128)(2,1)} %copy-done.21) | copy-start | bytes 589828
  109.9 30.1 %collective-permute-start.7 = (bf16[3,64,512]{2,1,0:T(8,128)(2,1)S(1)}, bf16[3,64,512]{2,1,0:T(8,128)(2,1)S(1)}, u32[]{:S(2)}, u32[]{:S(2)}) collective-permute-start(bf16[3,64,512]{2,1,0:T(8,128)(2,1)S(1)} %fusion.69), channel_id=1, source_target_pairs={{0,2},{2,0},{1,3},{3,1},{4,6},{6,4},{5,7},{7,5},{8,10},{10,8},{9,1... | collective-permute-start | bytes 589832 | tf_op jit(solution)/shard_map/ppermute | solution.py:109
  140.3 10.6 %copy-start.32 = (bf16[3,64,512]{2,1,0:T(8,128)(2,1)S(1)}, bf16[3,64,512]{2,1,0:T(8,128)(2,1)}, u32[]{:S(2)}) copy-start(bf16[3,64,512]{2,1,0:T(8,128)(2,1)} %param.13) | copy-start | bytes 589828
  141.6 26.9 %copy-start.1 = (bf16[512,1024]{1,0:T(8,128)(2,1)S(1)}, bf16[512,1024]{1,0:T(8,128)(2,1)}, u32[]{:S(2)}) copy-start(bf16[512,1024]{1,0:T(8,128)(2,1)} %param.11) | copy-start | bytes 3145732
  142.7 16.2 %all-to-all-start.1 = ((bf16[8,8,1024]{2,1,0:T(8,128)(2,1)}), bf16[8,8,1024]{2,1,0:T(8,128)(2,1)S(1)}, u32[]{:S(2)}, u32[]{:S(2)}) async-start(bf16[8,8,1024]{2,1,0:T(8,128)(2,1)} %bitcast.249), calls=%async_computation.1 | async-start | bytes 262144 | tf_op jit(solution)/shard_map/all_to_all | solution.py:130
  (27 other events, 46.5 us)

commit v2 on v1

v2 whole, which is shorter than its diff:
```python
import math

import jax
import jax.numpy as jnp
from jax import lax
from jax.experimental import pallas as pl
from jax.experimental.pallas import tpu as pltpu
from jax.sharding import PartitionSpec as P

F32 = jnp.float32
BF16 = jnp.bfloat16
HEAD_DIM = 64
SOFTMAX_SCALE = 8.0
WIDTH = 512
HIDDEN = 1024
ROWS_DEV = 3
SECTOR = 64
TOKENS = ROWS_DEV * SECTOR
KEYS = 4 * SECTOR
GROUP = 256
GELU_A = math.sqrt(2.0 / math.pi)
GELU_B = 0.044715
NEAR_MB = 20
FRONT_MB = 28
BACK_MB = 28


def lat_index(z, y, x_hi):
    return (z * 4 + y) * 2 + x_hi


CORE = [(0, 1), (1, 0), (2, 3), (3, 2)]
X_LO = [(0, 2), (2, 0), (1, 3), (3, 1)]
Z_GROUPS = [[lat_index(z, y, x) for z in range(8)] for y in range(4) for x in range(2)]
PLANE_GROUPS = [
    [lat_index(z, y, x_hi) * 4 + x_lo * 2 + core for y in range(4) for x_hi in range(2) for x_lo in range(2)]
    for z in range(8)
    for core in range(2)
]


def mm(left, right):
    return lax.dot_general(left, right, (((1,), (0,)), ((), ())), preferred_element_type=F32)


def mm_nt(left, right):
    return lax.dot_general(left, right, (((1,), (1,)), ((), ())), preferred_element_type=F32)


def mm_tn(left, right):
    return lax.dot_general(left, right, (((0,), (0,)), ((), ())), preferred_element_type=F32)


def mean_last(values):
    return jnp.sum(values, axis=-1, keepdims=True) * (1.0 / values.shape[-1])


def layer_norm(values):
    centered = values - mean_last(values)
    inverse = lax.rsqrt(mean_last(centered * centered) + 1e-05)
    return centered * inverse, inverse


def layer_norm_back(normed, inverse, grad):
    return inverse * (grad - mean_last(grad) - normed * mean_last(grad * normed))


def head_blocks():
    same = lax.broadcasted_iota(jnp.int32, (GROUP, GROUP), 0) // HEAD_DIM == (
        lax.broadcasted_iota(jnp.int32, (GROUP, GROUP), 1) // HEAD_DIM
    )
    return jnp.where(same, 1.0, 0.0).astype(BF16)


def head_mean(values, blocks):
    parts = [
        mm(values[:, at : at + GROUP].astype(BF16), blocks) for at in range(0, values.shape[1], GROUP)
    ]
    return (parts[0] if len(parts) == 1 else jnp.concatenate(parts, axis=1)) * (1.0 / HEAD_DIM)


def head_masks(dtype):
    lane = lax.broadcasted_iota(jnp.int32, (1, GROUP), 1) // HEAD_DIM
    return [jnp.where(lane == head, 1.0, 0.0).astype(dtype) for head in range(4)]


def stack_heads(values, masks):
    return jnp.concatenate([values * mask for mask in masks], axis=0)


def unstack_heads(values, masks):
    return sum(values[head * SECTOR : (head + 1) * SECTOR] * masks[head] for head in range(4))


def store_pieces(out_ref, x_lo, column, product):
    width = product.shape[1]
    split = product.reshape(8, 8, 8, width)
    for place in range(8):
        piece = jnp.concatenate([split[z, place] for z in range(8)], axis=0)
        out_ref[place * 2 + x_lo, :, column : column + width] = piece.astype(BF16)


def rows_of(row, width=SECTOR):
    return slice(row * width, (row + 1) * width)


def key_value(tok_ref, w_qkv_ref, blocks, slot, slots, normed_ref, key_ref, value_ref, inv_k_ref):
    normed = layer_norm(tok_ref[...].astype(F32))[0].astype(BF16)
    key_raw = mm(normed, w_qkv_ref[:, WIDTH : 2 * WIDTH])
    inv_k = lax.rsqrt(head_mean(key_raw * key_raw, blocks) + 1e-06)
    key_b = (key_raw * inv_k).astype(BF16)
    inv_kb = inv_k.astype(BF16)
    value_b = mm(normed, w_qkv_ref[:, 2 * WIDTH :]).astype(BF16)
    for row in range(ROWS_DEV):
        at = (row * slots + slot) * SECTOR
        for ref, val in (
            (normed_ref, normed),
            (key_ref, key_b),
            (inv_k_ref, inv_kb),
            (value_ref, value_b),
        ):
            ref[at : at + SECTOR, :] = val[rows_of(row)]
    return normed


def own_mask(count_ref):
    place = lax.broadcasted_iota(jnp.int32, (SECTOR, 1), 0)
    return jnp.concatenate(
        [jnp.where(place < count_ref[row, 0], 1.0, 0.0) for row in range(ROWS_DEV)], axis=0
    )


def near_kernel(
    count_ref,
    tok0_ref,
    w_qkv_ref,
    w_down_ref,
    cot_ref,
    normed_ref,
    key_ref,
    value_ref,
    inv_k_ref,
    query_ref,
    inv_q_ref,
    grad_active_ref,
):
    blocks = head_blocks()
    normed = key_value(tok0_ref, w_qkv_ref, blocks, 0, 1, normed_ref, key_ref, value_ref, inv_k_ref)
    query_raw = mm(normed, w_qkv_ref[:, :WIDTH])
    inv_q = lax.rsqrt(head_mean(query_raw * query_raw, blocks) + 1e-06)
    inv_q_ref[...] = inv_q.astype(BF16)
    query_ref[...] = (query_raw * inv_q).astype(BF16)
    branch = (own_mask(count_ref) * cot_ref[...].astype(F32)).astype(BF16)
    grad_active_ref[...] = mm_nt(branch, w_down_ref[...]).astype(BF16)


def mate_kernel(tok1_ref, w_qkv_ref, normed_ref, key_ref, value_ref, inv_k_ref):
    key_value(tok1_ref, w_qkv_ref, head_blocks(), 0, 1, normed_ref, key_ref, value_ref, inv_k_ref)


def row_join(row, lanes, own_ref, mate_ref, far_ref):
    own = rows_of(row)
    return jnp.concatenate(
        [own_ref[own, lanes], mate_ref[own, lanes], far_ref[rows_of(row, 2 * SECTOR), lanes]], axis=0
    )


def front_kernel(
    core_ref,
    count_ref,
    count1_ref,
    count2_ref,
    count3_ref,
    tok0_ref,
    tok2_ref,
    tok3_ref,
    w_qkv_ref,
    w_out_ref,
    w_up_ref,
    w_down_ref,
    cot_ref,
    query_ref,
    own_key_ref,
    own_value_ref,
    mate_key_ref,
    mate_value_ref,
    grad_active_ref,
    block_out_ref,
    keep_ref,
    send_ref,
    grad_middle_ref,
    normed_ref,
    key_ref,
    value_ref,
    inv_k_ref,
    probs_ref,
    grad_att_ref,
    att_ref,
    lift_ref,
    attn_ref,
    branch_ref,
):
    blocks = head_blocks()
    masks_b = head_masks(BF16)
    masks_f = head_masks(F32)
    core = core_ref[0]
    key_value(tok2_ref, w_qkv_ref, blocks, 0, 2, normed_ref, key_ref, value_ref, inv_k_ref)
    key_value(tok3_ref, w_qkv_ref, blocks, 1, 2, normed_ref, key_ref, value_ref, inv_k_ref)

    key_place = lax.broadcasted_iota(jnp.int32, (1, KEYS), 1)
    for row in range(ROWS_DEV):
        limit = jnp.zeros((1, KEYS), jnp.int32)
        for sector, ref in enumerate((count_ref, count1_ref, count2_ref, count3_ref)):
            limit = jnp.where(key_place // SECTOR == sector, ref[row, 0], limit)
        key_mask = jnp.where(key_place % SECTOR < limit, 1.0, 0.0)
        for group in range(2):
            lanes = slice(group * GROUP, (group + 1) * GROUP)
            stacked = stack_heads(query_ref[rows_of(row), lanes], masks_b)
            keys = row_join(row, lanes, own_key_ref, mate_key_ref, key_ref)
            values = row_join(row, lanes, own_value_ref, mate_value_ref, value_ref)
            scores = mm_nt(stacked, keys)
            expscore = jnp.exp(scores * (SOFTMAX_SCALE / HEAD_DIM) - SOFTMAX_SCALE) * key_mask
            total = jnp.sum(expscore, axis=1, keepdims=True)
            probs = (expscore * (1.0 / total)).astype(BF16)
            probs_ref[row * 2 + group] = probs
            att_ref[rows_of(row), lanes] = unstack_heads(mm(probs, values), masks_f).astype(BF16)

    mask = own_mask(count_ref)
    attended = att_ref[...]
    middle = tok0_ref[...].astype(F32) + mask * mm(attended, w_out_ref[...])
    normed_two, inverse = layer_norm(middle)
    normed_two_b = normed_two.astype(BF16)
    lifted = mm(normed_two_b, w_up_ref[...])
    square = lifted * lifted
    bent = jnp.tanh(GELU_A * lifted * (1.0 + GELU_B * square))
    half = 0.5 * (1.0 + bent)
    active = (lifted * half).astype(BF16)
    slope = half + 0.5 * lifted * (1.0 - bent * bent) * (GELU_A * (1.0 + 3.0 * GELU_B * square))
    block_out_ref[...] = (middle + mask * mm(active, w_down_ref[...])).astype(BF16)
    upstream = cot_ref[...].astype(F32)
    branch = (mask * upstream).astype(BF16)
    grad_lifted = (slope * grad_active_ref[...].astype(F32)).astype(BF16)
    grad_normed = mm_nt(grad_lifted, w_up_ref[...])
    grad_middle = upstream + layer_norm_back(normed_two, inverse, grad_normed)
    grad_middle_ref[...] = grad_middle
    grad_attn = (mask * grad_middle).astype(BF16)
    grad_att_ref[...] = mm_nt(grad_attn, w_out_ref[...]).astype(BF16)

    for part in range(4):
        lift_ref[part] = grad_lifted[:, part * 256 : (part + 1) * 256]
        attn_ref[part] = grad_attn[:, part * 128 : (part + 1) * 128]
    for part in range(2):
        branch_ref[part] = branch[:, part * 256 : (part + 1) * 256]
    for out_ref, half_index in ((keep_ref, core), (send_ref, 1 - core)):
        pair = jnp.concatenate([attn_ref[half_index], attn_ref[half_index + 2]], axis=1)
        term_out = mm_tn(attended, pair)
        for x_lo in range(2):
            store_pieces(out_ref, x_lo, 0, term_out[:, x_lo * 128 : (x_lo + 1) * 128])
            store_pieces(out_ref, x_lo, 128, mm_tn(normed_two_b, lift_ref[half_index + 2 * x_lo]))
        term_down = mm_tn(active, branch_ref[half_index]).reshape(64, 2, 8, 256)
        for x_lo in range(2):
            store_pieces(out_ref, x_lo, 384, term_down[:, x_lo].reshape(512, 256))


def norm_back(normed_b, inverse_b, grad, blocks):
    normed = normed_b.astype(F32)
    shift = head_mean(normed * grad, blocks)
    return (inverse_b.astype(F32) * (grad - normed * shift)).astype(BF16)


def back_kernel(
    core_ref,
    query_ref,
    inv_q_ref,
    own_normed_ref,
    own_key_ref,
    own_value_ref,
    own_inv_k_ref,
    mate_normed_ref,
    mate_key_ref,
    mate_value_ref,
    mate_inv_k_ref,
    normed_ref,
    key_ref,
    value_ref,
    inv_k_ref,
    probs_ref,
    grad_att_ref,
    keep_ref,
    send_ref,
    gq_ref,
    gk_ref,
    gv_ref,
):
    blocks = head_blocks()
    masks_b = head_masks(BF16)
    masks_f = head_masks(F32)
    core = core_ref[0]
    for row in range(ROWS_DEV):
        own = rows_of(row)
        mate = slice(own.start + TOKENS, own.stop + TOKENS)
        far = rows_of(row, 2 * SECTOR)
        far = slice(far.start + 2 * TOKENS, far.stop + 2 * TOKENS)
        for group in range(2):
            lanes = slice(group * GROUP, (group + 1) * GROUP)
            keys = row_join(row, lanes, own_key_ref, mate_key_ref, key_ref)
            values = row_join(row, lanes, own_value_ref, mate_value_ref, value_ref)
            inv_k = row_join(row, lanes, own_inv_k_ref, mate_inv_k_ref, inv_k_ref)
            stacked_q = stack_heads(query_ref[own, lanes], masks_b)
            stacked_g = stack_heads(grad_att_ref[own, lanes], masks_b)
            probs_b = probs_ref[row * 2 + group]
            probs = probs_b.astype(F32)
            grad_probs = mm_nt(stacked_g, values)
            delta = jnp.sum(probs * grad_probs, axis=1, keepdims=True)
            grad_scores = (probs * (grad_probs - delta) * (SOFTMAX_SCALE / HEAD_DIM)).astype(BF16)
            grad_q = unstack_heads(mm(grad_scores, keys), masks_f)
            grad_k = mm_tn(grad_scores, stacked_q)
            grad_v = mm_tn(probs_b, stacked_g).astype(BF16)
            grad_q = norm_back(query_ref[own, lanes], inv_q_ref[own, lanes], grad_q, blocks)
            grad_k = norm_back(keys, inv_k, grad_k, blocks)
            for part in range(2):
                at = slice(part * 128, (part + 1) * 128)
                gq_ref[group * 2 + part, own, :] = grad_q[:, at]
                for ref, grad in ((gk_ref, grad_k), (gv_ref, grad_v)):
                    ref[group * 2 + part, own, :] = grad[:SECTOR, at]
                    ref[group * 2 + part, mate, :] = grad[SECTOR : 2 * SECTOR, at]
                    ref[group * 2 + part, far, :] = grad[2 * SECTOR :, at]

    normed_all = jnp.concatenate([own_normed_ref[...], mate_normed_ref[...], normed_ref[...]], axis=0)
    for out_ref, half_index in ((keep_ref, core), (send_ref, 1 - core)):
        pair = jnp.concatenate([gq_ref[half_index], gq_ref[half_index + 2]], axis=1)
        term_q = mm_tn(own_normed_ref[...], pair)
        for x_lo in range(2):
            store_pieces(out_ref, x_lo, 0, term_q[:, x_lo * 128 : (x_lo + 1) * 128])
            pair = jnp.concatenate([gk_ref[half_index + 2 * x_lo], gv_ref[half_index + 2 * x_lo]], axis=1)
            store_pieces(out_ref, x_lo, 128, mm_tn(normed_all, pair))


def push_kernel(w_qkv_ref, gq_ref, gk_ref, gv_ref, for_core_ref, for_x_ref, own_ref):
    grad_q = jnp.concatenate([gq_ref[part] for part in range(4)], axis=1)

    def grad_normed(rows):
        grads = [ref[part, rows, :] for ref in (gk_ref, gv_ref) for part in range(4)]
        return mm_nt(jnp.concatenate(grads, axis=1), w_qkv_ref[:, WIDTH:])

    for_core_ref[0] = grad_normed(slice(TOKENS, 2 * TOKENS)).astype(BF16)
    far = grad_normed(slice(2 * TOKENS, 4 * TOKENS)).astype(BF16)
    for row in range(ROWS_DEV):
        at = row * 2 * SECTOR
        for_x_ref[rows_of(row), :] = far[at : at + SECTOR]
        for_core_ref[1, rows_of(row), :] = far[at + SECTOR : at + 2 * SECTOR]
    own_ref[...] = grad_normed(slice(0, TOKENS)) + mm_nt(grad_q, w_qkv_ref[:, :WIDTH])


def join_kernel(keep1_ref, recv1_ref, keep2_ref, recv2_ref, out_ref):
    for piece in range(16):
        out_ref[piece, :, :384] = (keep2_ref[piece].astype(F32) + recv2_ref[piece].astype(F32)).astype(BF16)
        out_ref[piece, :, 384:] = (keep1_ref[piece].astype(F32) + recv1_ref[piece].astype(F32)).astype(BF16)


def final_kernel(whole_ref, qkv_ref, out_ref, up_ref, down_ref):
    whole = whole_ref[...].astype(F32) * (1.0 / math.sqrt(64 * 4 * TOKENS))
    for quarter in range(4):
        part = whole[quarter * 8 : (quarter + 1) * 8]
        at = slice(quarter * 128, (quarter + 1) * 128)
        for matrix in range(3):
            low = matrix * WIDTH + quarter * 128
            qkv_ref[:, low : low + 128] = part[:, matrix * 128 : (matrix + 1) * 128]
        out_ref[:, at] = part[:, 384:512]
        up_ref[:, quarter * 256 : (quarter + 1) * 256] = part[:, 512:768]
        side = (quarter % 2) * 256
        down_ref[(quarter // 2) * 8 : (quarter // 2) * 8 + 8, side : side + 256] = part[:, 768:]


def vmem(count):
    return [pl.BlockSpec(memory_space=pltpu.VMEM)] * count


def smem(count):
    return [pl.BlockSpec(memory_space=pltpu.SMEM)] * count


def shape(dims, dtype):
    return jax.ShapeDtypeStruct(dims, dtype)


TOKEN = (TOKENS, WIDTH)
PAIR = (2 * TOKENS, WIDTH)


def params(megabytes):
    return pltpu.CompilerParams(vmem_limit_bytes=megabytes * 1024 * 1024)


def run_near(count, tok0, w_qkv, w_down, cot):
    outs = [shape(TOKEN, BF16)] * 6 + [shape((TOKENS, HIDDEN), BF16)]
    return pl.pallas_call(
        near_kernel,
        out_shape=outs,
        in_specs=smem(1) + vmem(4),
        out_specs=vmem(len(outs)),
        compiler_params=params(NEAR_MB),
        cost_estimate=pl.CostEstimate(flops=2_500_000_000, bytes_accessed=4_000_000, transcendentals=0),
        name="near",
    )(count, tok0, w_qkv, w_down, cot)


def run_mate(tok1, w_qkv):
    outs = [shape(TOKEN, BF16)] * 4
    return pl.pallas_call(
        mate_kernel,
        out_shape=outs,
        in_specs=vmem(2),
        out_specs=vmem(len(outs)),
        compiler_params=params(NEAR_MB),
        cost_estimate=pl.CostEstimate(flops=5_000_000_000, bytes_accessed=2_000_000, transcendentals=0),
        name="mate",
    )(tok1, w_qkv)


def run_front(core, counts, sectors, w_qkv, w_out, w_up, w_down, cot, near):
    outs = [
        shape(TOKEN, BF16),
        shape((16, 64, 640), BF16),
        shape((16, 64, 640), BF16),
        shape(TOKEN, F32),
        shape(PAIR, BF16),
        shape(PAIR, BF16),
        shape(PAIR, BF16),
        shape(PAIR, BF16),
        shape((6, GROUP, KEYS), BF16),
        shape(TOKEN, BF16),
    ]
    return pl.pallas_call(
        front_kernel,
        out_shape=outs,
        in_specs=smem(5) + vmem(8 + len(near)),
        out_specs=vmem(len(outs)),
        scratch_shapes=[
            pltpu.VMEM(TOKEN, BF16),
            pltpu.VMEM((4, TOKENS, 256), BF16),
            pltpu.VMEM((4, TOKENS, 128), BF16),
            pltpu.VMEM((2, TOKENS, 256), BF16),
        ],
        compiler_params=params(FRONT_MB),
        cost_estimate=pl.CostEstimate(flops=5_000_000_000, bytes_accessed=12_000_000, transcendentals=600_000),
        name="front",
    )(core, *counts, *sectors, w_qkv, w_out, w_up, w_down, cot, *near)


def run_back(core, saved):
    outs = [
        shape((16, 64, 384), BF16),
        shape((16, 64, 384), BF16),
        shape((4, TOKENS, 128), BF16),
        shape((4, 4 * TOKENS, 128), BF16),
        shape((4, 4 * TOKENS, 128), BF16),
    ]
    return pl.pallas_call(
        back_kernel,
        out_shape=outs,
        in_specs=smem(1) + vmem(len(saved)),
        out_specs=vmem(len(outs)),
        compiler_params=params(BACK_MB),
        cost_estimate=pl.CostEstimate(flops=6_000_000_000, bytes_accessed=12_000_000, transcendentals=0),
        name="back",
    )(core, *saved)


def run_push(w_qkv, grads):
    outs = [shape((2,) + TOKEN, BF16), shape(TOKEN, BF16), shape(TOKEN, F32)]
    return pl.pallas_call(
        push_kernel,
        out_shape=outs,
        in_specs=vmem(4),
        out_specs=vmem(3),
        compiler_params=params(NEAR_MB),
        cost_estimate=pl.CostEstimate(flops=2_000_000_000, bytes_accessed=4_000_000, transcendentals=0),
        name="push",
    )(w_qkv, *grads)


def run_join(*halves):
    return pl.pallas_call(
        join_kernel,
        out_shape=shape((16, 64, 1024), BF16),
        in_specs=vmem(4),
        out_specs=vmem(1)[0],
        compiler_params=params(NEAR_MB),
        cost_estimate=pl.CostEstimate(flops=1_000_000, bytes_accessed=6_000_000, transcendentals=0),
        name="join",
    )(*halves)


def run_final(whole):
    outs = [shape((8, 1536), F32), shape((8, 512), F32), shape((8, 1024), F32), shape((16, 512), F32)]
    return pl.pallas_call(
        final_kernel,
        out_shape=outs,
        in_specs=vmem(1),
        out_specs=vmem(4),
        cost_estimate=pl.CostEstimate(flops=1_000_000, bytes_accessed=200_000, transcendentals=0),
        name="final",
    )(whole)


def sum_sources(values):
    return jnp.sum(values.astype(F32), axis=0).astype(BF16)


def swap(values):
    return lax.ppermute(values, "lon", CORE)


def local(tokens, ocean_count, w_qkv, w_out, w_up, w_down, cotangent):
    flat = tokens.reshape(TOKEN)
    cot = cotangent.reshape(TOKEN)
    tok2 = lax.ppermute(flat, "lon", X_LO)
    count2 = lax.ppermute(ocean_count, "lon", X_LO)
    tok1 = swap(flat)
    count1 = swap(ocean_count)
    core = (lax.axis_index("lon") % 2).reshape(1)
    near = run_near(ocean_count, flat, w_qkv, w_down, cot)
    own_kv, query, inv_q, grad_active = near[:4], near[4], near[5], near[6]
    mate_kv = run_mate(tok1, w_qkv)
    tok3 = swap(tok2)
    count3 = swap(count2)
    front = run_front(
        core,
        (ocean_count, count1, count2, count3),
        (flat, tok2, tok3),
        w_qkv,
        w_out,
        w_up,
        w_down,
        cot,
        (query, own_kv[1], own_kv[2], mate_kv[1], mate_kv[2], grad_active),
    )
    block_out, keep1, send1, grad_middle = front[:4]
    recv1 = swap(send1)
    saved = [query, inv_q] + list(own_kv) + list(mate_kv) + list(front[4:])
    keep2, send2, *grads = run_back(core, saved)
    recv2 = swap(send2)
    for_core, for_x, grad_own = run_push(w_qkv, grads)
    joined = run_join(keep1, recv1, keep2, recv2)
    plane = sum_sources(
        lax.all_to_all(joined, ("lat", "lon"), 0, 0, axis_index_groups=PLANE_GROUPS, tiled=True)
    )
    from_core = swap(for_core).astype(F32)
    for_x = (for_x.astype(F32) + from_core[1]).astype(BF16)
    plane, for_x = lax.optimization_barrier((plane, for_x))
    column = sum_sources(
        lax.all_to_all(plane.reshape(8, 8, 1024), "lat", 0, 0, axis_index_groups=Z_GROUPS, tiled=True)
    )
    grad_normed = grad_own + from_core[0] + lax.ppermute(for_x, "lon", X_LO).astype(F32)
    normed, inverse = layer_norm(flat.astype(F32))
    grad_tokens = (grad_middle + layer_norm_back(normed, inverse, grad_normed)).astype(BF16)
    whole = lax.all_gather(column, "lon", axis=0, tiled=True)
    return (block_out.reshape(tokens.shape), grad_tokens.reshape(tokens.shape), *run_final(whole))


def solution(mesh):
    in_specs = (P("lat", "lon", None), P("lat", "lon"), P(), P(), P(), P(), P("lat", "lon", None))
    out_specs = (
        P("lat", "lon", None),
        P("lat", "lon", None),
        P("lat", None),
        P("lat", None),
        P("lat", None),
        P("lat", None),
    )
    return jax.shard_map(local, mesh=mesh, in_specs=in_specs, out_specs=out_specs, check_vma=False)
```

time: 170 us -> 98.1 us (0.58)
  local copies, waits for them, and re-layouts: 48.9 us -> 9.57 us
  matrix products: 30.8 us -> 0 us
  Pallas kernels: 0 us -> 16.6 us
  other arithmetic: 20.7 us -> 4.24 us
  starting transfers between devices: 24.4 us -> 20.7 us
  waiting for transfers between devices: 34.6 us -> 37.4 us
    dot_general x21 -> x0, matrix products: 30.8 us -> none  [elementwise_product(): jnp.einsum(pattern, left_side, right_side, preferred_element_type=jnp.flo...]
    all_to_all x2, waiting for transfers between devices: 5.92 us -> 34 us  [the longest x1 27.1 us: local(): lax.all_to_all(joined, ('lat', 'lon'), 0, 0, axis_index_groups=PLANE_GROU...]
    ppermute x9 -> x10, waiting for transfers between devices: 28.7 us -> 3.44 us  [the longest x7 3.43 us: swap(): return lax.ppermute(values, 'lon', CORE)]
    reshape x9 -> x0, local copies, waits for them, and re-layouts: 19.4 us -> none  [the longest x6 14.2 us: split_heads(): values.reshape(values.shape[:-1] + (head_count, values.shape[-1] // head_...]
    pallas_call x0 -> x7, Pallas kernels: none -> 16.6 us  [the longest x1 5.25 us: run_front(): pl.pallas_call(front_kernel, out_shape=outs, in_specs=smem(5) + vmem(8 +...]
    convert_element_type x10 -> x3, other arithmetic: 10.1 us -> 0.99 us  [the longest x1 0.86 us: local(): (grad_middle + layer_norm_back(normed, inverse, grad_normed)).astype(BF16)]
    mul x2 -> x1, local copies, waits for them, and re-layouts: 4.99 us -> 0.08 us  [mean_last(): return jnp.sum(values, axis=-1, keepdims=True) * (1.0 / values.shape[-1])]
    transpose x2 -> x0, local copies, waits for them, and re-layouts: 4.34 us -> none  [the longest x1 2.79 us: elementwise_product(): jnp.einsum(pattern, left_side, right_side, preferred_element_type=jnp.flo...]
  transfers between devices with their start and end apart: 11 -> 12, of which waited for: 4 -> 5; matrix products, arithmetic and copies ran while one was open for 9% -> 3% of each run, Pallas kernels for 0% -> 8%
where the time goes in v2:
time: 98.1 us; the launch traced here: 97.6 us
  waiting for transfers between devices  37.4 us (38%)
  starting transfers between devices  20.7 us (21%)
  Pallas kernels  16.6 us (17%)
  local copies, waits for them, and re-layouts  9.57 us (10%)
  blocking collectives  8.22 us (8%)
  other arithmetic  4.24 us (4%)
    all_to_all x1, waiting for transfers between devices, local(): lax.all_to_all(joined, ('lat', 'lon'), 0, 0, axis_index_groups=PLANE_GROU...  27.1 us
    unnamed x29, local copies, waits for them, and re-layouts  9.4 us
    all_to_all x1, starting transfers between devices, local(): lax.all_to_all(plane.reshape(8, 8, 1024), 'lat', 0, 0, axis_index_groups=...  8.25 us
    all_gather x1, blocking collectives, local(): whole = lax.all_gather(column, 'lon', axis=0, tiled=True)  8.22 us
    all_to_all x1, waiting for transfers between devices, local(): lax.all_to_all(plane.reshape(8, 8, 1024), 'lat', 0, 0, axis_index_groups=...  6.84 us
    ppermute x7, starting transfers between devices, swap(): return lax.ppermute(values, 'lon', CORE)  5.88 us
    pallas_call x1, Pallas kernels, run_front(): pl.pallas_call(front_kernel, out_shape=outs, in_specs=smem(5) + vmem(8 +...  5.25 us
    all_to_all x1, starting transfers between devices, local(): lax.all_to_all(joined, ('lat', 'lon'), 0, 0, axis_index_groups=PLANE_GROU...  5.08 us
  transfers between devices with their start and end apart: 12, of which 5 were waited for; matrix products, arithmetic and copies ran while one was open for 3% of the time, Pallas kernels for 8%

profile of v2, /device:TPU:1, one launch (start us, length us, event | category | flops | bytes accessed | tf_op | source)
XLA Modules:
  0.0 97.6 jit_solution(14004865876069936055)
XLA Ops:
  0.6 3.3 %collective-permute-start.5 = (bf16[192,512]{1,0:T(8,128)(2,1)}, bf16[192,512]{1,0:T(8,128)(2,1)S(1)}, u32[]{:S(2)}, u32[]{:S(2)}) collective-permute-start(bf16[192,512]{1,0:T(8,128)(2,1)} %bitcast.20), channel_id=1, source_target_pairs={{0,1},{1,0},{2,3},{3,2},{4,5},{5,4},{6,7},{7,6},{8,9},{9,8},{10,11... | collective-permute-start | bytes 589832 | tf_op jit(solution)/shard_map/ppermute | solution.py:512
  4.7 1.5 %collective-permute-start.1 = (s32[3,1]{1,0:T(4,128)S(1)}, s32[3,1]{1,0:T(4,128)S(1)}, u32[]{:S(2)}, u32[]{:S(2)}) collective-permute-start(s32[3,1]{1,0:T(4,128)S(1)} %copy.20.count_ref), channel_id=1, source_target_pairs={{0,2},{2,0},{1,3},{3,1},{4,6},{6,4},{5,7},{7,5},{8,10},{10,8},{9,1... | collective-permute-start | bytes 44 | tf_op jit(solution)/shard_map/ppermute | solution.py:519
  6.8 0.9 copy-done
  7.8 1.4 %copy-done.2 = bf16[512,1536]{1,0:T(8,128)(2,1)S(1)} copy-done((bf16[512,1536]{1,0:T(8,128)(2,1)S(1)}, bf16[512,1536]{1,0:T(8,128)(2,1)}, u32[]{:S(2)}) %copy-start.2) | copy-done | bytes 1572888
  9.2 1.2 %copy-done.5 = bf16[1024,512]{1,0:T(8,128)(2,1)S(1)} copy-done((bf16[1024,512]{1,0:T(8,128)(2,1)S(1)}, bf16[1024,512]{1,0:T(8,128)(2,1)}, u32[]{:S(2)}) %copy-start.5) | copy-done | bytes 1048600
  10.4 0.9 copy-done.8
  11.3 1.9 %near.1 = (bf16[192,512]{1,0:T(8,128)(2,1)S(1)}, bf16[192,512]{1,0:T(8,128)(2,1)S(1)}, bf16[192,512]{1,0:T(8,128)(2,1)S(1)}, bf16[192,512]{1,0:T(8,128)(2,1)S(1)...) custom-call(s32[3,1]{1,0:T(4,128)S(1)} %copy.20.count_ref, ...), custom_call_target="tpu_custom_call" | custom-call | flops 2500000000 | bytes 4000000 | tf_op jit(solution)/shard_map/near/pallas_call | solution.py:397
  15.0 5.2 %front.1 = (bf16[192,512]{1,0:T(8,128)(2,1)}, bf16[16,64,640]{2,1,0:T(8,128)(2,1)S(1)}, bf16[16,64,640]{2,1,0:T(8,128)(2,1)S(1)}, f32[192,512]{1,0:T(8,128)S(1)}...) custom-call(s32[1]{0:T(128)} %bitcast.core_ref, ...), custom_call_target="tpu_custom_call" | custom-call | flops 5000000000 | bytes 12000000 | tf_op jit(solution)/shard_map/front/pallas_call | solution.py:434
  20.9 4.1 %back.1 = (bf16[16,64,384]{2,1,0:T(8,128)(2,1)S(1)}, bf16[16,64,384]{2,1,0:T(8,128)(2,1)S(1)}, bf16[4,192,128]{2,1,0:T(8,128)(2,1)S(1)}, bf16[4,768,128]{2,1,0:T(8,128)(2,1)S(1)}, bf16[4,768,128]{2,1,0:T(8,128)(2,1)S(1)}) custom-call(s32[1]{0:T(128)} %bitcast.core_ref, bf16[192,512]{1,0:T(8,128)(2,1)S(1)} %get-tuple-element.41.query_ref, ...), custom_call_target="tpu_custom_call" | custom-call | flops 6000000000 | bytes 12000000 | tf_op jit(solution)/shard_map/back/pallas_call | solution.py:459
  25.0 0.9 copy-done.10
  25.9 0.9 copy-done.12
  27.0 2.1 %collective-permute-done.8.recv2_ref = bf16[16,64,384]{2,1,0:T(8,128)(2,1)S(1)} collective-permute-done((bf16[16,64,384]{2,1,0:T(8,128)(2,1)S(1)}, bf16[16,64,384]{2,1,0:T(8,128)(2,1)S(1)}, u32[]{:S(2)}, u32[]{:S(2)}) %collective-permute-start.8) | collective-permute-done | bytes 786464 | tf_op jit(solution)/shard_map/ppermute | solution.py:512
  29.1 1.8 %join.1 = bf16[16,64,1024]{2,1,0:T(8,128)(2,1)} custom-call(bf16[16,64,640]{2,1,0:T(8,128)(2,1)S(1)} %get-tuple-element.65.keep1_ref, bf16[16,64,640]{2,1,0:T(8,128)(2,1)S(1)} %collective-permute-done.7.recv1_ref, bf16[16,64,384]{2,1,0:T(8,128)(2,1)S(1)} %get-tuple-element.67.keep2_ref, bf16[16,64,384]{2,1,0:T(8,128)(2,1)S(1)} %collective-permute-done.8.recv2_ref), custom_call_target="tpu_custom_call" | custom-call | flops 1000000 | bytes 6000000 | tf_op jit(solution)/shard_map/join/pallas_call | solution.py:484
  30.9 5.1 %all-to-all-start = ((bf16[16,64,1024]{2,1,0:T(8,128)(2,1)}), bf16[16,64,1024]{2,1,0:T(8,128)(2,1)}, u32[]{:S(2)}, u32[]{:S(2)}) async-start(bf16[16,64,1024]{2,1,0:T(8,128)(2,1)} %join.1), calls=%async_computation | async-start | bytes 4194304 | tf_op jit(solution)/shard_map/all_to_all | solution.py:547
  36.0 1.1 %copy-done.11 = bf16[4,768,128]{2,1,0:T(8,128)(2,1)S(1)} copy-done((bf16[4,768,128]{2,1,0:T(8,128)(2,1)S(1)}, bf16[4,768,128]{2,1,0:T(8,128)(2,1)}, u32[]{:S(2)}) %copy-start.11) | copy-done | bytes 786456
  37.1 1.1 %copy-done.13 = bf16[4,768,128]{2,1,0:T(8,128)(2,1)S(1)} copy-done((bf16[4,768,128]{2,1,0:T(8,128)(2,1)S(1)}, bf16[4,768,128]{2,1,0:T(8,128)(2,1)}, u32[]{:S(2)}) %copy-start.13) | copy-done | bytes 786456
  38.3 1.4 %push.1 = (bf16[2,192,512]{2,1,0:T(8,128)(2,1)S(1)}, bf16[192,512]{1,0:T(8,128)(2,1)S(1)}, f32[192,512]{1,0:T(8,128)S(1)}) custom-call(bf16[512,1536]{1,0:T(8,128)(2,1)S(1)} %copy-done.3, bf16[4,192,128]{2,1,0:T(8,128)(2,1)S(1)} %get-tuple-element.60.gq_ref, bf16[4,768,128]{2,1,0:T(8,128)(2,1)S(1)} %copy-done.11, bf16[4,768,128]{2,1,0:T(8,128)(2,1)S(1)} %copy-done.13), custom_call_target="tpu_custom_call" | custom-call | flops 2000000000 | bytes 4000000 | tf_op jit(solution)/shard_map/push/pallas_call | solution.py:472
  40.6 1.0 collective-permute-done.6
  41.7 27.1 %all-to-all-done = bf16[16,64,1024]{2,1,0:T(8,128)(2,1)} async-done(((bf16[16,64,1024]{2,1,0:T(8,128)(2,1)}), bf16[16,64,1024]{2,1,0:T(8,128)(2,1)}, u32[]{:S(2)}, u32[]{:S(2)}) %all-to-all-start) | async-done | bytes 2097184 | tf_op jit(solution)/shard_map/all_to_all | solution.py:547
  68.9 2.7 %reduce_sum.62 = bf16[64,1024]{1,0:T(8,128)(2,1)} reduce(bf16[16,64,1024]{2,1,0:T(8,128)(2,1)} %all-to-all-done, bf16[]{:T(256)} %constant.25.clone.1), dimensions={0}, to_apply=%region_2.3 | reduce | flops 983040 | bytes 2228226 | tf_op jit(solution)/shard_map/reduce_sum | solution.py:508
  71.6 8.2 %all-to-all-start.1 = ((bf16[8,8,1024]{2,1,0:T(8,128)(2,1)}), bf16[8,8,1024]{2,1,0:T(8,128)(2,1)S(1)}, u32[]{:S(2)}, u32[]{:S(2)}) async-start(bf16[8,8,1024]{2,1,0:T(8,128)(2,1)} %bitcast.7), calls=%async_computation.1 | async-start | bytes 262144 | tf_op jit(solution)/shard_map/all_to_all | solution.py:553
  81.0 6.8 %all-to-all-done.1 = bf16[8,8,1024]{2,1,0:T(8,128)(2,1)S(1)} async-done(((bf16[8,8,1024]{2,1,0:T(8,128)(2,1)}), bf16[8,8,1024]{2,1,0:T(8,128)(2,1)S(1)}, u32[]{:S(2)}, u32[]{:S(2)}) %all-to-all-start.1) | async-done | bytes 131104 | tf_op jit(solution)/shard_map/all_to_all | solution.py:553
  87.9 8.2 %all_gather.3.whole_ref = bf16[32,1024]{1,0:T(8,128)(2,1)} all-gather(bf16[8,1024]{1,0:T(8,128)(2,1)S(1)} %reduce_sum.65), channel_id=1, replica_groups=mesh['lat'=64,'lon'=4] {'lon'}, dimensions={0}, use_global_device_ids=true | all-gather | bytes 81920 | tf_op jit(solution)/shard_map/all_gather | solution.py:558
  96.1 1.5 %final.1 = (f32[8,1536]{1,0:T(8,128)}, f32[8,512]{1,0:T(8,128)}, f32[8,1024]{1,0:T(8,128)}, f32[16,512]{1,0:T(8,128)}) custom-call(bf16[32,1024]{1,0:T(8,128)(2,1)} %all_gather.3.whole_ref), custom_call_target="tpu_custom_call" | custom-call | flops 1000000 | bytes 200000 | tf_op jit(solution)/shard_map/final/pallas_call | solution.py:497
  (50 shorter events, 6.2 us)
Async XLA Ops:
  0.6 13.2 %collective-permute-start.5 = (bf16[192,512]{1,0:T(8,128)(2,1)}, bf16[192,512]{1,0:T(8,128)(2,1)S(1)}, u32[]{:S(2)}, u32[]{:S(2)}) collective-permute-start(bf16[192,512]{1,0:T(8,128)(2,1)} %bitcast.20), channel_id=1, source_target_pairs={{0,1},{1,0},{2,3},{3,2},{4,5},{5,4},{6,7},{7,6},{8,9},{9,8},{10,11... | collective-permute-start | bytes 589832 | tf_op jit(solution)/shard_map/ppermute | solution.py:512
  4.0 9.4 %collective-permute-start.3 = (bf16[192,512]{1,0:T(8,128)(2,1)}, bf16[192,512]{1,0:T(8,128)(2,1)S(1)}, u32[]{:S(2)}, u32[]{:S(2)}) collective-permute-start(bf16[192,512]{1,0:T(8,128)(2,1)} %bitcast.21), channel_id=1, source_target_pairs={{0,2},{2,0},{1,3},{3,1},{4,6},{6,4},{5,7},{7,5},{8,10},{10,8},{9,1... | collective-permute-start | bytes 589832 | tf_op jit(solution)/shard_map/ppermute | solution.py:518
  4.7 8.5 %collective-permute-start.1 = (s32[3,1]{1,0:T(4,128)S(1)}, s32[3,1]{1,0:T(4,128)S(1)}, u32[]{:S(2)}, u32[]{:S(2)}) collective-permute-start(s32[3,1]{1,0:T(4,128)S(1)} %copy.20.count_ref), channel_id=1, source_target_pairs={{0,2},{2,0},{1,3},{3,1},{4,6},{6,4},{5,7},{7,5},{8,10},{10,8},{9,1... | collective-permute-start | bytes 44 | tf_op jit(solution)/shard_map/ppermute | solution.py:519
  6.2 8.4 %collective-permute-start = (s32[3,1]{1,0:T(4,128)S(1)}, s32[3,1]{1,0:T(4,128)S(1)}, u32[]{:S(2)}, u32[]{:S(2)}) collective-permute-start(s32[3,1]{1,0:T(4,128)S(1)} %copy.20.count_ref), channel_id=1, source_target_pairs={{0,1},{1,0},{2,3},{3,2},{4,5},{5,4},{6,7},{7,6},{8,9},{9,8},{10,11... | collective-permute-start | bytes 44 | tf_op jit(solution)/shard_map/ppermute | solution.py:512
  6.8 0.9 copy-start
  7.8 1.4 %copy-start.2 = (bf16[512,1536]{1,0:T(8,128)(2,1)S(1)}, bf16[512,1536]{1,0:T(8,128)(2,1)}, u32[]{:S(2)}) copy-start(bf16[512,1536]{1,0:T(8,128)(2,1)} %w_qkv_ref.7) | copy-start | bytes 4718596
  9.2 1.2 %copy-start.5 = (bf16[1024,512]{1,0:T(8,128)(2,1)S(1)}, bf16[1024,512]{1,0:T(8,128)(2,1)}, u32[]{:S(2)}) copy-start(bf16[1024,512]{1,0:T(8,128)(2,1)} %w_down_ref.3) | copy-start | bytes 3145732
  10.4 0.9 copy-start.8
  11.3 2.5 %copy-start.3 = (bf16[512,1536]{1,0:T(8,128)(2,1)S(1)}, bf16[512,1536]{1,0:T(8,128)(2,1)}, u32[]{:S(2)}) copy-start(bf16[512,1536]{1,0:T(8,128)(2,1)} %w_qkv_ref.7) | copy-start | bytes 4718596
  13.2 1.7 %copy-start.1 = (bf16[3,64,512]{2,1,0:T(8,128)(2,1)S(1)}, bf16[3,64,512]{2,1,0:T(8,128)(2,1)}, u32[]{:S(2)}) copy-start(bf16[3,64,512]{2,1,0:T(8,128)(2,1)} %param.7) | copy-start | bytes 589828
  13.2 1.7 %copy-start.4 = (bf16[512,1024]{1,0:T(8,128)(2,1)S(1)}, bf16[512,1024]{1,0:T(8,128)(2,1)}, u32[]{:S(2)}) copy-start(bf16[512,1024]{1,0:T(8,128)(2,1)} %w_up_ref.1) | copy-start | bytes 3145732
  13.2 1.7 %copy-start.6 = (bf16[1024,512]{1,0:T(8,128)(2,1)S(1)}, bf16[1024,512]{1,0:T(8,128)(2,1)}, u32[]{:S(2)}) copy-start(bf16[1024,512]{1,0:T(8,128)(2,1)} %w_down_ref.3) | copy-start | bytes 3145732
  13.2 1.8 %copy-start.7 = (bf16[512,512]{1,0:T(8,128)(2,1)S(1)}, bf16[512,512]{1,0:T(8,128)(2,1)}, u32[]{:S(2)}) copy-start(bf16[512,512]{1,0:T(8,128)(2,1)} %w_out_ref.1) | copy-start | bytes 1572868
  13.2 1.8 %copy-start.9 = (bf16[3,64,512]{2,1,0:T(8,128)(2,1)S(1)}, bf16[3,64,512]{2,1,0:T(8,128)(2,1)}, u32[]{:S(2)}) copy-start(bf16[3,64,512]{2,1,0:T(8,128)(2,1)} %param.13) | copy-start | bytes 589828
  13.2 1.3 %collective-permute-start.2 = (s32[3,1]{1,0:T(4,128)S(1)}, s32[3,1]{1,0:T(4,128)S(1)}, u32[]{:S(2)}, u32[]{:S(2)}) collective-permute-start(s32[3,1]{1,0:T(4,128)S(1)} %collective-permute-done.1.count2_ref), channel_id=1, source_target_pairs={{0,1},{1,0},{2,3},{3,2},{4,5},{5,4},{6,7},{7,6},{8,9},{9,8},{10,11... | collective-permute-start | bytes 44 | tf_op jit(solution)/shard_map/ppermute | solution.py:512
  13.4 1.6 %collective-permute-start.4 = (bf16[192,512]{1,0:T(8,128)(2,1)S(1)}, bf16[192,512]{1,0:T(8,128)(2,1)S(1)}, u32[]{:S(2)}, u32[]{:S(2)}) collective-permute-start(bf16[192,512]{1,0:T(8,128)(2,1)S(1)} %collective-permute-done.3.tok2_ref), channel_id=1, source_target_pairs={{0,1},{1,0},{2,3},{3,2},{4,5},{5,4},{6,7},{7,6},{8,9},{9,8},{10,11... | collective-permute-start | bytes 589832 | tf_op jit(solution)/shard_map/ppermute | solution.py:512
  20.3 8.8 %collective-permute-start.7 = (bf16[16,64,640]{2,1,0:T(8,128)(2,1)S(1)}, bf16[16,64,640]{2,1,0:T(8,128)(2,1)S(1)}, u32[]{:S(2)}, u32[]{:S(2)}) collective-permute-start(bf16[16,64,640]{2,1,0:T(8,128)(2,1)S(1)} %get-tuple-element.66), channel_id=1, source_target_pairs={{0,1},{1,0},{2,3},{3,2},{4,5},{5,4},{6,7},{7,6},{8,9},{9,8},{10,11... | collective-permute-start | bytes 3932168 | tf_op jit(solution)/shard_map/ppermute | solution.py:512
  26.8 2.3 %collective-permute-start.8 = (bf16[16,64,384]{2,1,0:T(8,128)(2,1)S(1)}, bf16[16,64,384]{2,1,0:T(8,128)(2,1)S(1)}, u32[]{:S(2)}, u32[]{:S(2)}) collective-permute-start(bf16[16,64,384]{2,1,0:T(8,128)(2,1)S(1)} %get-tuple-element.68), channel_id=1, source_target_pairs={{0,1},{1,0},{2,3},{3,2},{4,5},{5,4},{6,7},{7,6},{8,9},{9,8},{10,11... | collective-permute-start | bytes 2359304 | tf_op jit(solution)/shard_map/ppermute | solution.py:512
  30.9 37.9 %all-to-all-start = ((bf16[16,64,1024]{2,1,0:T(8,128)(2,1)}), bf16[16,64,1024]{2,1,0:T(8,128)(2,1)}, u32[]{:S(2)}, u32[]{:S(2)}) async-start(bf16[16,64,1024]{2,1,0:T(8,128)(2,1)} %join.1), calls=%async_computation | async-start | bytes 4194304 | tf_op jit(solution)/shard_map/all_to_all | solution.py:547
  36.0 1.1 %copy-start.11 = (bf16[4,768,128]{2,1,0:T(8,128)(2,1)S(1)}, bf16[4,768,128]{2,1,0:T(8,128)(2,1)}, u32[]{:S(2)}) copy-start(bf16[4,768,128]{2,1,0:T(8,128)(2,1)} %copy-done.10) | copy-start | bytes 2359300
  37.1 1.1 %copy-start.13 = (bf16[4,768,128]{2,1,0:T(8,128)(2,1)S(1)}, bf16[4,768,128]{2,1,0:T(8,128)(2,1)}, u32[]{:S(2)}) copy-start(bf16[4,768,128]{2,1,0:T(8,128)(2,1)} %copy-done.12) | copy-start | bytes 2359300
  39.7 1.9 %collective-permute-start.6 = (bf16[2,192,512]{2,1,0:T(8,128)(2,1)S(1)}, bf16[2,192,512]{2,1,0:T(8,128)(2,1)S(1)}, u32[]{:S(2)}, u32[]{:S(2)}) collective-permute-start(bf16[2,192,512]{2,1,0:T(8,128)(2,1)S(1)} %get-tuple-element.64), channel_id=1, source_target_pairs={{0,1},{1,0},{2,3},{3,2},{4,5},{5,4},{6,7},{7,6},{8,9},{9,8},{10,11... | collective-permute-start | bytes 1179656 | tf_op jit(solution)/shard_map/ppermute | solution.py:512
  71.5 8.3 %collective-permute-start.9 = (bf16[192,512]{1,0:T(8,128)(2,1)S(1)}, bf16[192,512]{1,0:T(8,128)(2,1)S(1)}, u32[]{:S(2)}, u32[]{:S(2)}) collective-permute-start(bf16[192,512]{1,0:T(8,128)(2,1)S(1)} %fusion.3), channel_id=1, source_target_pairs={{0,2},{2,0},{1,3},{3,1},{4,6},{6,4},{5,7},{7,5},{8,10},{10,8},{9,1... | collective-permute-start | bytes 589832 | tf_op jit(solution)/shard_map/ppermute | solution.py:555
  71.6 16.2 %all-to-all-start.1 = ((bf16[8,8,1024]{2,1,0:T(8,128)(2,1)}), bf16[8,8,1024]{2,1,0:T(8,128)(2,1)S(1)}, u32[]{:S(2)}, u32[]{:S(2)}) async-start(bf16[8,8,1024]{2,1,0:T(8,128)(2,1)} %bitcast.7), calls=%async_computation.1 | async-start | bytes 262144 | tf_op jit(solution)/shard_map/all_to_all | solution.py:553
  (2 other events, 1.8 us)

commit v3 on v2

--- a/solution.py
+++ b/solution.py
@@ -31,6 +31,7 @@
 
 CORE = [(0, 1), (1, 0), (2, 3), (3, 2)]
 X_LO = [(0, 2), (2, 0), (1, 3), (3, 1)]
+DIAGONAL = [(0, 3), (3, 0), (1, 2), (2, 1)]
 Z_GROUPS = [[lat_index(z, y, x) for z in range(8)] for y in range(4) for x in range(2)]
 PLANE_GROUPS = [
     [lat_index(z, y, x_hi) * 4 + x_lo * 2 + core for y in range(4) for x_hi in range(2) for x_lo in range(2)]
@@ -131,8 +132,26 @@
 
 
 def near_kernel(
+    tok0_ref,
+    w_qkv_ref,
+    normed_ref,
+    key_ref,
+    value_ref,
+    inv_k_ref,
+    query_ref,
+    inv_q_ref,
+):
+    blocks = head_blocks()
+    normed = key_value(tok0_ref, w_qkv_ref, blocks, 0, 1, normed_ref, key_ref, value_ref, inv_k_ref)
+    query_raw = mm(normed, w_qkv_ref[:, :WIDTH])
+    inv_q = lax.rsqrt(head_mean(query_raw * query_raw, blocks) + 1e-06)
+    inv_q_ref[...] = inv_q.astype(BF16)
+    query_ref[...] = (query_raw * inv_q).astype(BF16)
+
+
+def mate_kernel(
     count_ref,
-    tok0_ref,
+    tok1_ref,
     w_qkv_ref,
     w_down_ref,
     cot_ref,
@@ -140,21 +159,10 @@
     key_ref,
     value_ref,
     inv_k_ref,
-    query_ref,
-    inv_q_ref,
     grad_active_ref,
 ):
-    blocks = head_blocks()
-    normed = key_value(tok0_ref, w_qkv_ref, blocks, 0, 1, normed_ref, key_ref, value_ref, inv_k_ref)
-    query_raw = mm(normed, w_qkv_ref[:, :WIDTH])
-    inv_q = lax.rsqrt(head_mean(query_raw * query_raw, blocks) + 1e-06)
-    inv_q_ref[...] = inv_q.astype(BF16)
-    query_ref[...] = (query_raw * inv_q).astype(BF16)
     branch = (own_mask(count_ref) * cot_ref[...].astype(F32)).astype(BF16)
     grad_active_ref[...] = mm_nt(branch, w_down_ref[...]).astype(BF16)
-
-
-def mate_kernel(tok1_ref, w_qkv_ref, normed_ref, key_ref, value_ref, inv_k_ref):
     key_value(tok1_ref, w_qkv_ref, head_blocks(), 0, 1, normed_ref, key_ref, value_ref, inv_k_ref)
 
 
@@ -251,13 +259,14 @@
         attn_ref[part] = grad_attn[:, part * 128 : (part + 1) * 128]
     for part in range(2):
         branch_ref[part] = branch[:, part * 256 : (part + 1) * 256]
+    attended_t, normed_two_t, active_t = attended.T, normed_two_b.T, active.T
     for out_ref, half_index in ((keep_ref, core), (send_ref, 1 - core)):
         pair = jnp.concatenate([attn_ref[half_index], attn_ref[half_index + 2]], axis=1)
-        term_out = mm_tn(attended, pair)
+        term_out = mm(attended_t, pair)
         for x_lo in range(2):
             store_pieces(out_ref, x_lo, 0, term_out[:, x_lo * 128 : (x_lo + 1) * 128])
-            store_pieces(out_ref, x_lo, 128, mm_tn(normed_two_b, lift_ref[half_index + 2 * x_lo]))
-        term_down = mm_tn(active, branch_ref[half_index]).reshape(64, 2, 8, 256)
+            store_pieces(out_ref, x_lo, 128, mm(normed_two_t, lift_ref[half_index + 2 * x_lo]))
+        term_down = mm(active_t, branch_ref[half_index]).reshape(64, 2, 8, 256)
         for x_lo in range(2):
             store_pieces(out_ref, x_lo, 384, term_down[:, x_lo].reshape(512, 256))
 
@@ -327,13 +336,14 @@
                     ref[group * 2 + part, far, :] = grad[2 * SECTOR :, at]
 
     normed_all = jnp.concatenate([own_normed_ref[...], mate_normed_ref[...], normed_ref[...]], axis=0)
+    own_normed_t, normed_all_t = own_normed_ref[...].T, normed_all.T
     for out_ref, half_index in ((keep_ref, core), (send_ref, 1 - core)):
         pair = jnp.concatenate([gq_ref[half_index], gq_ref[half_index + 2]], axis=1)
-        term_q = mm_tn(own_normed_ref[...], pair)
+        term_q = mm(own_normed_t, pair)
         for x_lo in range(2):
             store_pieces(out_ref, x_lo, 0, term_q[:, x_lo * 128 : (x_lo + 1) * 128])
             pair = jnp.concatenate([gk_ref[half_index + 2 * x_lo], gv_ref[half_index + 2 * x_lo]], axis=1)
-            store_pieces(out_ref, x_lo, 128, mm_tn(normed_all, pair))
+            store_pieces(out_ref, x_lo, 128, mm(normed_all_t, pair))
 
 
 def push_kernel(w_qkv_ref, gq_ref, gk_ref, gv_ref, for_core_ref, for_x_ref, own_ref):
@@ -352,16 +362,38 @@
     own_ref[...] = grad_normed(slice(0, TOKENS)) + mm_nt(grad_q, w_qkv_ref[:, :WIDTH])
 
 
-def join_kernel(keep1_ref, recv1_ref, keep2_ref, recv2_ref, out_ref):
+def join_kernel(keep1_ref, recv1_ref, keep2_ref, recv2_ref, after_ref, out_ref):
+    del after_ref
     for piece in range(16):
         out_ref[piece, :, :384] = (keep2_ref[piece].astype(F32) + recv2_ref[piece].astype(F32)).astype(BF16)
         out_ref[piece, :, 384:] = (keep1_ref[piece].astype(F32) + recv1_ref[piece].astype(F32)).astype(BF16)
 
 
-def final_kernel(whole_ref, qkv_ref, out_ref, up_ref, down_ref):
-    whole = whole_ref[...].astype(F32) * (1.0 / math.sqrt(64 * 4 * TOKENS))
+def add_x_kernel(for_x_ref, recv_core_ref, out_ref):
+    out_ref[...] = (for_x_ref[...].astype(F32) + recv_core_ref[1].astype(F32)).astype(BF16)
+
+
+def sum_kernel(parts_ref, out_ref):
+    total = parts_ref[0].astype(F32)
+    for part in range(1, parts_ref.shape[0]):
+        total = total + parts_ref[part].astype(F32)
+    out_ref[...] = total.astype(BF16)
+
+
+def finish_kernel(tok_ref, own_ref, recv_core_ref, from_x_ref, middle_ref, out_ref):
+    grad = own_ref[...] + recv_core_ref[0].astype(F32) + from_x_ref[...].astype(F32)
+    normed, inverse = layer_norm(tok_ref[...].astype(F32))
+    out_ref[...] = (middle_ref[...] + layer_norm_back(normed, inverse, grad)).astype(BF16)
+
+
+def final_kernel(lon_ref, own_ref, core_ref, x_ref, diagonal_ref, qkv_ref, out_ref, up_ref, down_ref):
+    lon = lon_ref[0]
+    scale = 1.0 / math.sqrt(64 * 4 * TOKENS)
+    held = [ref[...].astype(F32) * scale for ref in (own_ref, core_ref, x_ref, diagonal_ref)]
     for quarter in range(4):
-        part = whole[quarter * 8 : (quarter + 1) * 8]
+        part = held[3]
+        for distance in range(3):
+            part = jnp.where(lon == (quarter ^ distance), held[distance], part)
         at = slice(quarter * 128, (quarter + 1) * 128)
         for matrix in range(3):
             low = matrix * WIDTH + quarter * 128
@@ -392,30 +424,30 @@
     return pltpu.CompilerParams(vmem_limit_bytes=megabytes * 1024 * 1024)
 
 
-def run_near(count, tok0, w_qkv, w_down, cot):
-    outs = [shape(TOKEN, BF16)] * 6 + [shape((TOKENS, HIDDEN), BF16)]
+def run_near(tok0, w_qkv):
+    outs = [shape(TOKEN, BF16)] * 6
     return pl.pallas_call(
         near_kernel,
+        out_shape=outs,
+        in_specs=vmem(2),
+        out_specs=vmem(len(outs)),
+        compiler_params=params(NEAR_MB),
+        cost_estimate=pl.CostEstimate(flops=2_500_000_000, bytes_accessed=4_000_000, transcendentals=0),
+        name="near",
+    )(tok0, w_qkv)
+
+
+def run_mate(count, tok1, w_qkv, w_down, cot):
+    outs = [shape(TOKEN, BF16)] * 4 + [shape((TOKENS, HIDDEN), BF16)]
+    return pl.pallas_call(
+        mate_kernel,
         out_shape=outs,
         in_specs=smem(1) + vmem(4),
         out_specs=vmem(len(outs)),
         compiler_params=params(NEAR_MB),
-        cost_estimate=pl.CostEstimate(flops=2_500_000_000, bytes_accessed=4_000_000, transcendentals=0),
-        name="near",
-    )(count, tok0, w_qkv, w_down, cot)
-
-
-def run_mate(tok1, w_qkv):
-    outs = [shape(TOKEN, BF16)] * 4
-    return pl.pallas_call(
-        mate_kernel,
-        out_shape=outs,
-        in_specs=vmem(2),
-        out_specs=vmem(len(outs)),
-        compiler_params=params(NEAR_MB),
         cost_estimate=pl.CostEstimate(flops=5_000_000_000, bytes_accessed=2_000_000, transcendentals=0),
         name="mate",
-    )(tok1, w_qkv)
+    )(count, tok1, w_qkv, w_down, cot)
 
 
 def run_front(core, counts, sectors, w_qkv, w_out, w_up, w_down, cot, near):
@@ -480,28 +512,45 @@
     )(w_qkv, *grads)
 
 
-def run_join(*halves):
+def small_call(kernel, outs, scalars, arrays, name):
+    return pl.pallas_call(
+        kernel,
+        out_shape=outs,
+        in_specs=smem(len(scalars)) + vmem(len(arrays)),
+        out_specs=vmem(len(outs)),
+        compiler_params=params(NEAR_MB),
+        cost_estimate=pl.CostEstimate(flops=1_000_000, bytes_accessed=4_000_000, transcendentals=0),
+        name=name,
+    )(*scalars, *arrays)
+
+
+def run_join(keep1, recv1, keep2, recv2, after):
     return pl.pallas_call(
         join_kernel,
         out_shape=shape((16, 64, 1024), BF16),
-        in_specs=vmem(4),
+        in_specs=vmem(4) + [pl.BlockSpec(memory_space=pl.ANY)],
         out_specs=vmem(1)[0],
         compiler_params=params(NEAR_MB),
-        cost_estimate=pl.CostEstimate(flops=1_000_000, bytes_accessed=6_000_000, transcendentals=0),
+        cost_estimate=pl.CostEstimate(flops=1_000_000, bytes_accessed=4_000_000, transcendentals=0),
         name="join",
-    )(*halves)
-
-
-def run_final(whole):
+    )(keep1, recv1, keep2, recv2, after)
+
+
+def run_add_x(*parts):
+    return small_call(add_x_kernel, [shape(TOKEN, BF16)], [], parts, "add_x")[0]
+
+
+def run_sum(parts):
+    return small_call(sum_kernel, [shape((64, 1024), BF16)], [], [parts], "plane_sum")[0]
+
+
+def run_finish(*parts):
+    return small_call(finish_kernel, [shape(TOKEN, BF16)], [], parts, "finish")[0]
+
+
+def run_final(lon, parts):
     outs = [shape((8, 1536), F32), shape((8, 512), F32), shape((8, 1024), F32), shape((16, 512), F32)]
-    return pl.pallas_call(
-        final_kernel,
-        out_shape=outs,
-        in_specs=vmem(1),
-        out_specs=vmem(4),
-        cost_estimate=pl.CostEstimate(flops=1_000_000, bytes_accessed=200_000, transcendentals=0),
-        name="final",
-    )(whole)
+    return small_call(final_kernel, outs, [lon], parts, "final")
 
 
 def sum_sources(values):
@@ -519,10 +568,10 @@
     count2 = lax.ppermute(ocean_count, "lon", X_LO)
     tok1 = swap(flat)
     count1 = swap(ocean_count)
-    core = (lax.axis_index("lon") % 2).reshape(1)
-    near = run_near(ocean_count, flat, w_qkv, w_down, cot)
-    own_kv, query, inv_q, grad_active = near[:4], near[4], near[5], near[6]
-    mate_kv = run_mate(tok1, w_qkv)
+    lon = lax.axis_index("lon")
+    core = (lon % 2).reshape(1)
+    *own_kv, query, inv_q = run_near(flat, w_qkv)
+    *mate_kv, grad_active = run_mate(ocean_count, tok1, w_qkv, w_down, cot)
     tok3 = swap(tok2)
     count3 = swap(count2)
     front = run_front(
@@ -542,21 +591,18 @@
     keep2, send2, *grads = run_back(core, saved)
     recv2 = swap(send2)
     for_core, for_x, grad_own = run_push(w_qkv, grads)
-    joined = run_join(keep1, recv1, keep2, recv2)
-    plane = sum_sources(
-        lax.all_to_all(joined, ("lat", "lon"), 0, 0, axis_index_groups=PLANE_GROUPS, tiled=True)
-    )
-    from_core = swap(for_core).astype(F32)
-    for_x = (for_x.astype(F32) + from_core[1]).astype(BF16)
-    plane, for_x = lax.optimization_barrier((plane, for_x))
+    recv_core = swap(for_core)
+    joined = run_join(keep1, recv1, keep2, recv2, recv_core)
+    plane = lax.all_to_all(joined, ("lat", "lon"), 0, 0, axis_index_groups=PLANE_GROUPS, tiled=True)
+    plane, for_x, recv_core = lax.optimization_barrier((run_sum(plane), for_x, recv_core))
+    from_x = lax.ppermute(run_add_x(for_x, recv_core), "lon", X_LO)
     column = sum_sources(
         lax.all_to_all(plane.reshape(8, 8, 1024), "lat", 0, 0, axis_index_groups=Z_GROUPS, tiled=True)
     )
-    grad_normed = grad_own + from_core[0] + lax.ppermute(for_x, "lon", X_LO).astype(F32)
-    normed, inverse = layer_norm(flat.astype(F32))
-    grad_tokens = (grad_middle + layer_norm_back(normed, inverse, grad_normed)).astype(BF16)
-    whole = lax.all_gather(column, "lon", axis=0, tiled=True)
-    return (block_out.reshape(tokens.shape), grad_tokens.reshape(tokens.shape), *run_final(whole))
+    gathered = [column] + [lax.ppermute(column, "lon", table) for table in (CORE, X_LO, DIAGONAL)]
+    grad_tokens = run_finish(flat, grad_own, recv_core, from_x, grad_middle)
+    weights = run_final(lon.reshape(1), gathered)
+    return (block_out.reshape(tokens.shape), grad_tokens.reshape(tokens.shape), *weights)
 
 
 def solution(mesh):

time: 98.1 us -> 85.6 us (0.87)
  waiting for transfers between devices: 37.4 us -> 10.5 us
  blocking collectives: 8.22 us -> 33.6 us
  local copies, waits for them, and re-layouts: 9.57 us -> 3.14 us
  other arithmetic: 4.24 us -> 0.02 us
    all_to_all x0 -> x1, blocking collectives: none -> 33.6 us  [local(): lax.all_to_all(joined, ('lat', 'lon'), 0, 0, axis_index_groups=PLANE_GROU...]
    all_to_all x1 -> x0, waiting for transfers between devices: 27.1 us -> none  [local(): lax.all_to_all(joined, ('lat', 'lon'), 0, 0, axis_index_groups=PLANE_GROU...]
    all_gather x1 -> x0, blocking collectives: 8.22 us -> none  [local(): whole = lax.all_gather(column, 'lon', axis=0, tiled=True)]
    unnamed x29 -> x17, local copies, waits for them, and re-layouts: 9.4 us -> 3.14 us
    all_to_all x1 -> x0, starting transfers between devices: 5.08 us -> none  [local(): lax.all_to_all(joined, ('lat', 'lon'), 0, 0, axis_index_groups=PLANE_GROU...]
    ppermute x1 -> x4, starting transfers between devices: 0.01 us -> 4.81 us  [the longest x3 4.44 us: local(): lax.ppermute(column, 'lon', table)]
    reduce_sum x2 -> x1, other arithmetic: 2.7 us -> 0.02 us  [sum_sources(): return jnp.sum(values.astype(F32), axis=0).astype(BF16)]
    ppermute x7, waiting for transfers between devices: 3.43 us -> 1.72 us  [swap(): return lax.ppermute(values, 'lon', CORE)]
  transfers between devices with their start and end apart: 12 -> 14, of which waited for: 5 -> 4; matrix products, arithmetic and copies ran while one was open for 3% -> 0% of each run, Pallas kernels for 8% -> 11%
where the time goes in v3:
time: 85.6 us; the launch traced here: 85.4 us
  blocking collectives  33.6 us (39%)
  starting transfers between devices  20.9 us (24%)
  Pallas kernels  16.4 us (19%)
  waiting for transfers between devices  10.5 us (12%)
  local copies, waits for them, and re-layouts  3.14 us (4%)
    all_to_all x1, blocking collectives, local(): lax.all_to_all(joined, ('lat', 'lon'), 0, 0, axis_index_groups=PLANE_GROU...  33.6 us
    all_to_all x1, starting transfers between devices, local(): lax.all_to_all(plane.reshape(8, 8, 1024), 'lat', 0, 0, axis_index_groups=...  8.21 us
    all_to_all x1, waiting for transfers between devices, local(): lax.all_to_all(plane.reshape(8, 8, 1024), 'lat', 0, 0, axis_index_groups=...  7.51 us
    pallas_call x1, Pallas kernels, run_front(): pl.pallas_call(front_kernel, out_shape=outs, in_specs=smem(5) + vmem(8 +...  5.32 us
    ppermute x3, starting transfers between devices, local(): lax.ppermute(column, 'lon', table)  4.44 us
    ppermute x7, starting transfers between devices, swap(): return lax.ppermute(values, 'lon', CORE)  4.19 us
    pallas_call x1, Pallas kernels, run_back(): pl.pallas_call(back_kernel, out_shape=outs, in_specs=smem(1) + vmem(len(s...  4.16 us
    unnamed x17, local copies, waits for them, and re-layouts  3.14 us
  transfers between devices with their start and end apart: 14, of which 4 were waited for; matrix products, arithmetic and copies ran while one was open for 0% of the time, Pallas kernels for 11%

profile of v3, /device:TPU:1, one launch (start us, length us, event | category | flops | bytes accessed | tf_op | source)
XLA Modules:
  0.0 85.4 jit_solution(16408596979642190943)
XLA Ops:
  0.6 0.7 copy.16.count_ref
  1.4 2.0 %collective-permute-start.1 = (s32[3,1]{1,0:T(4,128)S(1)}, s32[3,1]{1,0:T(4,128)S(1)}, u32[]{:S(2)}, u32[]{:S(2)}) collective-permute-start(s32[3,1]{1,0:T(4,128)S(1)} %copy.16.count_ref), channel_id=1, source_target_pairs={{0,2},{2,0},{1,3},{3,1},{4,6},{6,4},{5,7},{7,5},{8,10},{10,8},{9,1... | collective-permute-start | bytes 44 | tf_op jit(solution)/shard_map/ppermute | solution.py:568
  3.4 1.2 %collective-permute-start = (s32[3,1]{1,0:T(4,128)S(1)}, s32[3,1]{1,0:T(4,128)S(1)}, u32[]{:S(2)}, u32[]{:S(2)}) collective-permute-start(s32[3,1]{1,0:T(4,128)S(1)} %copy.16.count_ref), channel_id=1, source_target_pairs={{0,1},{1,0},{2,3},{3,2},{4,5},{5,4},{6,7},{7,6},{8,9},{9,8},{10,11... | collective-permute-start | bytes 44 | tf_op jit(solution)/shard_map/ppermute | solution.py:561
  4.7 1.6 %collective-permute-start.3 = (bf16[192,512]{1,0:T(8,128)(2,1)}, bf16[192,512]{1,0:T(8,128)(2,1)S(1)}, u32[]{:S(2)}, u32[]{:S(2)}) collective-permute-start(bf16[192,512]{1,0:T(8,128)(2,1)} %bitcast.8), channel_id=1, source_target_pairs={{0,2},{2,0},{1,3},{3,1},{4,6},{6,4},{5,7},{7,5},{8,10},{10,8},{9,1... | collective-permute-start | bytes 589832 | tf_op jit(solution)/shard_map/ppermute | solution.py:567
  6.4 1.0 %copy-done = bf16[3,64,512]{2,1,0:T(8,128)(2,1)S(1)} copy-done((bf16[3,64,512]{2,1,0:T(8,128)(2,1)S(1)}, bf16[3,64,512]{2,1,0:T(8,128)(2,1)}, u32[]{:S(2)}) %copy-start) | copy-done | bytes 196632
  7.3 1.4 %copy-done.2 = bf16[512,1536]{1,0:T(8,128)(2,1)S(1)} copy-done((bf16[512,1536]{1,0:T(8,128)(2,1)S(1)}, bf16[512,1536]{1,0:T(8,128)(2,1)}, u32[]{:S(2)}) %copy-start.2) | copy-done | bytes 1572888
  8.7 0.9 %near.1 = (bf16[192,512]{1,0:T(8,128)(2,1)S(1)}, bf16[192,512]{1,0:T(8,128)(2,1)S(1)}, bf16[192,512]{1,0:T(8,128)(2,1)S(1)}, bf16[192,512]{1,0:T(8,128)(2,1)S(1)...) custom-call(bf16[192,512]{1,0:T(8,128)(2,1)S(1)} %bitcast.9, bf16[512,1536]{1,0:T(8,128)(2,1)S(1)} %copy-done.2), custom_call_target="tpu_custom_call" | custom-call | flops 2500000000 | bytes 4000000 | tf_op jit(solution)/shard_map/near/pallas_call | solution.py:429
  9.7 0.9 %collective-permute-start.2 = (s32[3,1]{1,0:T(4,128)S(1)}, s32[3,1]{1,0:T(4,128)S(1)}, u32[]{:S(2)}, u32[]{:S(2)}) collective-permute-start(s32[3,1]{1,0:T(4,128)S(1)} %collective-permute-done.1.count2_ref), channel_id=1, source_target_pairs={{0,1},{1,0},{2,3},{3,2},{4,5},{5,4},{6,7},{7,6},{8,9},{9,8},{10,11... | collective-permute-start | bytes 44 | tf_op jit(solution)/shard_map/ppermute | solution.py:561
  10.6 0.8 collective-permute-done.3.tok2_ref
  11.4 1.0 %collective-permute-start.4 = (bf16[192,512]{1,0:T(8,128)(2,1)S(1)}, bf16[192,512]{1,0:T(8,128)(2,1)S(1)}, u32[]{:S(2)}, u32[]{:S(2)}) collective-permute-start(bf16[192,512]{1,0:T(8,128)(2,1)S(1)} %collective-permute-done.3.tok2_ref), channel_id=1, source_target_pairs={{0,1},{1,0},{2,3},{3,2},{4,5},{5,4},{6,7},{7,6},{8,9},{9,8},{10,11... | collective-permute-start | bytes 589832 | tf_op jit(solution)/shard_map/ppermute | solution.py:561
  12.5 1.5 %mate.1 = (bf16[192,512]{1,0:T(8,128)(2,1)S(1)}, bf16[192,512]{1,0:T(8,128)(2,1)S(1)}, bf16[192,512]{1,0:T(8,128)(2,1)S(1)}, bf16[192,512]{1,0:T(8,128)(2,1)S(1)}, bf16[192,1024]{1,0:T(8,128)(2,1)S(1)}) custom-call(s32[3,1]{1,0:T(4,128)S(1)} %copy.16.count_ref, bf16[192,512]{1,0:T(8,128)(2,1)S(1)} %collective-permute-done.5.tok1_ref, ...), custom_call_target="tpu_custom_call" | custom-call | flops 5000000000 | bytes 2000000 | tf_op jit(solution)/shard_map/mate/pallas_call | solution.py:442
  14.0 5.3 %front.1 = (bf16[192,512]{1,0:T(8,128)(2,1)}, bf16[16,64,640]{2,1,0:T(8,128)(2,1)S(1)}, bf16[16,64,640]{2,1,0:T(8,128)(2,1)S(1)}, f32[192,512]{1,0:T(8,128)S(1)}...) custom-call(s32[1]{0:T(128)} %bitcast.core_ref, ...), custom_call_target="tpu_custom_call" | custom-call | flops 5000000000 | bytes 12000000 | tf_op jit(solution)/shard_map/front/pallas_call | solution.py:466
  19.7 4.2 %back.1 = (bf16[16,64,384]{2,1,0:T(8,128)(2,1)S(1)}, bf16[16,64,384]{2,1,0:T(8,128)(2,1)S(1)}, bf16[4,192,128]{2,1,0:T(8,128)(2,1)S(1)}, bf16[4,768,128]{2,1,0:T(8,128)(2,1)S(1)}, bf16[4,768,128]{2,1,0:T(8,128)(2,1)S(1)}) custom-call(s32[1]{0:T(128)} %bitcast.core_ref, bf16[192,512]{1,0:T(8,128)(2,1)S(1)} %get-tuple-element.42.query_ref, ...), custom_call_target="tpu_custom_call" | custom-call | flops 6000000000 | bytes 12000000 | tf_op jit(solution)/shard_map/back/pallas_call | solution.py:491
  23.8 0.6 collective-permute-start.7
  24.4 1.4 %push.1 = (bf16[2,192,512]{2,1,0:T(8,128)(2,1)S(1)}, bf16[192,512]{1,0:T(8,128)(2,1)S(1)}, f32[192,512]{1,0:T(8,128)S(1)}) custom-call(bf16[512,1536]{1,0:T(8,128)(2,1)S(1)} %copy-done.3, bf16[4,192,128]{2,1,0:T(8,128)(2,1)S(1)} %get-tuple-element.60.gq_ref, bf16[4,768,128]{2,1,0:T(8,128)(2,1)S(1)} %get-tuple-element.61.gk_ref, ...), custom_call_target="tpu_custom_call" | custom-call | flops 2000000000 | bytes 4000000 | tf_op jit(solution)/shard_map/push/pallas_call | solution.py:504
  25.9 1.7 %collective-permute-done.8.after_ref.recv_core_ref = bf16[2,192,512]{2,1,0:T(8,128)(2,1)S(1)} collective-permute-done((bf16[2,192,512]{2,1,0:T(8,128)(2,1)S(1)}, bf16[2,192,512]{2,1,0:T(8,128)(2,1)S(1)}, u32[]{:S(2)}, u32[]{:S(2)}) %collective-permute-start.8) | collective-permute-done | bytes 393248 | tf_op jit(solution)/shard_map/ppermute | solution.py:561
  28.1 33.6 %all_to_all.10.parts_ref = bf16[16,64,1024]{2,1,0:T(8,128)(2,1)S(1)} all-to-all(bf16[16,64,1024]{2,1,0:T(8,128)(2,1)S(1)} %join.1), channel_id=1, replica_groups={{0,2,4,6,8,10,12,14,16,18,20,22,24,26,28,30},{1,3,5,7,9,11,13,15,17,19,..., dimensions={0} | all-to-all | bytes 4194304 | tf_op jit(solution)/shard_map/all_to_all | solution.py:596
  61.7 0.9 %plane_sum.1 = bf16[64,1024]{1,0:T(8,128)(2,1)} custom-call(bf16[16,64,1024]{2,1,0:T(8,128)(2,1)S(1)} %all_to_all.10.parts_ref), custom_call_target="tpu_custom_call" | custom-call | flops 1000000 | bytes 4000000 | tf_op jit(solution)/shard_map/plane_sum/pallas_call | solution.py:516
  62.7 8.2 %all-to-all-start.1 = ((bf16[8,8,1024]{2,1,0:T(8,128)(2,1)}), bf16[8,8,1024]{2,1,0:T(8,128)(2,1)S(1)}, u32[]{:S(2)}, u32[]{:S(2)}) async-start(bf16[8,8,1024]{2,1,0:T(8,128)(2,1)} %bitcast.6), calls=%async_computation.1 | async-start | bytes 262144 | tf_op jit(solution)/shard_map/all_to_all | solution.py:600
  71.3 7.5 %all-to-all-done.1 = bf16[8,8,1024]{2,1,0:T(8,128)(2,1)S(1)} async-done(((bf16[8,8,1024]{2,1,0:T(8,128)(2,1)}), bf16[8,8,1024]{2,1,0:T(8,128)(2,1)S(1)}, u32[]{:S(2)}, u32[]{:S(2)}) %all-to-all-start.1) | async-done | bytes 131104 | tf_op jit(solution)/shard_map/all_to_all | solution.py:600
  78.8 3.3 %collective-permute-start.12 = (bf16[8,1024]{1,0:T(8,128)(2,1)S(1)}, bf16[8,1024]{1,0:T(8,128)(2,1)S(1)}, u32[]{:S(2)}, u32[]{:S(2)}) collective-permute-start(bf16[8,1024]{1,0:T(8,128)(2,1)S(1)} %reduce_sum.12.own_ref), channel_id=1, source_target_pairs={{0,3},{3,0},{1,2},{2,1},{4,7},{7,4},{5,6},{6,5},{8,11},{11,8},{9,1... | collective-permute-start | bytes 49160 | tf_op jit(solution)/shard_map/ppermute | solution.py:602
  82.1 1.2 %collective-permute-start.11 = (bf16[8,1024]{1,0:T(8,128)(2,1)S(1)}, bf16[8,1024]{1,0:T(8,128)(2,1)S(1)}, u32[]{:S(2)}, u32[]{:S(2)}) collective-permute-start(bf16[8,1024]{1,0:T(8,128)(2,1)S(1)} %reduce_sum.12.own_ref), channel_id=1, source_target_pairs={{0,2},{2,0},{1,3},{3,1},{4,6},{6,4},{5,7},{7,5},{8,10},{10,8},{9,1... | collective-permute-start | bytes 49160 | tf_op jit(solution)/shard_map/ppermute | solution.py:602
  83.3 1.0 %finish.1 = bf16[192,512]{1,0:T(8,128)(2,1)} custom-call(bf16[192,512]{1,0:T(8,128)(2,1)S(1)} %bitcast.11, f32[192,512]{1,0:T(8,128)S(1)} %get-tuple-element.63.own_ref, bf16[2,192,512]{2,1,0:T(8,128)(2,1)S(1)} %collective-permute-done.8.after_ref.recv_core_ref, bf16[192,512]{1,0:T(8,128)(2,1)S(1)} %collective-permute-done.9.from_x_ref, ...), custom_call_target="tpu_custom_call" | custom-call | flops 1000000 | bytes 4000000 | tf_op jit(solution)/shard_map/finish/pallas_call | solution.py:516
  84.7 0.7 final.1
  (33 shorter events, 1.9 us)
Async XLA Ops:
  1.4 8.3 %collective-permute-start.1 = (s32[3,1]{1,0:T(4,128)S(1)}, s32[3,1]{1,0:T(4,128)S(1)}, u32[]{:S(2)}, u32[]{:S(2)}) collective-permute-start(s32[3,1]{1,0:T(4,128)S(1)} %copy.16.count_ref), channel_id=1, source_target_pairs={{0,2},{2,0},{1,3},{3,1},{4,6},{6,4},{5,7},{7,5},{8,10},{10,8},{9,1... | collective-permute-start | bytes 44 | tf_op jit(solution)/shard_map/ppermute | solution.py:568
  3.4 10.6 %collective-permute-start = (s32[3,1]{1,0:T(4,128)S(1)}, s32[3,1]{1,0:T(4,128)S(1)}, u32[]{:S(2)}, u32[]{:S(2)}) collective-permute-start(s32[3,1]{1,0:T(4,128)S(1)} %copy.16.count_ref), channel_id=1, source_target_pairs={{0,1},{1,0},{2,3},{3,2},{4,5},{5,4},{6,7},{7,6},{8,9},{9,8},{10,11... | collective-permute-start | bytes 44 | tf_op jit(solution)/shard_map/ppermute | solution.py:561
  4.6 7.8 %collective-permute-start.5 = (bf16[192,512]{1,0:T(8,128)(2,1)}, bf16[192,512]{1,0:T(8,128)(2,1)S(1)}, u32[]{:S(2)}, u32[]{:S(2)}) collective-permute-start(bf16[192,512]{1,0:T(8,128)(2,1)} %bitcast.7), channel_id=1, source_target_pairs={{0,1},{1,0},{2,3},{3,2},{4,5},{5,4},{6,7},{7,6},{8,9},{9,8},{10,11... | collective-permute-start | bytes 589832 | tf_op jit(solution)/shard_map/ppermute | solution.py:561
  4.7 6.7 %collective-permute-start.3 = (bf16[192,512]{1,0:T(8,128)(2,1)}, bf16[192,512]{1,0:T(8,128)(2,1)S(1)}, u32[]{:S(2)}, u32[]{:S(2)}) collective-permute-start(bf16[192,512]{1,0:T(8,128)(2,1)} %bitcast.8), channel_id=1, source_target_pairs={{0,2},{2,0},{1,3},{3,1},{4,6},{6,4},{5,7},{7,5},{8,10},{10,8},{9,1... | collective-permute-start | bytes 589832 | tf_op jit(solution)/shard_map/ppermute | solution.py:567
  6.4 1.0 %copy-start = (bf16[3,64,512]{2,1,0:T(8,128)(2,1)S(1)}, bf16[3,64,512]{2,1,0:T(8,128)(2,1)}, u32[]{:S(2)}) copy-start(bf16[3,64,512]{2,1,0:T(8,128)(2,1)} %param.7) | copy-start | bytes 589828
  7.3 1.4 %copy-start.2 = (bf16[512,1536]{1,0:T(8,128)(2,1)S(1)}, bf16[512,1536]{1,0:T(8,128)(2,1)}, u32[]{:S(2)}) copy-start(bf16[512,1536]{1,0:T(8,128)(2,1)} %w_qkv_ref.7) | copy-start | bytes 4718596
  8.7 3.7 %copy-start.3 = (bf16[512,1536]{1,0:T(8,128)(2,1)S(1)}, bf16[512,1536]{1,0:T(8,128)(2,1)}, u32[]{:S(2)}) copy-start(bf16[512,1536]{1,0:T(8,128)(2,1)} %w_qkv_ref.7) | copy-start | bytes 4718596
  8.7 3.7 %copy-start.5 = (bf16[1024,512]{1,0:T(8,128)(2,1)S(1)}, bf16[1024,512]{1,0:T(8,128)(2,1)}, u32[]{:S(2)}) copy-start(bf16[1024,512]{1,0:T(8,128)(2,1)} %w_down_ref.3) | copy-start | bytes 3145732
  8.7 3.7 %copy-start.7 = (bf16[3,64,512]{2,1,0:T(8,128)(2,1)S(1)}, bf16[3,64,512]{2,1,0:T(8,128)(2,1)}, u32[]{:S(2)}) copy-start(bf16[3,64,512]{2,1,0:T(8,128)(2,1)} %param.13) | copy-start | bytes 589828
  9.7 4.3 %collective-permute-start.2 = (s32[3,1]{1,0:T(4,128)S(1)}, s32[3,1]{1,0:T(4,128)S(1)}, u32[]{:S(2)}, u32[]{:S(2)}) collective-permute-start(s32[3,1]{1,0:T(4,128)S(1)} %collective-permute-done.1.count2_ref), channel_id=1, source_target_pairs={{0,1},{1,0},{2,3},{3,2},{4,5},{5,4},{6,7},{7,6},{8,9},{9,8},{10,11... | collective-permute-start | bytes 44 | tf_op jit(solution)/shard_map/ppermute | solution.py:561
  11.4 2.6 %collective-permute-start.4 = (bf16[192,512]{1,0:T(8,128)(2,1)S(1)}, bf16[192,512]{1,0:T(8,128)(2,1)S(1)}, u32[]{:S(2)}, u32[]{:S(2)}) collective-permute-start(bf16[192,512]{1,0:T(8,128)(2,1)S(1)} %collective-permute-done.3.tok2_ref), channel_id=1, source_target_pairs={{0,1},{1,0},{2,3},{3,2},{4,5},{5,4},{6,7},{7,6},{8,9},{9,8},{10,11... | collective-permute-start | bytes 589832 | tf_op jit(solution)/shard_map/ppermute | solution.py:561
  12.5 1.6 %copy-start.1 = (bf16[3,64,512]{2,1,0:T(8,128)(2,1)S(1)}, bf16[3,64,512]{2,1,0:T(8,128)(2,1)}, u32[]{:S(2)}) copy-start(bf16[3,64,512]{2,1,0:T(8,128)(2,1)} %param.7) | copy-start | bytes 589828
  12.5 1.6 %copy-start.4 = (bf16[512,1024]{1,0:T(8,128)(2,1)S(1)}, bf16[512,1024]{1,0:T(8,128)(2,1)}, u32[]{:S(2)}) copy-start(bf16[512,1024]{1,0:T(8,128)(2,1)} %w_up_ref.1) | copy-start | bytes 3145732
  12.5 1.6 %copy-start.6 = (bf16[512,512]{1,0:T(8,128)(2,1)S(1)}, bf16[512,512]{1,0:T(8,128)(2,1)}, u32[]{:S(2)}) copy-start(bf16[512,512]{1,0:T(8,128)(2,1)} %w_out_ref.1) | copy-start | bytes 1572868
  19.4 8.3 %collective-permute-start.6 = (bf16[16,64,640]{2,1,0:T(8,128)(2,1)S(1)}, bf16[16,64,640]{2,1,0:T(8,128)(2,1)S(1)}, u32[]{:S(2)}, u32[]{:S(2)}) collective-permute-start(bf16[16,64,640]{2,1,0:T(8,128)(2,1)S(1)} %get-tuple-element.65), channel_id=1, source_target_pairs={{0,1},{1,0},{2,3},{3,2},{4,5},{5,4},{6,7},{7,6},{8,9},{9,8},{10,11... | collective-permute-start | bytes 3932168 | tf_op jit(solution)/shard_map/ppermute | solution.py:561
  23.8 3.8 %collective-permute-start.7 = (bf16[16,64,384]{2,1,0:T(8,128)(2,1)S(1)}, bf16[16,64,384]{2,1,0:T(8,128)(2,1)S(1)}, u32[]{:S(2)}, u32[]{:S(2)}) collective-permute-start(bf16[16,64,384]{2,1,0:T(8,128)(2,1)S(1)} %get-tuple-element.67), channel_id=1, source_target_pairs={{0,1},{1,0},{2,3},{3,2},{4,5},{5,4},{6,7},{7,6},{8,9},{9,8},{10,11... | collective-permute-start | bytes 2359304 | tf_op jit(solution)/shard_map/ppermute | solution.py:561
  25.8 1.8 %collective-permute-start.8 = (bf16[2,192,512]{2,1,0:T(8,128)(2,1)S(1)}, bf16[2,192,512]{2,1,0:T(8,128)(2,1)S(1)}, u32[]{:S(2)}, u32[]{:S(2)}) collective-permute-start(bf16[2,192,512]{2,1,0:T(8,128)(2,1)S(1)} %get-tuple-element.68), channel_id=1, source_target_pairs={{0,1},{1,0},{2,3},{3,2},{4,5},{5,4},{6,7},{7,6},{8,9},{9,8},{10,11... | collective-permute-start | bytes 1179656 | tf_op jit(solution)/shard_map/ppermute | solution.py:561
  62.7 16.1 %all-to-all-start.1 = ((bf16[8,8,1024]{2,1,0:T(8,128)(2,1)}), bf16[8,8,1024]{2,1,0:T(8,128)(2,1)S(1)}, u32[]{:S(2)}, u32[]{:S(2)}) async-start(bf16[8,8,1024]{2,1,0:T(8,128)(2,1)} %bitcast.6), calls=%async_computation.1 | async-start | bytes 262144 | tf_op jit(solution)/shard_map/all_to_all | solution.py:600
  70.9 12.3 %collective-permute-start.9 = (bf16[192,512]{1,0:T(8,128)(2,1)S(1)}, bf16[192,512]{1,0:T(8,128)(2,1)S(1)}, u32[]{:S(2)}, u32[]{:S(2)}) collective-permute-start(bf16[192,512]{1,0:T(8,128)(2,1)S(1)} %add_x.1), channel_id=1, source_target_pairs={{0,2},{2,0},{1,3},{3,1},{4,6},{6,4},{5,7},{7,5},{8,10},{10,8},{9,1... | collective-permute-start | bytes 589832 | tf_op jit(solution)/shard_map/ppermute | solution.py:598
  78.8 5.4 %collective-permute-start.12 = (bf16[8,1024]{1,0:T(8,128)(2,1)S(1)}, bf16[8,1024]{1,0:T(8,128)(2,1)S(1)}, u32[]{:S(2)}, u32[]{:S(2)}) collective-permute-start(bf16[8,1024]{1,0:T(8,128)(2,1)S(1)} %reduce_sum.12.own_ref), channel_id=1, source_target_pairs={{0,3},{3,0},{1,2},{2,1},{4,7},{7,4},{5,6},{6,5},{8,11},{11,8},{9,1... | collective-permute-start | bytes 49160 | tf_op jit(solution)/shard_map/ppermute | solution.py:602
  82.1 2.6 %collective-permute-start.11 = (bf16[8,1024]{1,0:T(8,128)(2,1)S(1)}, bf16[8,1024]{1,0:T(8,128)(2,1)S(1)}, u32[]{:S(2)}, u32[]{:S(2)}) collective-permute-start(bf16[8,1024]{1,0:T(8,128)(2,1)S(1)} %reduce_sum.12.own_ref), channel_id=1, source_target_pairs={{0,2},{2,0},{1,3},{3,1},{4,6},{6,4},{5,7},{7,5},{8,10},{10,8},{9,1... | collective-permute-start | bytes 49160 | tf_op jit(solution)/shard_map/ppermute | solution.py:602
  83.3 1.4 %collective-permute-start.10 = (bf16[8,1024]{1,0:T(8,128)(2,1)S(1)}, bf16[8,1024]{1,0:T(8,128)(2,1)S(1)}, u32[]{:S(2)}, u32[]{:S(2)}) collective-permute-start(bf16[8,1024]{1,0:T(8,128)(2,1)S(1)} %reduce_sum.12.own_ref), channel_id=1, source_target_pairs={{0,1},{1,0},{2,3},{3,2},{4,5},{5,4},{6,7},{7,6},{8,9},{9,8},{10,11... | collective-permute-start | bytes 49160 | tf_op jit(solution)/shard_map/ppermute | solution.py:602

commit v4 on v3

v4 whole, which is shorter than its diff:
```python
import math

import jax
import jax.numpy as jnp
from jax import lax
from jax.experimental import pallas as pl
from jax.experimental.pallas import tpu as pltpu
from jax.sharding import PartitionSpec as P

F32 = jnp.float32
BF16 = jnp.bfloat16
HEAD_DIM = 64
SOFTMAX_SCALE = 8.0
WIDTH = 512
HIDDEN = 1024
ROWS_DEV = 3
SECTOR = 64
TOKENS = ROWS_DEV * SECTOR
KEYS = 4 * SECTOR
GROUP = 256
GELU_A = math.sqrt(2.0 / math.pi)
GELU_B = 0.044715
NEAR_MB = 20
FRONT_MB = 28
BACK_MB = 28


def lat_index(z, y, x_hi):
    return (z * 4 + y) * 2 + x_hi


CORE = [(0, 1), (1, 0), (2, 3), (3, 2)]
X_LO = [(0, 2), (2, 0), (1, 3), (3, 1)]
DIAGONAL = [(0, 3), (3, 0), (1, 2), (2, 1)]
Z_ORDER = (0, 7, 1, 6, 2, 5, 3, 4)
Z_GROUPS = [[lat_index(z, y, x) for z in Z_ORDER] for y in range(4) for x in range(2)]
PLANE_GROUPS = [
    [
        lat_index(z, y, x_hi) * 4 + x_lo * 2 + core
        for y in reversed(range(4))
        for x_hi in reversed(range(2))
        for x_lo in reversed(range(2))
    ]
    for z in range(8)
    for core in range(2)
]


def mm(left, right):
    return lax.dot_general(left, right, (((1,), (0,)), ((), ())), preferred_element_type=F32)


def mm_nt(left, right):
    return lax.dot_general(left, right, (((1,), (1,)), ((), ())), preferred_element_type=F32)


def mm_tn(left, right):
    return lax.dot_general(left, right, (((0,), (0,)), ((), ())), preferred_element_type=F32)


def mean_last(values):
    return jnp.sum(values, axis=-1, keepdims=True) * (1.0 / values.shape[-1])


def layer_norm(values):
    centered = values - mean_last(values)
    inverse = lax.rsqrt(mean_last(centered * centered) + 1e-05)
    return centered * inverse, inverse


def layer_norm_back(normed, inverse, grad):
    return inverse * (grad - mean_last(grad) - normed * mean_last(grad * normed))


def head_blocks():
    same = lax.broadcasted_iota(jnp.int32, (GROUP, GROUP), 0) // HEAD_DIM == (
        lax.broadcasted_iota(jnp.int32, (GROUP, GROUP), 1) // HEAD_DIM
    )
    return jnp.where(same, 1.0, 0.0).astype(BF16)


def head_mean(values, blocks):
    parts = [
        mm(values[:, at : at + GROUP].astype(BF16), blocks) for at in range(0, values.shape[1], GROUP)
    ]
    return (parts[0] if len(parts) == 1 else jnp.concatenate(parts, axis=1)) * (1.0 / HEAD_DIM)


def head_masks(dtype):
    lane = lax.broadcasted_iota(jnp.int32, (1, GROUP), 1) // HEAD_DIM
    return [jnp.where(lane == head, 1.0, 0.0).astype(dtype) for head in range(4)]


def stack_heads(values, masks):
    return jnp.concatenate([values * mask for mask in masks], axis=0)


def unstack_heads(values, masks):
    return sum(values[head * SECTOR : (head + 1) * SECTOR] * masks[head] for head in range(4))


def store_pieces(out_ref, x_lo, column, product):
    width = product.shape[1]
    split = product.reshape(8, 8, 8, width)
    for place in range(8):
        piece = jnp.concatenate([split[z, place] for z in Z_ORDER], axis=0)
        out_ref[15 - place * 2 - x_lo, :, column : column + width] = piece.astype(BF16)


def rows_of(row, width=SECTOR):
    return slice(row * width, (row + 1) * width)


def key_value(tok_refs, w_qkv_ref, blocks, *out_refs):
    tokens = jnp.concatenate([ref[...] for ref in tok_refs], axis=0).astype(F32)
    normed = layer_norm(tokens)[0].astype(BF16)
    key_raw = mm(normed, w_qkv_ref[:, WIDTH : 2 * WIDTH])
    value = mm(normed, w_qkv_ref[:, 2 * WIDTH :]).astype(BF16)
    inv_k = lax.rsqrt(head_mean(key_raw * key_raw, blocks) + 1e-06)
    made = (normed, (key_raw * inv_k).astype(BF16), value, inv_k.astype(BF16))
    for at, ref in enumerate(out_refs):
        first = at // 4 * TOKENS
        ref[...] = made[at % 4][first : first + TOKENS]
    return normed


def own_mask(count_ref):
    place = lax.broadcasted_iota(jnp.int32, (SECTOR, 1), 0)
    return jnp.concatenate(
        [jnp.where(place < count_ref[0, row], 1.0, 0.0) for row in range(ROWS_DEV)], axis=0
    )


def near_kernel(tok0_ref, w_qkv_ref, query_ref, inv_q_ref, *own_refs):
    blocks = head_blocks()
    normed = key_value([tok0_ref], w_qkv_ref, blocks, *own_refs)
    query_raw = mm(normed, w_qkv_ref[:, :WIDTH])
    inv_q = lax.rsqrt(head_mean(query_raw * query_raw, blocks) + 1e-06)
    inv_q_ref[...] = inv_q.astype(BF16)
    query_ref[...] = (query_raw * inv_q).astype(BF16)


def pair_kernel(count_ref, tok1_ref, tok2_ref, w_qkv_ref, w_down_ref, cot_ref, grad_active_ref, *refs):
    blocks = head_blocks()
    branch = (own_mask(count_ref) * cot_ref[...].astype(F32)).astype(BF16)
    grad_active_ref[...] = mm_nt(branch, w_down_ref[...]).astype(BF16)
    key_value([tok1_ref, tok2_ref], w_qkv_ref, blocks, *refs)


PLACES = [(row, slice(low, low + GROUP)) for row in range(ROWS_DEV) for low in (0, GROUP)]


def row_join(row, lanes, refs):
    return jnp.concatenate([ref[rows_of(row), lanes] for ref in refs], axis=0)


def front_kernel(
    core_ref,
    count_ref,
    count1_ref,
    count2_ref,
    count3_ref,
    tok0_ref,
    tok3_ref,
    w_qkv_ref,
    w_out_ref,
    w_up_ref,
    w_down_ref,
    cot_ref,
    query_ref,
    own_key_ref,
    own_value_ref,
    mate_key_ref,
    mate_value_ref,
    across_key_ref,
    across_value_ref,
    grad_active_ref,
    block_out_ref,
    keep_ref,
    send_ref,
    grad_middle_ref,
    normed_ref,
    key_ref,
    value_ref,
    inv_k_ref,
    probs_ref,
    grad_att_ref,
    att_ref,
    lift_ref,
    attn_ref,
    branch_ref,
):
    blocks = head_blocks()
    masks_b = head_masks(BF16)
    masks_f = head_masks(F32)
    core = core_ref[0]
    key_value([tok3_ref], w_qkv_ref, blocks, normed_ref, key_ref, value_ref, inv_k_ref)
    key_refs = (own_key_ref, mate_key_ref, across_key_ref, key_ref)
    value_refs = (own_value_ref, mate_value_ref, across_value_ref, value_ref)

    key_place = lax.broadcasted_iota(jnp.int32, (1, KEYS), 1)
    key_masks = []
    for row in range(ROWS_DEV):
        limit = jnp.zeros((1, KEYS), jnp.int32)
        for sector, ref in enumerate((count_ref, count1_ref, count2_ref, count3_ref)):
            limit = jnp.where(key_place // SECTOR == sector, ref[0, row], limit)
        key_masks.append(jnp.where(key_place % SECTOR < limit, 1.0, 0.0))
    scores = [
        mm_nt(stack_heads(query_ref[rows_of(row), lanes], masks_b), row_join(row, lanes, key_refs))
        for row, lanes in PLACES
    ]
    for at, (row, lanes) in enumerate(PLACES):
        expscore = jnp.exp(scores[at] * (SOFTMAX_SCALE / HEAD_DIM) - SOFTMAX_SCALE) * key_masks[row]
        total = jnp.sum(expscore, axis=1, keepdims=True)
        probs_ref[at] = (expscore * (1.0 / total)).astype(BF16)
    mixed = [mm(probs_ref[at], row_join(row, lanes, value_refs)) for at, (row, lanes) in enumerate(PLACES)]
    for at, (row, lanes) in enumerate(PLACES):
        att_ref[rows_of(row), lanes] = unstack_heads(mixed[at], masks_f).astype(BF16)

    mask = own_mask(count_ref)
    attended = att_ref[...]
    middle = tok0_ref[...].astype(F32) + mask * mm(attended, w_out_ref[...])
    normed_two, inverse = layer_norm(middle)
    normed_two_b = normed_two.astype(BF16)
    lifted = mm(normed_two_b, w_up_ref[...])
    square = lifted * lifted
    bent = jnp.tanh(GELU_A * lifted * (1.0 + GELU_B * square))
    half = 0.5 * (1.0 + bent)
    active = (lifted * half).astype(BF16)
    slope = half + 0.5 * lifted * (1.0 - bent * bent) * (GELU_A * (1.0 + 3.0 * GELU_B * square))
    branch = (mask * cot_ref[...].astype(F32)).astype(BF16)
    grad_lifted = (slope * grad_active_ref[...].astype(F32)).astype(BF16)
    grad_normed = mm_nt(grad_lifted, w_up_ref[...])
    for part in range(2):
        branch_ref[part] = branch[:, part * 256 : (part + 1) * 256]
    for part in range(4):
        lift_ref[part] = grad_lifted[:, part * 256 : (part + 1) * 256]
    halves = ((keep_ref, core), (send_ref, 1 - core))
    active_t, normed_two_t = active.T, normed_two_b.T
    for out_ref, half_index in halves:
        term_down = mm(active_t, branch_ref[half_index]).reshape(64, 2, 8, 256)
        for x_lo in range(2):
            store_pieces(out_ref, x_lo, 384, term_down[:, x_lo].reshape(512, 256))
    grad_middle = cot_ref[...].astype(F32) + layer_norm_back(normed_two, inverse, grad_normed)
    grad_middle_ref[...] = grad_middle
    grad_attn = (mask * grad_middle).astype(BF16)
    grad_att_ref[...] = mm_nt(grad_attn, w_out_ref[...]).astype(BF16)
    block_out_ref[...] = (middle + mask * mm(active, w_down_ref[...])).astype(BF16)
    for out_ref, half_index in halves:
        for x_lo in range(2):
            store_pieces(out_ref, x_lo, 128, mm(normed_two_t, lift_ref[half_index + 2 * x_lo]))
    for part in range(4):
        attn_ref[part] = grad_attn[:, part * 128 : (part + 1) * 128]
    attended_t = attended.T
    for out_ref, half_index in halves:
        pair = jnp.concatenate([attn_ref[half_index], attn_ref[half_index + 2]], axis=1)
        term_out = mm(attended_t, pair)
        for x_lo in range(2):
            store_pieces(out_ref, x_lo, 0, term_out[:, x_lo * 128 : (x_lo + 1) * 128])


def norm_back(normed_b, inverse_b, grad, blocks):
    normed = normed_b.astype(F32)
    shift = head_mean(normed * grad, blocks)
    return (inverse_b.astype(F32) * (grad - normed * shift)).astype(BF16)


def back_kernel(core_ref, query_ref, inv_q_ref, *refs):
    sectors, (probs_ref, grad_att_ref, keep_ref, send_ref, gq_ref, gk_ref, gv_ref) = refs[:16], refs[16:]
    normed_refs, key_refs, value_refs, inv_k_refs = (sectors[at::4] for at in range(4))
    blocks = head_blocks()
    masks_b = head_masks(BF16)
    masks_f = head_masks(F32)
    core = core_ref[0]
    stacked_q = [stack_heads(query_ref[rows_of(row), lanes], masks_b) for row, lanes in PLACES]
    stacked_g = [stack_heads(grad_att_ref[rows_of(row), lanes], masks_b) for row, lanes in PLACES]
    keys = [row_join(row, lanes, key_refs) for row, lanes in PLACES]
    grad_probs = [
        mm_nt(stacked_g[at], row_join(row, lanes, value_refs)) for at, (row, lanes) in enumerate(PLACES)
    ]
    grad_scores = []
    for at in range(len(PLACES)):
        probs = probs_ref[at].astype(F32)
        delta = jnp.sum(probs * grad_probs[at], axis=1, keepdims=True)
        grad_scores.append((probs * (grad_probs[at] - delta) * (SOFTMAX_SCALE / HEAD_DIM)).astype(BF16))
    grad_v = [mm_tn(probs_ref[at], stacked_g[at]).astype(BF16) for at in range(len(PLACES))]
    grad_k = [mm_tn(grad_scores[at], stacked_q[at]) for at in range(len(PLACES))]
    grad_q = [unstack_heads(mm(grad_scores[at], keys[at]), masks_f) for at in range(len(PLACES))]
    for at, (row, lanes) in enumerate(PLACES):
        own = rows_of(row)
        back_q = norm_back(query_ref[own, lanes], inv_q_ref[own, lanes], grad_q[at], blocks)
        back_k = norm_back(keys[at], row_join(row, lanes, inv_k_refs), grad_k[at], blocks)
        for part in range(2):
            cut = slice(part * 128, (part + 1) * 128)
            quarter = lanes.start // 128 + part
            gq_ref[quarter, own, :] = back_q[:, cut]
            for ref, grad in ((gk_ref, back_k), (gv_ref, grad_v[at])):
                for sector in range(4):
                    rows = slice(sector * TOKENS + own.start, sector * TOKENS + own.stop)
                    ref[quarter, rows, :] = grad[sector * SECTOR : (sector + 1) * SECTOR, cut]

    normed_all = jnp.concatenate([ref[...] for ref in normed_refs], axis=0)
    own_normed_t, normed_all_t = normed_refs[0][...].T, normed_all.T
    for out_ref, half_index in ((keep_ref, core), (send_ref, 1 - core)):
        pair = jnp.concatenate([gq_ref[half_index], gq_ref[half_index + 2]], axis=1)
        term_q = mm(own_normed_t, pair)
        for x_lo in range(2):
            store_pieces(out_ref, x_lo, 0, term_q[:, x_lo * 128 : (x_lo + 1) * 128])
            pair = jnp.concatenate([gk_ref[half_index + 2 * x_lo], gv_ref[half_index + 2 * x_lo]], axis=1)
            store_pieces(out_ref, x_lo, 128, mm(normed_all_t, pair))


def push_kernel(w_qkv_ref, gq_ref, gk_ref, gv_ref, for_core_ref, for_x_ref, own_ref):
    grad_q = jnp.concatenate([gq_ref[part] for part in range(4)], axis=1)
    grad_kv = jnp.concatenate([ref[part] for ref in (gk_ref, gv_ref) for part in range(4)], axis=1)
    grad_normed = mm_nt(grad_kv, w_qkv_ref[:, WIDTH:])
    for_core_ref[0] = grad_normed[TOKENS : 2 * TOKENS].astype(BF16)
    for_x_ref[...] = grad_normed[2 * TOKENS : 3 * TOKENS].astype(BF16)
    for_core_ref[1] = grad_normed[3 * TOKENS :].astype(BF16)
    own_ref[...] = grad_normed[:TOKENS] + mm_nt(grad_q, w_qkv_ref[:, :WIDTH])


def join_kernel(keep1_ref, recv1_ref, keep2_ref, recv2_ref, after_ref, out_ref):
    del after_ref
    for piece in range(16):
        out_ref[piece, :, :384] = (keep2_ref[piece].astype(F32) + recv2_ref[piece].astype(F32)).astype(BF16)
        out_ref[piece, :, 384:] = (keep1_ref[piece].astype(F32) + recv1_ref[piece].astype(F32)).astype(BF16)


def add_x_kernel(for_x_ref, recv_core_ref, out_ref):
    out_ref[...] = (for_x_ref[...].astype(F32) + recv_core_ref[1].astype(F32)).astype(BF16)


def sum_kernel(parts_ref, out_ref):
    total = parts_ref[0].astype(F32)
    for part in range(1, parts_ref.shape[0]):
        total = total + parts_ref[part].astype(F32)
    out_ref[...] = total.astype(BF16)


def finish_kernel(tok_ref, own_ref, recv_core_ref, from_x_ref, middle_ref, out_ref, done_ref):
    done_ref[...] = jnp.zeros((8, 128), F32)
    grad = own_ref[...] + recv_core_ref[0].astype(F32) + from_x_ref[...].astype(F32)
    normed, inverse = layer_norm(tok_ref[...].astype(F32))
    out_ref[...] = (middle_ref[...] + layer_norm_back(normed, inverse, grad)).astype(BF16)


def final_kernel(lon_ref, after_ref, own_ref, core_ref, x_ref, diagonal_ref, qkv_ref, out_ref, up_ref, down_ref):
    del after_ref
    lon = lon_ref[0]
    scale = 1.0 / math.sqrt(64 * 4 * TOKENS)
    held = [ref[...].astype(F32) * scale for ref in (own_ref, core_ref, x_ref, diagonal_ref)]
    for quarter in range(4):
        part = held[3]
        for distance in range(3):
            part = jnp.where(lon == (quarter ^ distance), held[distance], part)
        at = slice(quarter * 128, (quarter + 1) * 128)
        for matrix in range(3):
            low = matrix * WIDTH + quarter * 128
            qkv_ref[:, low : low + 128] = part[:, matrix * 128 : (matrix + 1) * 128]
        out_ref[:, at] = part[:, 384:512]
        up_ref[:, quarter * 256 : (quarter + 1) * 256] = part[:, 512:768]
        side = (quarter % 2) * 256
        down_ref[(quarter // 2) * 8 : (quarter // 2) * 8 + 8, side : side + 256] = part[:, 768:]


def vmem(count):
    return [pl.BlockSpec(memory_space=pltpu.VMEM)] * count


def smem(count):
    return [pl.BlockSpec(memory_space=pltpu.SMEM)] * count


def shape(dims, dtype):
    return jax.ShapeDtypeStruct(dims, dtype)


TOKEN = (TOKENS, WIDTH)


def params(megabytes):
    return pltpu.CompilerParams(vmem_limit_bytes=megabytes * 1024 * 1024)


def run_near(tok0, w_qkv):
    outs = [shape(TOKEN, BF16)] * 6
    return pl.pallas_call(
        near_kernel,
        out_shape=outs,
        in_specs=vmem(2),
        out_specs=vmem(len(outs)),
        compiler_params=params(NEAR_MB),
        cost_estimate=pl.CostEstimate(flops=2_500_000_000, bytes_accessed=4_000_000, transcendentals=0),
        name="near",
    )(tok0, w_qkv)


def run_pair(count, tok1, tok2, w_qkv, w_down, cot):
    outs = [shape((TOKENS, HIDDEN), BF16)] + [shape(TOKEN, BF16)] * 8
    return pl.pallas_call(
        pair_kernel,
        out_shape=outs,
        in_specs=smem(1) + vmem(5),
        out_specs=vmem(len(outs)),
        compiler_params=params(NEAR_MB),
        cost_estimate=pl.CostEstimate(flops=20_000_000_000, bytes_accessed=2_000_000, transcendentals=0),
        name="pair",
    )(count, tok1, tok2, w_qkv, w_down, cot)


def run_front(core, counts, sectors, w_qkv, w_out, w_up, w_down, cot, near):
    outs = [
        shape(TOKEN, BF16),
        shape((16, 64, 640), BF16),
        shape((16, 64, 640), BF16),
        shape(TOKEN, F32),
        shape(TOKEN, BF16),
        shape(TOKEN, BF16),
        shape(TOKEN, BF16),
        shape(TOKEN, BF16),
        shape((6, GROUP, KEYS), BF16),
        shape(TOKEN, BF16),
    ]
    return pl.pallas_call(
        front_kernel,
        out_shape=outs,
        in_specs=smem(5) + vmem(7 + len(near)),
        out_specs=vmem(len(outs)),
        scratch_shapes=[
            pltpu.VMEM(TOKEN, BF16),
            pltpu.VMEM((4, TOKENS, 256), BF16),
            pltpu.VMEM((4, TOKENS, 128), BF16),
            pltpu.VMEM((2, TOKENS, 256), BF16),
        ],
        compiler_params=params(FRONT_MB),
        cost_estimate=pl.CostEstimate(flops=5_000_000_000, bytes_accessed=12_000_000, transcendentals=600_000),
        name="front",
    )(core, *counts, *sectors, w_qkv, w_out, w_up, w_down, cot, *near)


def run_back(core, saved):
    outs = [
        shape((16, 64, 384), BF16),
        shape((16, 64, 384), BF16),
        shape((4, TOKENS, 128), BF16),
        shape((4, 4 * TOKENS, 128), BF16),
        shape((4, 4 * TOKENS, 128), BF16),
    ]
    return pl.pallas_call(
        back_kernel,
        out_shape=outs,
        in_specs=smem(1) + vmem(len(saved)),
        out_specs=vmem(len(outs)),
        compiler_params=params(BACK_MB),
        cost_estimate=pl.CostEstimate(flops=6_000_000_000, bytes_accessed=12_000_000, transcendentals=0),
        name="back",
    )(core, *saved)


def run_push(w_qkv, grads):
    outs = [shape((2,) + TOKEN, BF16), shape(TOKEN, BF16), shape(TOKEN, F32)]
    return pl.pallas_call(
        push_kernel,
        out_shape=outs,
        in_specs=vmem(4),
        out_specs=vmem(3),
        compiler_params=params(NEAR_MB),
        cost_estimate=pl.CostEstimate(flops=2_000_000_000, bytes_accessed=4_000_000, transcendentals=0),
        name="push",
    )(w_qkv, *grads)


def small_call(kernel, outs, scalars, arrays, name):
    return pl.pallas_call(
        kernel,
        out_shape=outs,
        in_specs=smem(len(scalars)) + vmem(len(arrays)),
        out_specs=vmem(len(outs)),
        compiler_params=params(NEAR_MB),
        cost_estimate=pl.CostEstimate(flops=1_000_000, bytes_accessed=4_000_000, transcendentals=0),
        name=name,
    )(*scalars, *arrays)


def run_join(keep1, recv1, keep2, recv2, after):
    return pl.pallas_call(
        join_kernel,
        out_shape=shape((16, 64, 1024), BF16),
        in_specs=vmem(4) + [pl.BlockSpec(memory_space=pl.ANY)],
        out_specs=vmem(1)[0],
        compiler_params=params(NEAR_MB),
        cost_estimate=pl.CostEstimate(flops=1_000_000, bytes_accessed=4_000_000, transcendentals=0),
        name="join",
    )(keep1, recv1, keep2, recv2, after)


def run_add_x(*parts):
    return small_call(add_x_kernel, [shape(TOKEN, BF16)], [], parts, "add_x")[0]


def run_sum(parts):
    return small_call(sum_kernel, [shape((64, 1024), BF16)], [], [parts], "plane_sum")[0]


def run_finish(*parts):
    return small_call(finish_kernel, [shape(TOKEN, BF16), shape((8, 128), F32)], [], parts, "finish")


def run_final(lon, after, parts):
    outs = [shape((8, 1536), F32), shape((8, 512), F32), shape((8, 1024), F32), shape((16, 512), F32)]
    return pl.pallas_call(
        final_kernel,
        out_shape=outs,
        in_specs=smem(1) + vmem(5),
        out_specs=vmem(len(outs)),
        compiler_params=params(NEAR_MB),
        cost_estimate=pl.CostEstimate(flops=1_000_000, bytes_accessed=400_000, transcendentals=0),
        name="final",
    )(lon, after, *parts)


def sum_sources(values):
    return jnp.sum(values.astype(F32), axis=0).astype(BF16)


def swap(values):
    return lax.ppermute(values, "lon", CORE)


def local(tokens, ocean_count, w_qkv, w_out, w_up, w_down, cotangent):
    flat = tokens.reshape(TOKEN)
    cot = cotangent.reshape(TOKEN)
    tok2 = lax.ppermute(flat, "lon", X_LO)
    count = ocean_count.reshape(1, ROWS_DEV)
    count2 = lax.ppermute(count, "lon", X_LO)
    count1 = swap(count)
    lon = lax.axis_index("lon")
    core = (lon % 2).reshape(1)
    tok1 = swap(flat)
    query, inv_q, *own_kv = run_near(flat, w_qkv)
    tok3 = swap(tok2)
    grad_active, *pair = run_pair(count, tok1, tok2, w_qkv, w_down, cot)
    mate_kv, across_kv = pair[:4], pair[4:]
    count3 = swap(count2)
    front = run_front(
        core,
        (count, count1, count2, count3),
        (flat, tok3),
        w_qkv,
        w_out,
        w_up,
        w_down,
        cot,
        (query, *own_kv[1:3], *mate_kv[1:3], *across_kv[1:3], grad_active),
    )
    block_out, keep1, send1, grad_middle = front[:4]
    recv1 = swap(send1)
    saved = [query, inv_q] + [*own_kv, *mate_kv, *across_kv, *front[4:]]
    keep2, send2, *grads = run_back(core, saved)
    recv2 = swap(send2)
    for_core, for_x, grad_own = run_push(w_qkv, grads)
    joined = run_join(keep1, recv1, keep2, recv2, for_x)
    plane = lax.all_to_all(joined, ("lat", "lon"), 0, 0, axis_index_groups=PLANE_GROUPS, tiled=True)
    plane, for_x, for_core = lax.optimization_barrier((run_sum(plane), for_x, for_core))
    recv_core = swap(for_core)
    from_x = lax.ppermute(run_add_x(for_x, recv_core), "lon", X_LO)
    column = sum_sources(
        lax.all_to_all(plane.reshape(8, 8, 1024), "lat", 0, 0, axis_index_groups=Z_GROUPS, tiled=True)
    )
    gathered = [column] + [lax.ppermute(column, "lon", table) for table in (CORE, X_LO, DIAGONAL)]
    grad_tokens, done = run_finish(flat, grad_own, recv_core, from_x, grad_middle)
    weights = run_final(lon.reshape(1), done, gathered)
    return (block_out.reshape(tokens.shape), grad_tokens.reshape(tokens.shape), *weights)


def solution(mesh):
    in_specs = (P("lat", "lon", None), P("lat", "lon"), P(), P(), P(), P(), P("lat", "lon", None))
    out_specs = (
        P("lat", "lon", None),
        P("lat", "lon", None),
        P("lat", None),
        P("lat", None),
        P("lat", None),
        P("lat", None),
    )
    return jax.shard_map(local, mesh=mesh, in_specs=in_specs, out_specs=out_specs, check_vma=False)
```

time: 85.6 us -> 79.5 us (0.929)
  blocking collectives: 33.6 us -> 31.1 us
  Pallas kernels: 16.4 us -> 14.6 us
    all_to_all x1, blocking collectives: 33.6 us -> 31.1 us  [local(): lax.all_to_all(joined, ('lat', 'lon'), 0, 0, axis_index_groups=PLANE_GROU...]
    ppermute x7, starting transfers between devices: 4.19 us -> 5.66 us  [swap(): return lax.ppermute(values, 'lon', CORE)]
    ppermute x3, starting transfers between devices: 4.44 us -> 3.15 us  [local(): lax.ppermute(column, 'lon', table)]
    pallas_call x1, Pallas kernels: 4.16 us -> 3.13 us  [run_back(): pl.pallas_call(back_kernel, out_shape=outs, in_specs=smem(1) + vmem(len(s...]
    ppermute x7, waiting for transfers between devices: 1.72 us -> 0.79 us  [swap(): return lax.ppermute(values, 'lon', CORE)]
    unnamed x17 -> x18, local copies, waits for them, and re-layouts: 3.14 us -> 2.4 us
    pallas_call x4 -> x3, Pallas kernels: 2.64 us -> 1.98 us  [small_call(): pl.pallas_call(kernel, out_shape=outs, in_specs=smem(len(scalars)) + vmem...]
    pallas_call x2 -> x3, Pallas kernels: 6.81 us -> 7.06 us  [the longest x1 4.71 us: run_front(): pl.pallas_call(front_kernel, out_shape=outs, in_specs=smem(5) + vmem(7 +...]
  transfers between devices with their start and end apart: 14 -> 14, of which waited for: 4 -> 4; matrix products, arithmetic and copies ran while one was open for 0% -> 0% of each run, Pallas kernels for 11% -> 10%
where the time goes in v4:
time: 79.5 us; the launch traced here: 79.3 us
  blocking collectives  31.1 us (39%)
  starting transfers between devices  20.6 us (26%)
  Pallas kernels  14.6 us (18%)
  waiting for transfers between devices  9.71 us (12%)
  local copies, waits for them, and re-layouts  2.4 us (3%)
    all_to_all x1, blocking collectives, local(): lax.all_to_all(joined, ('lat', 'lon'), 0, 0, axis_index_groups=PLANE_GROU...  31.1 us
    all_to_all x1, starting transfers between devices, local(): lax.all_to_all(plane.reshape(8, 8, 1024), 'lat', 0, 0, axis_index_groups=...  7.59 us
    all_to_all x1, waiting for transfers between devices, local(): lax.all_to_all(plane.reshape(8, 8, 1024), 'lat', 0, 0, axis_index_groups=...  7.52 us
    ppermute x7, starting transfers between devices, swap(): return lax.ppermute(values, 'lon', CORE)  5.66 us
    pallas_call x1, Pallas kernels, run_front(): pl.pallas_call(front_kernel, out_shape=outs, in_specs=smem(5) + vmem(7 +...  4.71 us
    ppermute x3, starting transfers between devices, local(): lax.ppermute(column, 'lon', table)  3.15 us
    pallas_call x1, Pallas kernels, run_back(): pl.pallas_call(back_kernel, out_shape=outs, in_specs=smem(1) + vmem(len(s...  3.13 us
    unnamed x18, local copies, waits for them, and re-layouts  2.4 us
  transfers between devices with their start and end apart: 14, of which 4 were waited for; matrix products, arithmetic and copies ran while one was open for 0% of the time, Pallas kernels for 10%

profile of v4, /device:TPU:1, one launch (start us, length us, event | category | flops | bytes accessed | tf_op | source)
XLA Modules:
  0.0 79.3 jit_solution(927418546854158625)
XLA Ops:
  0.6 2.1 %collective-permute-start.1 = (s32[1,3]{1,0:T(1,128)}, s32[1,3]{1,0:T(1,128)S(1)}, u32[]{:S(2)}, u32[]{:S(2)}) collective-permute-start(s32[1,3]{1,0:T(1,128)} %bitcast.15), channel_id=1, source_target_pairs={{0,2},{2,0},{1,3},{3,1},{4,6},{6,4},{5,7},{7,5},{8,10},{10,8},{9,1... | collective-permute-start | bytes 44 | tf_op jit(solution)/shard_map/ppermute | solution.py:536
  2.8 1.3 %collective-permute-start = (s32[1,3]{1,0:T(1,128)}, s32[1,3]{1,0:T(1,128)S(1)}, u32[]{:S(2)}, u32[]{:S(2)}) collective-permute-start(s32[1,3]{1,0:T(1,128)} %bitcast.16), channel_id=1, source_target_pairs={{0,1},{1,0},{2,3},{3,2},{4,5},{5,4},{6,7},{7,6},{8,9},{9,8},{10,11... | collective-permute-start | bytes 44 | tf_op jit(solution)/shard_map/ppermute | solution.py:528
  4.2 1.5 %collective-permute-start.3 = (bf16[192,512]{1,0:T(8,128)(2,1)}, bf16[192,512]{1,0:T(8,128)(2,1)S(1)}, u32[]{:S(2)}, u32[]{:S(2)}) collective-permute-start(bf16[192,512]{1,0:T(8,128)(2,1)} %bitcast.9), channel_id=1, source_target_pairs={{0,2},{2,0},{1,3},{3,1},{4,6},{6,4},{5,7},{7,5},{8,10},{10,8},{9,1... | collective-permute-start | bytes 589832 | tf_op jit(solution)/shard_map/ppermute | solution.py:534
  5.7 1.0 %copy-done = bf16[3,64,512]{2,1,0:T(8,128)(2,1)S(1)} copy-done((bf16[3,64,512]{2,1,0:T(8,128)(2,1)S(1)}, bf16[3,64,512]{2,1,0:T(8,128)(2,1)}, u32[]{:S(2)}) %copy-start) | copy-done | bytes 196632
  6.7 1.4 %copy-done.2 = bf16[512,1536]{1,0:T(8,128)(2,1)S(1)} copy-done((bf16[512,1536]{1,0:T(8,128)(2,1)S(1)}, bf16[512,1536]{1,0:T(8,128)(2,1)}, u32[]{:S(2)}) %copy-start.2) | copy-done | bytes 1572888
  8.1 0.8 %near.1 = (bf16[192,512]{1,0:T(8,128)(2,1)S(1)}, bf16[192,512]{1,0:T(8,128)(2,1)S(1)}, bf16[192,512]{1,0:T(8,128)(2,1)S(1)}, bf16[192,512]{1,0:T(8,128)(2,1)S(1)...) custom-call(bf16[192,512]{1,0:T(8,128)(2,1)S(1)} %bitcast.10, bf16[512,1536]{1,0:T(8,128)(2,1)S(1)} %copy-done.2), custom_call_target="tpu_custom_call" | custom-call | flops 2500000000 | bytes 4000000 | tf_op jit(solution)/shard_map/near/pallas_call | solution.py:388
  9.0 0.9 %collective-permute-start.2 = (s32[1,3]{1,0:T(1,128)S(1)}, s32[1,3]{1,0:T(1,128)S(1)}, u32[]{:S(2)}, u32[]{:S(2)}) collective-permute-start(s32[1,3]{1,0:T(1,128)S(1)} %collective-permute-done.1.count2_ref), channel_id=1, source_target_pairs={{0,1},{1,0},{2,3},{3,2},{4,5},{5,4},{6,7},{7,6},{8,9},{9,8},{10,11... | collective-permute-start | bytes 44 | tf_op jit(solution)/shard_map/ppermute | solution.py:528
  9.8 0.8 %collective-permute-done.3.tok2_ref = bf16[192,512]{1,0:T(8,128)(2,1)S(1)} collective-permute-done((bf16[192,512]{1,0:T(8,128)(2,1)}, bf16[192,512]{1,0:T(8,128)(2,1)S(1)}, u32[]{:S(2)}, u32[]{:S(2)}) %collective-permute-start.3) | collective-permute-done | bytes 196640 | tf_op jit(solution)/shard_map/ppermute | solution.py:534
  10.6 1.1 %collective-permute-start.4 = (bf16[192,512]{1,0:T(8,128)(2,1)S(1)}, bf16[192,512]{1,0:T(8,128)(2,1)S(1)}, u32[]{:S(2)}, u32[]{:S(2)}) collective-permute-start(bf16[192,512]{1,0:T(8,128)(2,1)S(1)} %collective-permute-done.3.tok2_ref), channel_id=1, source_target_pairs={{0,1},{1,0},{2,3},{3,2},{4,5},{5,4},{6,7},{7,6},{8,9},{9,8},{10,11... | collective-permute-start | bytes 589832 | tf_op jit(solution)/shard_map/ppermute | solution.py:528
  11.8 1.7 %pair.1 = (bf16[192,1024]{1,0:T(8,128)(2,1)S(1)}, bf16[192,512]{1,0:T(8,128)(2,1)S(1)}, bf16[192,512]{1,0:T(8,128)(2,1)S(1)}, bf16[192,512]{1,0:T(8,128)(2,1)S(1...) custom-call(s32[1,3]{1,0:T(1,128)S(1)} %bitcast.17, ...), custom_call_target="tpu_custom_call" | custom-call | flops 20000000000 | bytes 2000000 | tf_op jit(solution)/shard_map/pair/pallas_call | solution.py:401
  13.6 4.7 %front.1 = (bf16[192,512]{1,0:T(8,128)(2,1)}, bf16[16,64,640]{2,1,0:T(8,128)(2,1)S(1)}, bf16[16,64,640]{2,1,0:T(8,128)(2,1)S(1)}, f32[192,512]{1,0:T(8,128)S(1)}...) custom-call(s32[1]{0:T(128)} %bitcast.core_ref, ...), custom_call_target="tpu_custom_call" | custom-call | flops 5000000000 | bytes 12000000 | tf_op jit(solution)/shard_map/front/pallas_call | solution.py:425
  18.3 3.1 %back.1 = (bf16[16,64,384]{2,1,0:T(8,128)(2,1)S(1)}, bf16[16,64,384]{2,1,0:T(8,128)(2,1)S(1)}, bf16[4,192,128]{2,1,0:T(8,128)(2,1)S(1)}, bf16[4,768,128]{2,1,0:T(8,128)(2,1)S(1)}, bf16[4,768,128]{2,1,0:T(8,128)(2,1)S(1)}) custom-call(s32[1]{0:T(128)} %bitcast.core_ref, bf16[192,512]{1,0:T(8,128)(2,1)S(1)} %get-tuple-element.48.query_ref, ...), custom_call_target="tpu_custom_call" | custom-call | flops 6000000000 | bytes 12000000 | tf_op jit(solution)/shard_map/back/pallas_call | solution.py:450
  21.5 0.8 collective-permute-start.7
  22.2 1.1 %push.1 = (bf16[2,192,512]{2,1,0:T(8,128)(2,1)S(1)}, bf16[192,512]{1,0:T(8,128)(2,1)S(1)}, f32[192,512]{1,0:T(8,128)S(1)}) custom-call(bf16[512,1536]{1,0:T(8,128)(2,1)S(1)} %copy-done.3, bf16[4,192,128]{2,1,0:T(8,128)(2,1)S(1)} %get-tuple-element.70.gq_ref, bf16[4,768,128]{2,1,0:T(8,128)(2,1)S(1)} %get-tuple-element.71.gk_ref, ...), custom_call_target="tpu_custom_call" | custom-call | flops 2000000000 | bytes 4000000 | tf_op jit(solution)/shard_map/push/pallas_call | solution.py:463
  23.4 0.8 collective-permute-done.7.recv2_ref
  24.6 31.1 %all_to_all.10.parts_ref = bf16[16,64,1024]{2,1,0:T(8,128)(2,1)S(1)} all-to-all(bf16[16,64,1024]{2,1,0:T(8,128)(2,1)S(1)} %join.1), channel_id=1, replica_groups={{30,28,26,24,22,20,18,16,14,12,10,8,6,4,2,0},{31,29,27,25,23,21,19,17,1..., dimensions={0} | all-to-all | bytes 4194304 | tf_op jit(solution)/shard_map/all_to_all | solution.py:564
  55.7 0.9 %plane_sum.1 = bf16[64,1024]{1,0:T(8,128)(2,1)} custom-call(bf16[16,64,1024]{2,1,0:T(8,128)(2,1)S(1)} %all_to_all.10.parts_ref), custom_call_target="tpu_custom_call" | custom-call | flops 1000000 | bytes 4000000 | tf_op jit(solution)/shard_map/plane_sum/pallas_call | solution.py:475
  56.6 1.5 %collective-permute-start.8 = (bf16[2,192,512]{2,1,0:T(8,128)(2,1)S(1)}, bf16[2,192,512]{2,1,0:T(8,128)(2,1)S(1)}, u32[]{:S(2)}, u32[]{:S(2)}) collective-permute-start(bf16[2,192,512]{2,1,0:T(8,128)(2,1)S(1)} %get-tuple-element.80), channel_id=1, source_target_pairs={{0,1},{1,0},{2,3},{3,2},{4,5},{5,4},{6,7},{7,6},{8,9},{9,8},{10,11... | collective-permute-start | bytes 1179656 | tf_op jit(solution)/shard_map/ppermute | solution.py:528
  58.1 7.6 %all-to-all-start.1 = ((bf16[8,8,1024]{2,1,0:T(8,128)(2,1)}), bf16[8,8,1024]{2,1,0:T(8,128)(2,1)S(1)}, u32[]{:S(2)}, u32[]{:S(2)}) async-start(bf16[8,8,1024]{2,1,0:T(8,128)(2,1)} %bitcast.7), calls=%async_computation.1 | async-start | bytes 262144 | tf_op jit(solution)/shard_map/all_to_all | solution.py:569
  66.3 7.5 %all-to-all-done.1 = bf16[8,8,1024]{2,1,0:T(8,128)(2,1)S(1)} async-done(((bf16[8,8,1024]{2,1,0:T(8,128)(2,1)}), bf16[8,8,1024]{2,1,0:T(8,128)(2,1)S(1)}, u32[]{:S(2)}, u32[]{:S(2)}) %all-to-all-start.1) | async-done | bytes 131104 | tf_op jit(solution)/shard_map/all_to_all | solution.py:569
  73.9 2.2 %collective-permute-start.12 = (bf16[8,1024]{1,0:T(8,128)(2,1)S(1)}, bf16[8,1024]{1,0:T(8,128)(2,1)S(1)}, u32[]{:S(2)}, u32[]{:S(2)}) collective-permute-start(bf16[8,1024]{1,0:T(8,128)(2,1)S(1)} %reduce_sum.12.own_ref), channel_id=1, source_target_pairs={{0,3},{3,0},{1,2},{2,1},{4,7},{7,4},{5,6},{6,5},{8,11},{11,8},{9,1... | collective-permute-start | bytes 49160 | tf_op jit(solution)/shard_map/ppermute | solution.py:571
  76.0 1.0 %collective-permute-start.11 = (bf16[8,1024]{1,0:T(8,128)(2,1)S(1)}, bf16[8,1024]{1,0:T(8,128)(2,1)S(1)}, u32[]{:S(2)}, u32[]{:S(2)}) collective-permute-start(bf16[8,1024]{1,0:T(8,128)(2,1)S(1)} %reduce_sum.12.own_ref), channel_id=1, source_target_pairs={{0,2},{2,0},{1,3},{3,1},{4,6},{6,4},{5,7},{7,5},{8,10},{10,8},{9,1... | collective-permute-start | bytes 49160 | tf_op jit(solution)/shard_map/ppermute | solution.py:571
  77.0 1.0 %finish.1 = (bf16[192,512]{1,0:T(8,128)(2,1)}, f32[8,128]{1,0:T(8,128)S(1)}) custom-call(bf16[192,512]{1,0:T(8,128)(2,1)S(1)} %bitcast.12, f32[192,512]{1,0:T(8,128)S(1)} %get-tuple-element.73.own_ref, bf16[2,192,512]{2,1,0:T(8,128)(2,1)S(1)} %collective-permute-done.8.recv_core_ref, bf16[192,512]{1,0:T(8,128)(2,1)S(1)} %collective-permute-done.9.from_x_ref, ...), custom_call_target="tpu_custom_call" | custom-call | flops 1000000 | bytes 4000000 | tf_op jit(solution)/shard_map/finish/pallas_call | solution.py:475
  78.6 0.7 final.1
  (34 shorter events, 1.9 us)
Async XLA Ops:
  0.6 8.3 %collective-permute-start.1 = (s32[1,3]{1,0:T(1,128)}, s32[1,3]{1,0:T(1,128)S(1)}, u32[]{:S(2)}, u32[]{:S(2)}) collective-permute-start(s32[1,3]{1,0:T(1,128)} %bitcast.15), channel_id=1, source_target_pairs={{0,2},{2,0},{1,3},{3,1},{4,6},{6,4},{5,7},{7,5},{8,10},{10,8},{9,1... | collective-permute-start | bytes 44 | tf_op jit(solution)/shard_map/ppermute | solution.py:536
  2.8 10.8 %collective-permute-start = (s32[1,3]{1,0:T(1,128)}, s32[1,3]{1,0:T(1,128)S(1)}, u32[]{:S(2)}, u32[]{:S(2)}) collective-permute-start(s32[1,3]{1,0:T(1,128)} %bitcast.16), channel_id=1, source_target_pairs={{0,1},{1,0},{2,3},{3,2},{4,5},{5,4},{6,7},{7,6},{8,9},{9,8},{10,11... | collective-permute-start | bytes 44 | tf_op jit(solution)/shard_map/ppermute | solution.py:528
  4.1 7.7 %collective-permute-start.5 = (bf16[192,512]{1,0:T(8,128)(2,1)}, bf16[192,512]{1,0:T(8,128)(2,1)S(1)}, u32[]{:S(2)}, u32[]{:S(2)}) collective-permute-start(bf16[192,512]{1,0:T(8,128)(2,1)} %bitcast.8), channel_id=1, source_target_pairs={{0,1},{1,0},{2,3},{3,2},{4,5},{5,4},{6,7},{7,6},{8,9},{9,8},{10,11... | collective-permute-start | bytes 589832 | tf_op jit(solution)/shard_map/ppermute | solution.py:528
  4.2 6.5 %collective-permute-start.3 = (bf16[192,512]{1,0:T(8,128)(2,1)}, bf16[192,512]{1,0:T(8,128)(2,1)S(1)}, u32[]{:S(2)}, u32[]{:S(2)}) collective-permute-start(bf16[192,512]{1,0:T(8,128)(2,1)} %bitcast.9), channel_id=1, source_target_pairs={{0,2},{2,0},{1,3},{3,1},{4,6},{6,4},{5,7},{7,5},{8,10},{10,8},{9,1... | collective-permute-start | bytes 589832 | tf_op jit(solution)/shard_map/ppermute | solution.py:534
  5.7 1.0 %copy-start = (bf16[3,64,512]{2,1,0:T(8,128)(2,1)S(1)}, bf16[3,64,512]{2,1,0:T(8,128)(2,1)}, u32[]{:S(2)}) copy-start(bf16[3,64,512]{2,1,0:T(8,128)(2,1)} %param.7) | copy-start | bytes 589828
  6.7 1.4 %copy-start.2 = (bf16[512,1536]{1,0:T(8,128)(2,1)S(1)}, bf16[512,1536]{1,0:T(8,128)(2,1)}, u32[]{:S(2)}) copy-start(bf16[512,1536]{1,0:T(8,128)(2,1)} %w_qkv_ref.7) | copy-start | bytes 4718596
  8.1 3.7 %copy-start.3 = (bf16[512,1536]{1,0:T(8,128)(2,1)S(1)}, bf16[512,1536]{1,0:T(8,128)(2,1)}, u32[]{:S(2)}) copy-start(bf16[512,1536]{1,0:T(8,128)(2,1)} %w_qkv_ref.7) | copy-start | bytes 4718596
  8.1 3.7 %copy-start.5 = (bf16[1024,512]{1,0:T(8,128)(2,1)S(1)}, bf16[1024,512]{1,0:T(8,128)(2,1)}, u32[]{:S(2)}) copy-start(bf16[1024,512]{1,0:T(8,128)(2,1)} %w_down_ref.3) | copy-start | bytes 3145732
  8.1 3.7 %copy-start.7 = (bf16[3,64,512]{2,1,0:T(8,128)(2,1)S(1)}, bf16[3,64,512]{2,1,0:T(8,128)(2,1)}, u32[]{:S(2)}) copy-start(bf16[3,64,512]{2,1,0:T(8,128)(2,1)} %param.13) | copy-start | bytes 589828
  8.1 3.7 %copy-start.8 = (s32[3,1]{0,1:T(1,128)S(1)}, s32[3,1]{0,1:T(1,128)}, u32[]{:S(2)}) copy-start(s32[3,1]{0,1:T(1,128)} %param.8) | copy-start | bytes 40
  9.0 4.6 %collective-permute-start.2 = (s32[1,3]{1,0:T(1,128)S(1)}, s32[1,3]{1,0:T(1,128)S(1)}, u32[]{:S(2)}, u32[]{:S(2)}) collective-permute-start(s32[1,3]{1,0:T(1,128)S(1)} %collective-permute-done.1.count2_ref), channel_id=1, source_target_pairs={{0,1},{1,0},{2,3},{3,2},{4,5},{5,4},{6,7},{7,6},{8,9},{9,8},{10,11... | collective-permute-start | bytes 44 | tf_op jit(solution)/shard_map/ppermute | solution.py:528
  10.6 2.9 %collective-permute-start.4 = (bf16[192,512]{1,0:T(8,128)(2,1)S(1)}, bf16[192,512]{1,0:T(8,128)(2,1)S(1)}, u32[]{:S(2)}, u32[]{:S(2)}) collective-permute-start(bf16[192,512]{1,0:T(8,128)(2,1)S(1)} %collective-permute-done.3.tok2_ref), channel_id=1, source_target_pairs={{0,1},{1,0},{2,3},{3,2},{4,5},{5,4},{6,7},{7,6},{8,9},{9,8},{10,11... | collective-permute-start | bytes 589832 | tf_op jit(solution)/shard_map/ppermute | solution.py:528
  11.8 1.8 %copy-start.1 = (bf16[3,64,512]{2,1,0:T(8,128)(2,1)S(1)}, bf16[3,64,512]{2,1,0:T(8,128)(2,1)}, u32[]{:S(2)}) copy-start(bf16[3,64,512]{2,1,0:T(8,128)(2,1)} %param.7) | copy-start | bytes 589828
  11.8 1.8 %copy-start.4 = (bf16[512,1024]{1,0:T(8,128)(2,1)S(1)}, bf16[512,1024]{1,0:T(8,128)(2,1)}, u32[]{:S(2)}) copy-start(bf16[512,1024]{1,0:T(8,128)(2,1)} %w_up_ref.1) | copy-start | bytes 3145732
  11.8 1.8 %copy-start.6 = (bf16[512,512]{1,0:T(8,128)(2,1)S(1)}, bf16[512,512]{1,0:T(8,128)(2,1)}, u32[]{:S(2)}) copy-start(bf16[512,512]{1,0:T(8,128)(2,1)} %w_out_ref.1) | copy-start | bytes 1572868
  18.3 5.8 %collective-permute-start.6 = (bf16[16,64,640]{2,1,0:T(8,128)(2,1)S(1)}, bf16[16,64,640]{2,1,0:T(8,128)(2,1)S(1)}, u32[]{:S(2)}, u32[]{:S(2)}) collective-permute-start(bf16[16,64,640]{2,1,0:T(8,128)(2,1)S(1)} %get-tuple-element.75), channel_id=1, source_target_pairs={{0,1},{1,0},{2,3},{3,2},{4,5},{5,4},{6,7},{7,6},{8,9},{9,8},{10,11... | collective-permute-start | bytes 3932168 | tf_op jit(solution)/shard_map/ppermute | solution.py:528
  21.5 2.7 %collective-permute-start.7 = (bf16[16,64,384]{2,1,0:T(8,128)(2,1)S(1)}, bf16[16,64,384]{2,1,0:T(8,128)(2,1)S(1)}, u32[]{:S(2)}, u32[]{:S(2)}) collective-permute-start(bf16[16,64,384]{2,1,0:T(8,128)(2,1)S(1)} %get-tuple-element.77), channel_id=1, source_target_pairs={{0,1},{1,0},{2,3},{3,2},{4,5},{5,4},{6,7},{7,6},{8,9},{9,8},{10,11... | collective-permute-start | bytes 2359304 | tf_op jit(solution)/shard_map/ppermute | solution.py:528
  56.6 9.1 %collective-permute-start.8 = (bf16[2,192,512]{2,1,0:T(8,128)(2,1)S(1)}, bf16[2,192,512]{2,1,0:T(8,128)(2,1)S(1)}, u32[]{:S(2)}, u32[]{:S(2)}) collective-permute-start(bf16[2,192,512]{2,1,0:T(8,128)(2,1)S(1)} %get-tuple-element.80), channel_id=1, source_target_pairs={{0,1},{1,0},{2,3},{3,2},{4,5},{5,4},{6,7},{7,6},{8,9},{9,8},{10,11... | collective-permute-start | bytes 1179656 | tf_op jit(solution)/shard_map/ppermute | solution.py:528
  58.1 15.7 %all-to-all-start.1 = ((bf16[8,8,1024]{2,1,0:T(8,128)(2,1)}), bf16[8,8,1024]{2,1,0:T(8,128)(2,1)S(1)}, u32[]{:S(2)}, u32[]{:S(2)}) async-start(bf16[8,8,1024]{2,1,0:T(8,128)(2,1)} %bitcast.7), calls=%async_computation.1 | async-start | bytes 262144 | tf_op jit(solution)/shard_map/all_to_all | solution.py:569
  65.8 11.3 %collective-permute-start.9 = (bf16[192,512]{1,0:T(8,128)(2,1)S(1)}, bf16[192,512]{1,0:T(8,128)(2,1)S(1)}, u32[]{:S(2)}, u32[]{:S(2)}) collective-permute-start(bf16[192,512]{1,0:T(8,128)(2,1)S(1)} %add_x.1), channel_id=1, source_target_pairs={{0,2},{2,0},{1,3},{3,1},{4,6},{6,4},{5,7},{7,5},{8,10},{10,8},{9,1... | collective-permute-start | bytes 589832 | tf_op jit(solution)/shard_map/ppermute | solution.py:567
  73.9 4.2 %collective-permute-start.12 = (bf16[8,1024]{1,0:T(8,128)(2,1)S(1)}, bf16[8,1024]{1,0:T(8,128)(2,1)S(1)}, u32[]{:S(2)}, u32[]{:S(2)}) collective-permute-start(bf16[8,1024]{1,0:T(8,128)(2,1)S(1)} %reduce_sum.12.own_ref), channel_id=1, source_target_pairs={{0,3},{3,0},{1,2},{2,1},{4,7},{7,4},{5,6},{6,5},{8,11},{11,8},{9,1... | collective-permute-start | bytes 49160 | tf_op jit(solution)/shard_map/ppermute | solution.py:571
  76.0 2.6 %collective-permute-start.11 = (bf16[8,1024]{1,0:T(8,128)(2,1)S(1)}, bf16[8,1024]{1,0:T(8,128)(2,1)S(1)}, u32[]{:S(2)}, u32[]{:S(2)}) collective-permute-start(bf16[8,1024]{1,0:T(8,128)(2,1)S(1)} %reduce_sum.12.own_ref), channel_id=1, source_target_pairs={{0,2},{2,0},{1,3},{3,1},{4,6},{6,4},{5,7},{7,5},{8,10},{10,8},{9,1... | collective-permute-start | bytes 49160 | tf_op jit(solution)/shard_map/ppermute | solution.py:571
  77.0 1.6 %collective-permute-start.10 = (bf16[8,1024]{1,0:T(8,128)(2,1)S(1)}, bf16[8,1024]{1,0:T(8,128)(2,1)S(1)}, u32[]{:S(2)}, u32[]{:S(2)}) collective-permute-start(bf16[8,1024]{1,0:T(8,128)(2,1)S(1)} %reduce_sum.12.own_ref), channel_id=1, source_target_pairs={{0,1},{1,0},{2,3},{3,2},{4,5},{5,4},{6,7},{7,6},{8,9},{9,8},{10,11... | collective-permute-start | bytes 49160 | tf_op jit(solution)/shard_map/ppermute | solution.py:571

commit v5 on v4

--- a/solution.py
+++ b/solution.py
@@ -140,11 +140,13 @@
     query_ref[...] = (query_raw * inv_q).astype(BF16)
 
 
-def pair_kernel(count_ref, tok1_ref, tok2_ref, w_qkv_ref, w_down_ref, cot_ref, grad_active_ref, *refs):
-    blocks = head_blocks()
+def active_kernel(count_ref, w_down_ref, cot_ref, grad_active_ref):
     branch = (own_mask(count_ref) * cot_ref[...].astype(F32)).astype(BF16)
     grad_active_ref[...] = mm_nt(branch, w_down_ref[...]).astype(BF16)
-    key_value([tok1_ref, tok2_ref], w_qkv_ref, blocks, *refs)
+
+
+def pair_kernel(tok1_ref, tok2_ref, w_qkv_ref, *refs):
+    key_value([tok1_ref, tok2_ref], w_qkv_ref, head_blocks(), *refs)
 
 
 PLACES = [(row, slice(low, low + GROUP)) for row in range(ROWS_DEV) for low in (0, GROUP)]
@@ -189,6 +191,8 @@
     lift_ref,
     attn_ref,
     branch_ref,
+    active_ref,
+    glift_ref,
 ):
     blocks = head_blocks()
     masks_b = head_masks(BF16)
@@ -210,9 +214,12 @@
         for row, lanes in PLACES
     ]
     for at, (row, lanes) in enumerate(PLACES):
-        expscore = jnp.exp(scores[at] * (SOFTMAX_SCALE / HEAD_DIM) - SOFTMAX_SCALE) * key_masks[row]
-        total = jnp.sum(expscore, axis=1, keepdims=True)
-        probs_ref[at] = (expscore * (1.0 / total)).astype(BF16)
+        for head in range(4):
+            some = rows_of(head)
+            logits = scores[at][some] * (SOFTMAX_SCALE / HEAD_DIM) - SOFTMAX_SCALE
+            expscore = jnp.exp(logits) * key_masks[row]
+            total = jnp.sum(expscore, axis=1, keepdims=True)
+            probs_ref[at, some, :] = (expscore * (1.0 / total)).astype(BF16)
     mixed = [mm(probs_ref[at], row_join(row, lanes, value_refs)) for at, (row, lanes) in enumerate(PLACES)]
     for at, (row, lanes) in enumerate(PLACES):
         att_ref[rows_of(row), lanes] = unstack_heads(mixed[at], masks_f).astype(BF16)
@@ -223,13 +230,17 @@
     normed_two, inverse = layer_norm(middle)
     normed_two_b = normed_two.astype(BF16)
     lifted = mm(normed_two_b, w_up_ref[...])
-    square = lifted * lifted
-    bent = jnp.tanh(GELU_A * lifted * (1.0 + GELU_B * square))
-    half = 0.5 * (1.0 + bent)
-    active = (lifted * half).astype(BF16)
-    slope = half + 0.5 * lifted * (1.0 - bent * bent) * (GELU_A * (1.0 + 3.0 * GELU_B * square))
+    for low in range(0, TOKENS, 48):
+        rows = slice(low, low + 48)
+        some = lifted[rows]
+        square = some * some
+        bent = jnp.tanh(GELU_A * some * (1.0 + GELU_B * square))
+        half = 0.5 * (1.0 + bent)
+        active_ref[rows, :] = (some * half).astype(BF16)
+        slope = half + 0.5 * some * (1.0 - bent * bent) * (GELU_A * (1.0 + 3.0 * GELU_B * square))
+        glift_ref[rows, :] = (slope * grad_active_ref[rows, :].astype(F32)).astype(BF16)
+    active, grad_lifted = active_ref[...], glift_ref[...]
     branch = (mask * cot_ref[...].astype(F32)).astype(BF16)
-    grad_lifted = (slope * grad_active_ref[...].astype(F32)).astype(BF16)
     grad_normed = mm_nt(grad_lifted, w_up_ref[...])
     for part in range(2):
         branch_ref[part] = branch[:, part * 256 : (part + 1) * 256]
@@ -265,24 +276,37 @@
     return (inverse_b.astype(F32) * (grad - normed * shift)).astype(BF16)
 
 
+def qkv_half(out_ref, half_index, normed_refs, gq_ref, gk_ref, gv_ref):
+    normed_all = jnp.concatenate([ref[...] for ref in normed_refs], axis=0)
+    own_normed_t, normed_all_t = normed_refs[0][...].T, normed_all.T
+    pair = jnp.concatenate([gq_ref[half_index], gq_ref[half_index + 2]], axis=1)
+    term_q = mm(own_normed_t, pair)
+    for x_lo in range(2):
+        store_pieces(out_ref, x_lo, 0, term_q[:, x_lo * 128 : (x_lo + 1) * 128])
+        pair = jnp.concatenate([gk_ref[half_index + 2 * x_lo], gv_ref[half_index + 2 * x_lo]], axis=1)
+        store_pieces(out_ref, x_lo, 128, mm(normed_all_t, pair))
+
+
 def back_kernel(core_ref, query_ref, inv_q_ref, *refs):
-    sectors, (probs_ref, grad_att_ref, keep_ref, send_ref, gq_ref, gk_ref, gv_ref) = refs[:16], refs[16:]
+    sectors, (probs_ref, grad_att_ref, send_ref, gq_ref, gk_ref, gv_ref, scores_ref) = refs[:16], refs[16:]
     normed_refs, key_refs, value_refs, inv_k_refs = (sectors[at::4] for at in range(4))
     blocks = head_blocks()
     masks_b = head_masks(BF16)
     masks_f = head_masks(F32)
-    core = core_ref[0]
     stacked_q = [stack_heads(query_ref[rows_of(row), lanes], masks_b) for row, lanes in PLACES]
     stacked_g = [stack_heads(grad_att_ref[rows_of(row), lanes], masks_b) for row, lanes in PLACES]
     keys = [row_join(row, lanes, key_refs) for row, lanes in PLACES]
     grad_probs = [
         mm_nt(stacked_g[at], row_join(row, lanes, value_refs)) for at, (row, lanes) in enumerate(PLACES)
     ]
-    grad_scores = []
     for at in range(len(PLACES)):
-        probs = probs_ref[at].astype(F32)
-        delta = jnp.sum(probs * grad_probs[at], axis=1, keepdims=True)
-        grad_scores.append((probs * (grad_probs[at] - delta) * (SOFTMAX_SCALE / HEAD_DIM)).astype(BF16))
+        for head in range(4):
+            some = rows_of(head)
+            probs = probs_ref[at, some, :].astype(F32)
+            grads = grad_probs[at][some]
+            delta = jnp.sum(probs * grads, axis=1, keepdims=True)
+            scores_ref[at, some, :] = (probs * (grads - delta) * (SOFTMAX_SCALE / HEAD_DIM)).astype(BF16)
+    grad_scores = [scores_ref[at] for at in range(len(PLACES))]
     grad_v = [mm_tn(probs_ref[at], stacked_g[at]).astype(BF16) for at in range(len(PLACES))]
     grad_k = [mm_tn(grad_scores[at], stacked_q[at]) for at in range(len(PLACES))]
     grad_q = [unstack_heads(mm(grad_scores[at], keys[at]), masks_f) for at in range(len(PLACES))]
@@ -299,18 +323,11 @@
                     rows = slice(sector * TOKENS + own.start, sector * TOKENS + own.stop)
                     ref[quarter, rows, :] = grad[sector * SECTOR : (sector + 1) * SECTOR, cut]
 
-    normed_all = jnp.concatenate([ref[...] for ref in normed_refs], axis=0)
-    own_normed_t, normed_all_t = normed_refs[0][...].T, normed_all.T
-    for out_ref, half_index in ((keep_ref, core), (send_ref, 1 - core)):
-        pair = jnp.concatenate([gq_ref[half_index], gq_ref[half_index + 2]], axis=1)
-        term_q = mm(own_normed_t, pair)
-        for x_lo in range(2):
-            store_pieces(out_ref, x_lo, 0, term_q[:, x_lo * 128 : (x_lo + 1) * 128])
-            pair = jnp.concatenate([gk_ref[half_index + 2 * x_lo], gv_ref[half_index + 2 * x_lo]], axis=1)
-            store_pieces(out_ref, x_lo, 128, mm(normed_all_t, pair))
-
-
-def push_kernel(w_qkv_ref, gq_ref, gk_ref, gv_ref, for_core_ref, for_x_ref, own_ref):
+    qkv_half(send_ref, 1 - core_ref[0], normed_refs, gq_ref, gk_ref, gv_ref)
+
+
+def push_kernel(core_ref, w_qkv_ref, gq_ref, gk_ref, gv_ref, *refs):
+    normed_refs, (keep_ref, for_core_ref, for_x_ref, own_ref) = refs[:4], refs[4:]
     grad_q = jnp.concatenate([gq_ref[part] for part in range(4)], axis=1)
     grad_kv = jnp.concatenate([ref[part] for ref in (gk_ref, gv_ref) for part in range(4)], axis=1)
     grad_normed = mm_nt(grad_kv, w_qkv_ref[:, WIDTH:])
@@ -318,6 +335,7 @@
     for_x_ref[...] = grad_normed[2 * TOKENS : 3 * TOKENS].astype(BF16)
     for_core_ref[1] = grad_normed[3 * TOKENS :].astype(BF16)
     own_ref[...] = grad_normed[:TOKENS] + mm_nt(grad_q, w_qkv_ref[:, :WIDTH])
+    qkv_half(keep_ref, core_ref[0], normed_refs, gq_ref, gk_ref, gv_ref)
 
 
 def join_kernel(keep1_ref, recv1_ref, keep2_ref, recv2_ref, after_ref, out_ref):
@@ -332,10 +350,12 @@
 
 
 def sum_kernel(parts_ref, out_ref):
-    total = parts_ref[0].astype(F32)
-    for part in range(1, parts_ref.shape[0]):
-        total = total + parts_ref[part].astype(F32)
-    out_ref[...] = total.astype(BF16)
+    for low in range(0, out_ref.shape[0], 16):
+        rows = slice(low, low + 16)
+        total = parts_ref[0, rows, :].astype(F32)
+        for part in range(1, parts_ref.shape[0]):
+            total = total + parts_ref[part, rows, :].astype(F32)
+        out_ref[rows, :] = total.astype(BF16)
 
 
 def finish_kernel(tok_ref, own_ref, recv_core_ref, from_x_ref, middle_ref, out_ref, done_ref):
@@ -396,17 +416,29 @@
     )(tok0, w_qkv)
 
 
-def run_pair(count, tok1, tok2, w_qkv, w_down, cot):
-    outs = [shape((TOKENS, HIDDEN), BF16)] + [shape(TOKEN, BF16)] * 8
+def run_active(count, w_down, cot):
+    return pl.pallas_call(
+        active_kernel,
+        out_shape=shape((TOKENS, HIDDEN), BF16),
+        in_specs=smem(1) + vmem(2),
+        out_specs=vmem(1)[0],
+        compiler_params=params(NEAR_MB),
+        cost_estimate=pl.CostEstimate(flops=2_500_000_000, bytes_accessed=2_000_000, transcendentals=0),
+        name="active",
+    )(count, w_down, cot)
+
+
+def run_pair(tok1, tok2, w_qkv):
+    outs = [shape(TOKEN, BF16)] * 8
     return pl.pallas_call(
         pair_kernel,
         out_shape=outs,
-        in_specs=smem(1) + vmem(5),
+        in_specs=vmem(3),
         out_specs=vmem(len(outs)),
         compiler_params=params(NEAR_MB),
         cost_estimate=pl.CostEstimate(flops=20_000_000_000, bytes_accessed=2_000_000, transcendentals=0),
         name="pair",
-    )(count, tok1, tok2, w_qkv, w_down, cot)
+    )(tok1, tok2, w_qkv)
 
 
 def run_front(core, counts, sectors, w_qkv, w_out, w_up, w_down, cot, near):
@@ -432,6 +464,8 @@
             pltpu.VMEM((4, TOKENS, 256), BF16),
             pltpu.VMEM((4, TOKENS, 128), BF16),
             pltpu.VMEM((2, TOKENS, 256), BF16),
+            pltpu.VMEM((TOKENS, HIDDEN), BF16),
+            pltpu.VMEM((TOKENS, HIDDEN), BF16),
         ],
         compiler_params=params(FRONT_MB),
         cost_estimate=pl.CostEstimate(flops=5_000_000_000, bytes_accessed=12_000_000, transcendentals=600_000),
@@ -442,7 +476,6 @@
 def run_back(core, saved):
     outs = [
         shape((16, 64, 384), BF16),
-        shape((16, 64, 384), BF16),
         shape((4, TOKENS, 128), BF16),
         shape((4, 4 * TOKENS, 128), BF16),
         shape((4, 4 * TOKENS, 128), BF16),
@@ -452,23 +485,24 @@
         out_shape=outs,
         in_specs=smem(1) + vmem(len(saved)),
         out_specs=vmem(len(outs)),
+        scratch_shapes=[pltpu.VMEM((6, GROUP, KEYS), BF16)],
         compiler_params=params(BACK_MB),
         cost_estimate=pl.CostEstimate(flops=6_000_000_000, bytes_accessed=12_000_000, transcendentals=0),
         name="back",
     )(core, *saved)
 
 
-def run_push(w_qkv, grads):
-    outs = [shape((2,) + TOKEN, BF16), shape(TOKEN, BF16), shape(TOKEN, F32)]
+def run_push(core, w_qkv, grads, normed):
+    outs = [shape((16, 64, 384), BF16), shape((2,) + TOKEN, BF16), shape(TOKEN, BF16), shape(TOKEN, F32)]
     return pl.pallas_call(
         push_kernel,
         out_shape=outs,
-        in_specs=vmem(4),
-        out_specs=vmem(3),
-        compiler_params=params(NEAR_MB),
+        in_specs=smem(1) + vmem(8),
+        out_specs=vmem(4),
+        compiler_params=params(BACK_MB),
         cost_estimate=pl.CostEstimate(flops=2_000_000_000, bytes_accessed=4_000_000, transcendentals=0),
         name="push",
-    )(w_qkv, *grads)
+    )(core, w_qkv, *grads, *normed)
 
 
 def small_call(kernel, outs, scalars, arrays, name):
@@ -540,7 +574,8 @@
     tok1 = swap(flat)
     query, inv_q, *own_kv = run_near(flat, w_qkv)
     tok3 = swap(tok2)
-    grad_active, *pair = run_pair(count, tok1, tok2, w_qkv, w_down, cot)
+    grad_active = run_active(count, w_down, cot)
+    pair = run_pair(tok1, tok2, w_qkv)
     mate_kv, across_kv = pair[:4], pair[4:]
     count3 = swap(count2)
     front = run_front(
@@ -557,9 +592,10 @@
     block_out, keep1, send1, grad_middle = front[:4]
     recv1 = swap(send1)
     saved = [query, inv_q] + [*own_kv, *mate_kv, *across_kv, *front[4:]]
-    keep2, send2, *grads = run_back(core, saved)
+    send2, *grads = run_back(core, saved)
     recv2 = swap(send2)
-    for_core, for_x, grad_own = run_push(w_qkv, grads)
+    normed = [own_kv[0], mate_kv[0], across_kv[0], front[4]]
+    keep2, for_core, for_x, grad_own = run_push(core, w_qkv, grads, normed)
     joined = run_join(keep1, recv1, keep2, recv2, for_x)
     plane = lax.all_to_all(joined, ("lat", "lon"), 0, 0, axis_index_groups=PLANE_GROUPS, tiled=True)
     plane, for_x, for_core = lax.optimization_barrier((run_sum(plane), for_x, for_core))

time: 79.5 us -> 78.3 us (0.985)
  starting transfers between devices: 20.6 us -> 19.3 us
  waiting for transfers between devices: 9.71 us -> 8.72 us
    ppermute x7, starting transfers between devices: 5.66 us -> 4.48 us  [swap(): return lax.ppermute(values, 'lon', CORE)]
    pallas_call x2 -> x3, Pallas kernels: 2.83 us -> 3.64 us  [the longest x1 1.63 us: run_push(): pl.pallas_call(push_kernel, out_shape=outs, in_specs=smem(1) + vmem(8), o...]
    ppermute x1, waiting for transfers between devices: 0.81 us -> 0.01 us  [local(): tok2 = lax.ppermute(flat, 'lon', X_LO)]
    unnamed x18 -> x22, local copies, waits for them, and re-layouts: 2.4 us -> 3.08 us
where the time goes in v5:
time: 78.3 us; the launch traced here: 78.1 us
  blocking collectives  31.4 us (40%)
  starting transfers between devices  19.3 us (25%)
  Pallas kernels  14.8 us (19%)
  waiting for transfers between devices  8.72 us (11%)
  local copies, waits for them, and re-layouts  3.08 us (4%)
    all_to_all x1, blocking collectives, local(): lax.all_to_all(joined, ('lat', 'lon'), 0, 0, axis_index_groups=PLANE_GROU...  31.4 us
    all_to_all x1, waiting for transfers between devices, local(): lax.all_to_all(plane.reshape(8, 8, 1024), 'lat', 0, 0, axis_index_groups=...  7.67 us
    all_to_all x1, starting transfers between devices, local(): lax.all_to_all(plane.reshape(8, 8, 1024), 'lat', 0, 0, axis_index_groups=...  7.55 us
    pallas_call x1, Pallas kernels, run_front(): pl.pallas_call(front_kernel, out_shape=outs, in_specs=smem(5) + vmem(7 +...  4.64 us
    ppermute x7, starting transfers between devices, swap(): return lax.ppermute(values, 'lon', CORE)  4.48 us
    ppermute x3, starting transfers between devices, local(): lax.ppermute(column, 'lon', table)  3.15 us
    unnamed x22, local copies, waits for them, and re-layouts  3.08 us
    pallas_call x1, Pallas kernels, run_back(): pl.pallas_call(back_kernel, out_shape=outs, in_specs=smem(1) + vmem(len(s...  2.51 us
  transfers between devices with their start and end apart: 14, of which 4 were waited for; matrix products, arithmetic and copies ran while one was open for 0% of the time, Pallas kernels for 10%

profile of v5, /device:TPU:1, one launch (start us, length us, event | category | flops | bytes accessed | tf_op | source)
XLA Modules:
  0.0 78.1 jit_solution(12170972644325925759)
XLA Ops:
  0.6 2.1 %collective-permute-start.1 = (s32[1,3]{1,0:T(1,128)}, s32[1,3]{1,0:T(1,128)S(1)}, u32[]{:S(2)}, u32[]{:S(2)}) collective-permute-start(s32[1,3]{1,0:T(1,128)} %bitcast.15), channel_id=1, source_target_pairs={{0,2},{2,0},{1,3},{3,1},{4,6},{6,4},{5,7},{7,5},{8,10},{10,8},{9,1... | collective-permute-start | bytes 44 | tf_op jit(solution)/shard_map/ppermute | solution.py:570
  2.8 1.3 %collective-permute-start = (s32[1,3]{1,0:T(1,128)}, s32[1,3]{1,0:T(1,128)S(1)}, u32[]{:S(2)}, u32[]{:S(2)}) collective-permute-start(s32[1,3]{1,0:T(1,128)} %bitcast.16), channel_id=1, source_target_pairs={{0,1},{1,0},{2,3},{3,2},{4,5},{5,4},{6,7},{7,6},{8,9},{9,8},{10,11... | collective-permute-start | bytes 44 | tf_op jit(solution)/shard_map/ppermute | solution.py:562
  4.2 1.5 %collective-permute-start.3 = (bf16[192,512]{1,0:T(8,128)(2,1)}, bf16[192,512]{1,0:T(8,128)(2,1)S(1)}, u32[]{:S(2)}, u32[]{:S(2)}) collective-permute-start(bf16[192,512]{1,0:T(8,128)(2,1)} %bitcast.9), channel_id=1, source_target_pairs={{0,2},{2,0},{1,3},{3,1},{4,6},{6,4},{5,7},{7,5},{8,10},{10,8},{9,1... | collective-permute-start | bytes 589832 | tf_op jit(solution)/shard_map/ppermute | solution.py:568
  5.7 1.0 %copy-done = bf16[3,64,512]{2,1,0:T(8,128)(2,1)S(1)} copy-done((bf16[3,64,512]{2,1,0:T(8,128)(2,1)S(1)}, bf16[3,64,512]{2,1,0:T(8,128)(2,1)}, u32[]{:S(2)}) %copy-start) | copy-done | bytes 196632
  6.7 1.4 %copy-done.2 = bf16[512,1536]{1,0:T(8,128)(2,1)S(1)} copy-done((bf16[512,1536]{1,0:T(8,128)(2,1)S(1)}, bf16[512,1536]{1,0:T(8,128)(2,1)}, u32[]{:S(2)}) %copy-start.2) | copy-done | bytes 1572888
  8.1 0.8 %near.1 = (bf16[192,512]{1,0:T(8,128)(2,1)S(1)}, bf16[192,512]{1,0:T(8,128)(2,1)S(1)}, bf16[192,512]{1,0:T(8,128)(2,1)S(1)}, bf16[192,512]{1,0:T(8,128)(2,1)S(1)...) custom-call(bf16[192,512]{1,0:T(8,128)(2,1)S(1)} %bitcast.10, bf16[512,1536]{1,0:T(8,128)(2,1)S(1)} %copy-done.2), custom_call_target="tpu_custom_call" | custom-call | flops 2500000000 | bytes 4000000 | tf_op jit(solution)/shard_map/near/pallas_call | solution.py:408
  9.0 0.7 copy-done.9
  9.6 1.0 %active.1.grad_active_ref = bf16[192,1024]{1,0:T(8,128)(2,1)S(1)} custom-call(s32[1,3]{1,0:T(1,128)S(1)} %bitcast.17, bf16[1024,512]{1,0:T(8,128)(2,1)S(1)} %copy-done.5, bf16[192,512]{1,0:T(8,128)(2,1)S(1)} %bitcast.13), custom_call_target="tpu_custom_call" | custom-call | flops 2500000000 | bytes 2000000 | tf_op jit(solution)/shard_map/active/pallas_call | solution.py:420
  10.7 0.9 %collective-permute-start.2 = (s32[1,3]{1,0:T(1,128)S(1)}, s32[1,3]{1,0:T(1,128)S(1)}, u32[]{:S(2)}, u32[]{:S(2)}) collective-permute-start(s32[1,3]{1,0:T(1,128)S(1)} %collective-permute-done.1.count2_ref), channel_id=1, source_target_pairs={{0,1},{1,0},{2,3},{3,2},{4,5},{5,4},{6,7},{7,6},{8,9},{9,8},{10,11... | collective-permute-start | bytes 44 | tf_op jit(solution)/shard_map/ppermute | solution.py:562
  11.8 1.0 %pair.1 = (bf16[192,512]{1,0:T(8,128)(2,1)S(1)}, bf16[192,512]{1,0:T(8,128)(2,1)S(1)}, bf16[192,512]{1,0:T(8,128)(2,1)S(1)}, bf16[192,512]{1,0:T(8,128)(2,1)S(1)...) custom-call(bf16[192,512]{1,0:T(8,128)(2,1)S(1)} %collective-permute, ...), custom_call_target="tpu_custom_call" | custom-call | flops 20000000000 | bytes 2000000 | tf_op jit(solution)/shard_map/pair/pallas_call | solution.py:433
  13.1 4.6 %front.1 = (bf16[192,512]{1,0:T(8,128)(2,1)}, bf16[16,64,640]{2,1,0:T(8,128)(2,1)S(1)}, bf16[16,64,640]{2,1,0:T(8,128)(2,1)S(1)}, f32[192,512]{1,0:T(8,128)S(1)}...) custom-call(s32[1]{0:T(128)} %bitcast.core_ref, ...), custom_call_target="tpu_custom_call" | custom-call | flops 5000000000 | bytes 12000000 | tf_op jit(solution)/shard_map/front/pallas_call | solution.py:457
  17.9 2.5 %back.1 = (bf16[16,64,384]{2,1,0:T(8,128)(2,1)S(1)}, bf16[4,192,128]{2,1,0:T(8,128)(2,1)S(1)}, bf16[4,768,128]{2,1,0:T(8,128)(2,1)S(1)}, bf16[4,768,128]{2,1,0:T(8,128)(2,1)S(1)}) custom-call(s32[1]{0:T(128)} %bitcast.core_ref, bf16[192,512]{1,0:T(8,128)(2,1)S(1)} %get-tuple-element.47.query_ref, bf16[192,512]{1,0:T(8,128)(2,1)S(1)} %get-tuple-element.55.inv_q_ref, ...), custom_call_target="tpu_custom_call" | custom-call | flops 6000000000 | bytes 12000000 | tf_op jit(solution)/shard_map/back/pallas_call | solution.py:483
  20.4 0.6 collective-permute-start.7
  21.0 1.6 %push.1 = (bf16[16,64,384]{2,1,0:T(8,128)(2,1)S(1)}, bf16[2,192,512]{2,1,0:T(8,128)(2,1)S(1)}, bf16[192,512]{1,0:T(8,128)(2,1)S(1)}, f32[192,512]{1,0:T(8,128)S(1)}) custom-call(s32[1]{0:T(128)} %bitcast.core_ref, bf16[512,1536]{1,0:T(8,128)(2,1)S(1)} %copy-done.3, bf16[4,192,128]{2,1,0:T(8,128)(2,1)S(1)} %get-tuple-element.68.gq_ref, ...), custom_call_target="tpu_custom_call" | custom-call | flops 2000000000 | bytes 4000000 | tf_op jit(solution)/shard_map/push/pallas_call | solution.py:497
  23.0 0.5 join.1
  23.5 31.4 %all_to_all.10.parts_ref = bf16[16,64,1024]{2,1,0:T(8,128)(2,1)S(1)} all-to-all(bf16[16,64,1024]{2,1,0:T(8,128)(2,1)S(1)} %join.1), channel_id=1, replica_groups={{30,28,26,24,22,20,18,16,14,12,10,8,6,4,2,0},{31,29,27,25,23,21,19,17,1..., dimensions={0} | all-to-all | bytes 4194304 | tf_op jit(solution)/shard_map/all_to_all | solution.py:600
  54.9 0.9 %plane_sum.1 = bf16[64,1024]{1,0:T(8,128)(2,1)} custom-call(bf16[16,64,1024]{2,1,0:T(8,128)(2,1)S(1)} %all_to_all.10.parts_ref), custom_call_target="tpu_custom_call" | custom-call | flops 1000000 | bytes 4000000 | tf_op jit(solution)/shard_map/plane_sum/pallas_call | solution.py:509
  55.8 1.3 %collective-permute-start.8 = (bf16[2,192,512]{2,1,0:T(8,128)(2,1)S(1)}, bf16[2,192,512]{2,1,0:T(8,128)(2,1)S(1)}, u32[]{:S(2)}, u32[]{:S(2)}) collective-permute-start(bf16[2,192,512]{2,1,0:T(8,128)(2,1)S(1)} %get-tuple-element.78), channel_id=1, source_target_pairs={{0,1},{1,0},{2,3},{3,2},{4,5},{5,4},{6,7},{7,6},{8,9},{9,8},{10,11... | collective-permute-start | bytes 1179656 | tf_op jit(solution)/shard_map/ppermute | solution.py:562
  57.1 7.5 %all-to-all-start.1 = ((bf16[8,8,1024]{2,1,0:T(8,128)(2,1)}), bf16[8,8,1024]{2,1,0:T(8,128)(2,1)S(1)}, u32[]{:S(2)}, u32[]{:S(2)}) async-start(bf16[8,8,1024]{2,1,0:T(8,128)(2,1)} %bitcast.7), calls=%async_computation.1 | async-start | bytes 262144 | tf_op jit(solution)/shard_map/all_to_all | solution.py:605
  65.1 7.7 %all-to-all-done.1 = bf16[8,8,1024]{2,1,0:T(8,128)(2,1)S(1)} async-done(((bf16[8,8,1024]{2,1,0:T(8,128)(2,1)}), bf16[8,8,1024]{2,1,0:T(8,128)(2,1)S(1)}, u32[]{:S(2)}, u32[]{:S(2)}) %all-to-all-start.1) | async-done | bytes 131104 | tf_op jit(solution)/shard_map/all_to_all | solution.py:605
  72.8 2.0 %collective-permute-start.12 = (bf16[8,1024]{1,0:T(8,128)(2,1)S(1)}, bf16[8,1024]{1,0:T(8,128)(2,1)S(1)}, u32[]{:S(2)}, u32[]{:S(2)}) collective-permute-start(bf16[8,1024]{1,0:T(8,128)(2,1)S(1)} %reduce_sum.12.own_ref), channel_id=1, source_target_pairs={{0,3},{3,0},{1,2},{2,1},{4,7},{7,4},{5,6},{6,5},{8,11},{11,8},{9,1... | collective-permute-start | bytes 49160 | tf_op jit(solution)/shard_map/ppermute | solution.py:607
  74.8 1.1 %collective-permute-start.11 = (bf16[8,1024]{1,0:T(8,128)(2,1)S(1)}, bf16[8,1024]{1,0:T(8,128)(2,1)S(1)}, u32[]{:S(2)}, u32[]{:S(2)}) collective-permute-start(bf16[8,1024]{1,0:T(8,128)(2,1)S(1)} %reduce_sum.12.own_ref), channel_id=1, source_target_pairs={{0,2},{2,0},{1,3},{3,1},{4,6},{6,4},{5,7},{7,5},{8,10},{10,8},{9,1... | collective-permute-start | bytes 49160 | tf_op jit(solution)/shard_map/ppermute | solution.py:607
  76.0 1.0 %finish.1 = (bf16[192,512]{1,0:T(8,128)(2,1)}, f32[8,128]{1,0:T(8,128)S(1)}) custom-call(bf16[192,512]{1,0:T(8,128)(2,1)S(1)} %bitcast.12, f32[192,512]{1,0:T(8,128)S(1)} %get-tuple-element.71.own_ref, bf16[2,192,512]{2,1,0:T(8,128)(2,1)S(1)} %collective-permute-done.8.recv_core_ref, bf16[192,512]{1,0:T(8,128)(2,1)S(1)} %collective-permute-done.9.from_x_ref, ...), custom_call_target="tpu_custom_call" | custom-call | flops 1000000 | bytes 4000000 | tf_op jit(solution)/shard_map/finish/pallas_call | solution.py:509
  77.4 0.7 final.1
  (39 shorter events, 2.0 us)
Async XLA Ops:
  0.6 10.1 %collective-permute-start.1 = (s32[1,3]{1,0:T(1,128)}, s32[1,3]{1,0:T(1,128)S(1)}, u32[]{:S(2)}, u32[]{:S(2)}) collective-permute-start(s32[1,3]{1,0:T(1,128)} %bitcast.15), channel_id=1, source_target_pairs={{0,2},{2,0},{1,3},{3,1},{4,6},{6,4},{5,7},{7,5},{8,10},{10,8},{9,1... | collective-permute-start | bytes 44 | tf_op jit(solution)/shard_map/ppermute | solution.py:570
  2.8 10.0 %collective-permute-start = (s32[1,3]{1,0:T(1,128)}, s32[1,3]{1,0:T(1,128)S(1)}, u32[]{:S(2)}, u32[]{:S(2)}) collective-permute-start(s32[1,3]{1,0:T(1,128)} %bitcast.16), channel_id=1, source_target_pairs={{0,1},{1,0},{2,3},{3,2},{4,5},{5,4},{6,7},{7,6},{8,9},{9,8},{10,11... | collective-permute-start | bytes 44 | tf_op jit(solution)/shard_map/ppermute | solution.py:562
  4.1 7.7 %collective-permute-start.5 = (bf16[192,512]{1,0:T(8,128)(2,1)}, bf16[192,512]{1,0:T(8,128)(2,1)S(1)}, u32[]{:S(2)}, u32[]{:S(2)}) collective-permute-start(bf16[192,512]{1,0:T(8,128)(2,1)} %bitcast.8), channel_id=1, source_target_pairs={{0,1},{1,0},{2,3},{3,2},{4,5},{5,4},{6,7},{7,6},{8,9},{9,8},{10,11... | collective-permute-start | bytes 589832 | tf_op jit(solution)/shard_map/ppermute | solution.py:562
  4.2 7.5 %collective-permute-start.3 = (bf16[192,512]{1,0:T(8,128)(2,1)}, bf16[192,512]{1,0:T(8,128)(2,1)S(1)}, u32[]{:S(2)}, u32[]{:S(2)}) collective-permute-start(bf16[192,512]{1,0:T(8,128)(2,1)} %bitcast.9), channel_id=1, source_target_pairs={{0,2},{2,0},{1,3},{3,1},{4,6},{6,4},{5,7},{7,5},{8,10},{10,8},{9,1... | collective-permute-start | bytes 589832 | tf_op jit(solution)/shard_map/ppermute | solution.py:568
  5.7 1.0 %copy-start = (bf16[3,64,512]{2,1,0:T(8,128)(2,1)S(1)}, bf16[3,64,512]{2,1,0:T(8,128)(2,1)}, u32[]{:S(2)}) copy-start(bf16[3,64,512]{2,1,0:T(8,128)(2,1)} %param.7) | copy-start | bytes 589828
  6.7 1.4 %copy-start.2 = (bf16[512,1536]{1,0:T(8,128)(2,1)S(1)}, bf16[512,1536]{1,0:T(8,128)(2,1)}, u32[]{:S(2)}) copy-start(bf16[512,1536]{1,0:T(8,128)(2,1)} %w_qkv_ref.7) | copy-start | bytes 4718596
  8.1 1.5 %copy-start.5 = (bf16[1024,512]{1,0:T(8,128)(2,1)S(1)}, bf16[1024,512]{1,0:T(8,128)(2,1)}, u32[]{:S(2)}) copy-start(bf16[1024,512]{1,0:T(8,128)(2,1)} %w_down_ref.3) | copy-start | bytes 3145732
  8.1 1.5 %copy-start.7 = (bf16[3,64,512]{2,1,0:T(8,128)(2,1)S(1)}, bf16[3,64,512]{2,1,0:T(8,128)(2,1)}, u32[]{:S(2)}) copy-start(bf16[3,64,512]{2,1,0:T(8,128)(2,1)} %param.13) | copy-start | bytes 589828
  8.1 1.5 %copy-start.8 = (s32[3,1]{0,1:T(1,128)S(1)}, s32[3,1]{0,1:T(1,128)}, u32[]{:S(2)}) copy-start(s32[3,1]{0,1:T(1,128)} %param.8) | copy-start | bytes 40
  9.6 2.2 %copy-start.3 = (bf16[512,1536]{1,0:T(8,128)(2,1)S(1)}, bf16[512,1536]{1,0:T(8,128)(2,1)}, u32[]{:S(2)}) copy-start(bf16[512,1536]{1,0:T(8,128)(2,1)} %w_qkv_ref.7) | copy-start | bytes 4718596
  10.7 2.4 %copy-start.1 = (bf16[3,64,512]{2,1,0:T(8,128)(2,1)S(1)}, bf16[3,64,512]{2,1,0:T(8,128)(2,1)}, u32[]{:S(2)}) copy-start(bf16[3,64,512]{2,1,0:T(8,128)(2,1)} %param.7) | copy-start | bytes 589828
  10.7 2.4 %copy-start.4 = (bf16[512,1024]{1,0:T(8,128)(2,1)S(1)}, bf16[512,1024]{1,0:T(8,128)(2,1)}, u32[]{:S(2)}) copy-start(bf16[512,1024]{1,0:T(8,128)(2,1)} %w_up_ref.1) | copy-start | bytes 3145732
  10.7 2.4 %copy-start.6 = (bf16[512,512]{1,0:T(8,128)(2,1)S(1)}, bf16[512,512]{1,0:T(8,128)(2,1)}, u32[]{:S(2)}) copy-start(bf16[512,512]{1,0:T(8,128)(2,1)} %w_out_ref.1) | copy-start | bytes 1572868
  10.7 2.0 %collective-permute-start.2 = (s32[1,3]{1,0:T(1,128)S(1)}, s32[1,3]{1,0:T(1,128)S(1)}, u32[]{:S(2)}, u32[]{:S(2)}) collective-permute-start(s32[1,3]{1,0:T(1,128)S(1)} %collective-permute-done.1.count2_ref), channel_id=1, source_target_pairs={{0,1},{1,0},{2,3},{3,2},{4,5},{5,4},{6,7},{7,6},{8,9},{9,8},{10,11... | collective-permute-start | bytes 44 | tf_op jit(solution)/shard_map/ppermute | solution.py:562
  11.6 1.4 %collective-permute-start.4 = (bf16[192,512]{1,0:T(8,128)(2,1)S(1)}, bf16[192,512]{1,0:T(8,128)(2,1)S(1)}, u32[]{:S(2)}, u32[]{:S(2)}) collective-permute-start(bf16[192,512]{1,0:T(8,128)(2,1)S(1)} %collective-permute-done.3.tok2_ref), channel_id=1, source_target_pairs={{0,1},{1,0},{2,3},{3,2},{4,5},{5,4},{6,7},{7,6},{8,9},{9,8},{10,11... | collective-permute-start | bytes 589832 | tf_op jit(solution)/shard_map/ppermute | solution.py:562
  13.1 4.8 %copy-start.10 = (bf16[192,512]{1,0:T(8,128)(2,1)S(1)}, bf16[192,512]{1,0:T(8,128)(2,1)}, u32[]{:S(2)}) copy-start(bf16[192,512]{1,0:T(8,128)(2,1)} %copy-done.9) | copy-start | bytes 589828
  17.7 5.2 %collective-permute-start.6 = (bf16[16,64,640]{2,1,0:T(8,128)(2,1)S(1)}, bf16[16,64,640]{2,1,0:T(8,128)(2,1)S(1)}, u32[]{:S(2)}, u32[]{:S(2)}) collective-permute-start(bf16[16,64,640]{2,1,0:T(8,128)(2,1)S(1)} %get-tuple-element.73), channel_id=1, source_target_pairs={{0,1},{1,0},{2,3},{3,2},{4,5},{5,4},{6,7},{7,6},{8,9},{9,8},{10,11... | collective-permute-start | bytes 3932168 | tf_op jit(solution)/shard_map/ppermute | solution.py:562
  20.4 2.6 %collective-permute-start.7 = (bf16[16,64,384]{2,1,0:T(8,128)(2,1)S(1)}, bf16[16,64,384]{2,1,0:T(8,128)(2,1)S(1)}, u32[]{:S(2)}, u32[]{:S(2)}) collective-permute-start(bf16[16,64,384]{2,1,0:T(8,128)(2,1)S(1)} %get-tuple-element.75), channel_id=1, source_target_pairs={{0,1},{1,0},{2,3},{3,2},{4,5},{5,4},{6,7},{7,6},{8,9},{9,8},{10,11... | collective-permute-start | bytes 2359304 | tf_op jit(solution)/shard_map/ppermute | solution.py:562
  55.8 8.8 %collective-permute-start.8 = (bf16[2,192,512]{2,1,0:T(8,128)(2,1)S(1)}, bf16[2,192,512]{2,1,0:T(8,128)(2,1)S(1)}, u32[]{:S(2)}, u32[]{:S(2)}) collective-permute-start(bf16[2,192,512]{2,1,0:T(8,128)(2,1)S(1)} %get-tuple-element.78), channel_id=1, source_target_pairs={{0,1},{1,0},{2,3},{3,2},{4,5},{5,4},{6,7},{7,6},{8,9},{9,8},{10,11... | collective-permute-start | bytes 1179656 | tf_op jit(solution)/shard_map/ppermute | solution.py:562
  57.1 15.7 %all-to-all-start.1 = ((bf16[8,8,1024]{2,1,0:T(8,128)(2,1)}), bf16[8,8,1024]{2,1,0:T(8,128)(2,1)S(1)}, u32[]{:S(2)}, u32[]{:S(2)}) async-start(bf16[8,8,1024]{2,1,0:T(8,128)(2,1)} %bitcast.7), calls=%async_computation.1 | async-start | bytes 262144 | tf_op jit(solution)/shard_map/all_to_all | solution.py:605
  64.7 11.3 %collective-permute-start.9 = (bf16[192,512]{1,0:T(8,128)(2,1)S(1)}, bf16[192,512]{1,0:T(8,128)(2,1)S(1)}, u32[]{:S(2)}, u32[]{:S(2)}) collective-permute-start(bf16[192,512]{1,0:T(8,128)(2,1)S(1)} %add_x.1), channel_id=1, source_target_pairs={{0,2},{2,0},{1,3},{3,1},{4,6},{6,4},{5,7},{7,5},{8,10},{10,8},{9,1... | collective-permute-start | bytes 589832 | tf_op jit(solution)/shard_map/ppermute | solution.py:603
  72.8 4.2 %collective-permute-start.12 = (bf16[8,1024]{1,0:T(8,128)(2,1)S(1)}, bf16[8,1024]{1,0:T(8,128)(2,1)S(1)}, u32[]{:S(2)}, u32[]{:S(2)}) collective-permute-start(bf16[8,1024]{1,0:T(8,128)(2,1)S(1)} %reduce_sum.12.own_ref), channel_id=1, source_target_pairs={{0,3},{3,0},{1,2},{2,1},{4,7},{7,4},{5,6},{6,5},{8,11},{11,8},{9,1... | collective-permute-start | bytes 49160 | tf_op jit(solution)/shard_map/ppermute | solution.py:607
  74.8 2.6 %collective-permute-start.11 = (bf16[8,1024]{1,0:T(8,128)(2,1)S(1)}, bf16[8,1024]{1,0:T(8,128)(2,1)S(1)}, u32[]{:S(2)}, u32[]{:S(2)}) collective-permute-start(bf16[8,1024]{1,0:T(8,128)(2,1)S(1)} %reduce_sum.12.own_ref), channel_id=1, source_target_pairs={{0,2},{2,0},{1,3},{3,1},{4,6},{6,4},{5,7},{7,5},{8,10},{10,8},{9,1... | collective-permute-start | bytes 49160 | tf_op jit(solution)/shard_map/ppermute | solution.py:607
  76.0 1.4 %collective-permute-start.10 = (bf16[8,1024]{1,0:T(8,128)(2,1)S(1)}, bf16[8,1024]{1,0:T(8,128)(2,1)S(1)}, u32[]{:S(2)}, u32[]{:S(2)}) collective-permute-start(bf16[8,1024]{1,0:T(8,128)(2,1)S(1)} %reduce_sum.12.own_ref), channel_id=1, source_target_pairs={{0,1},{1,0},{2,3},{3,2},{4,5},{5,4},{6,7},{7,6},{8,9},{9,8},{10,11... | collective-permute-start | bytes 49160 | tf_op jit(solution)/shard_map/ppermute | solution.py:607
  (1 other events, 0.7 us)

commit v6 on v5

--- a/solution.py
+++ b/solution.py
@@ -32,7 +32,7 @@
 CORE = [(0, 1), (1, 0), (2, 3), (3, 2)]
 X_LO = [(0, 2), (2, 0), (1, 3), (3, 1)]
 DIAGONAL = [(0, 3), (3, 0), (1, 2), (2, 1)]
-Z_ORDER = (0, 7, 1, 6, 2, 5, 3, 4)
+Z_ORDER = (4, 3, 5, 2, 6, 1, 7, 0)
 Z_GROUPS = [[lat_index(z, y, x) for z in Z_ORDER] for y in range(4) for x in range(2)]
 PLANE_GROUPS = [
     [

time: 78.3 us -> 75.4 us (0.963)
  waiting for transfers between devices: 8.72 us -> 4.7 us
  starting transfers between devices: 19.3 us -> 20.4 us
    all_to_all x1, waiting for transfers between devices: 7.67 us -> 3.86 us  [local(): lax.all_to_all(plane.reshape(8, 8, 1024), 'lat', 0, 0, axis_index_groups=...]
    all_to_all x1, starting transfers between devices: 7.55 us -> 9.59 us  [local(): lax.all_to_all(plane.reshape(8, 8, 1024), 'lat', 0, 0, axis_index_groups=...]
    ppermute x3, starting transfers between devices: 3.15 us -> 2.23 us  [local(): lax.ppermute(column, 'lon', table)]
  transfers between devices with their start and end apart: 14 -> 14, of which waited for: 4 -> 4; matrix products, arithmetic and copies ran while one was open for 0% -> 0% of each run, Pallas kernels for 10% -> 11%
where the time goes in v6:
time: 75.4 us; the launch traced here: 75.2 us
  blocking collectives  31.4 us (42%)
  starting transfers between devices  20.4 us (27%)
  Pallas kernels  14.8 us (20%)
  waiting for transfers between devices  4.7 us (6%)
  local copies, waits for them, and re-layouts  3.08 us (4%)
  between operations  0.77 us (1%)
    all_to_all x1, blocking collectives, local(): lax.all_to_all(joined, ('lat', 'lon'), 0, 0, axis_index_groups=PLANE_GROU...  31.4 us
    all_to_all x1, starting transfers between devices, local(): lax.all_to_all(plane.reshape(8, 8, 1024), 'lat', 0, 0, axis_index_groups=...  9.59 us
    pallas_call x1, Pallas kernels, run_front(): pl.pallas_call(front_kernel, out_shape=outs, in_specs=smem(5) + vmem(7 +...  4.64 us
    ppermute x7, starting transfers between devices, swap(): return lax.ppermute(values, 'lon', CORE)  4.49 us
    all_to_all x1, waiting for transfers between devices, local(): lax.all_to_all(plane.reshape(8, 8, 1024), 'lat', 0, 0, axis_index_groups=...  3.86 us
    unnamed x22, local copies, waits for them, and re-layouts  3.08 us
    pallas_call x1, Pallas kernels, run_back(): pl.pallas_call(back_kernel, out_shape=outs, in_specs=smem(1) + vmem(len(s...  2.51 us
    ppermute x3, starting transfers between devices, local(): lax.ppermute(column, 'lon', table)  2.23 us
  transfers between devices with their start and end apart: 14, of which 4 were waited for; matrix products, arithmetic and copies ran while one was open for 0% of the time, Pallas kernels for 11%

profile of v6, /device:TPU:1, one launch (start us, length us, event | category | flops | bytes accessed | tf_op | source)
XLA Modules:
  0.0 75.2 jit_solution(2448117316535260113)
XLA Ops:
  0.6 2.1 %collective-permute-start.1 = (s32[1,3]{1,0:T(1,128)}, s32[1,3]{1,0:T(1,128)S(1)}, u32[]{:S(2)}, u32[]{:S(2)}) collective-permute-start(s32[1,3]{1,0:T(1,128)} %bitcast.15), channel_id=1, source_target_pairs={{0,2},{2,0},{1,3},{3,1},{4,6},{6,4},{5,7},{7,5},{8,10},{10,8},{9,1... | collective-permute-start | bytes 44 | tf_op jit(solution)/shard_map/ppermute | solution.py:570
  2.8 1.3 %collective-permute-start = (s32[1,3]{1,0:T(1,128)}, s32[1,3]{1,0:T(1,128)S(1)}, u32[]{:S(2)}, u32[]{:S(2)}) collective-permute-start(s32[1,3]{1,0:T(1,128)} %bitcast.16), channel_id=1, source_target_pairs={{0,1},{1,0},{2,3},{3,2},{4,5},{5,4},{6,7},{7,6},{8,9},{9,8},{10,11... | collective-permute-start | bytes 44 | tf_op jit(solution)/shard_map/ppermute | solution.py:562
  4.2 1.5 %collective-permute-start.3 = (bf16[192,512]{1,0:T(8,128)(2,1)}, bf16[192,512]{1,0:T(8,128)(2,1)S(1)}, u32[]{:S(2)}, u32[]{:S(2)}) collective-permute-start(bf16[192,512]{1,0:T(8,128)(2,1)} %bitcast.9), channel_id=1, source_target_pairs={{0,2},{2,0},{1,3},{3,1},{4,6},{6,4},{5,7},{7,5},{8,10},{10,8},{9,1... | collective-permute-start | bytes 589832 | tf_op jit(solution)/shard_map/ppermute | solution.py:568
  5.7 1.0 %copy-done = bf16[3,64,512]{2,1,0:T(8,128)(2,1)S(1)} copy-done((bf16[3,64,512]{2,1,0:T(8,128)(2,1)S(1)}, bf16[3,64,512]{2,1,0:T(8,128)(2,1)}, u32[]{:S(2)}) %copy-start) | copy-done | bytes 196632
  6.7 1.4 %copy-done.2 = bf16[512,1536]{1,0:T(8,128)(2,1)S(1)} copy-done((bf16[512,1536]{1,0:T(8,128)(2,1)S(1)}, bf16[512,1536]{1,0:T(8,128)(2,1)}, u32[]{:S(2)}) %copy-start.2) | copy-done | bytes 1572888
  8.1 0.8 %near.1 = (bf16[192,512]{1,0:T(8,128)(2,1)S(1)}, bf16[192,512]{1,0:T(8,128)(2,1)S(1)}, bf16[192,512]{1,0:T(8,128)(2,1)S(1)}, bf16[192,512]{1,0:T(8,128)(2,1)S(1)...) custom-call(bf16[192,512]{1,0:T(8,128)(2,1)S(1)} %bitcast.10, bf16[512,1536]{1,0:T(8,128)(2,1)S(1)} %copy-done.2), custom_call_target="tpu_custom_call" | custom-call | flops 2500000000 | bytes 4000000 | tf_op jit(solution)/shard_map/near/pallas_call | solution.py:408
  9.0 0.7 copy-done.9
  9.6 1.0 %active.1.grad_active_ref = bf16[192,1024]{1,0:T(8,128)(2,1)S(1)} custom-call(s32[1,3]{1,0:T(1,128)S(1)} %bitcast.17, bf16[1024,512]{1,0:T(8,128)(2,1)S(1)} %copy-done.5, bf16[192,512]{1,0:T(8,128)(2,1)S(1)} %bitcast.13), custom_call_target="tpu_custom_call" | custom-call | flops 2500000000 | bytes 2000000 | tf_op jit(solution)/shard_map/active/pallas_call | solution.py:420
  10.7 0.9 %collective-permute-start.2 = (s32[1,3]{1,0:T(1,128)S(1)}, s32[1,3]{1,0:T(1,128)S(1)}, u32[]{:S(2)}, u32[]{:S(2)}) collective-permute-start(s32[1,3]{1,0:T(1,128)S(1)} %collective-permute-done.1.count2_ref), channel_id=1, source_target_pairs={{0,1},{1,0},{2,3},{3,2},{4,5},{5,4},{6,7},{7,6},{8,9},{9,8},{10,11... | collective-permute-start | bytes 44 | tf_op jit(solution)/shard_map/ppermute | solution.py:562
  11.8 1.0 %pair.1 = (bf16[192,512]{1,0:T(8,128)(2,1)S(1)}, bf16[192,512]{1,0:T(8,128)(2,1)S(1)}, bf16[192,512]{1,0:T(8,128)(2,1)S(1)}, bf16[192,512]{1,0:T(8,128)(2,1)S(1)...) custom-call(bf16[192,512]{1,0:T(8,128)(2,1)S(1)} %collective-permute, ...), custom_call_target="tpu_custom_call" | custom-call | flops 20000000000 | bytes 2000000 | tf_op jit(solution)/shard_map/pair/pallas_call | solution.py:433
  13.1 4.6 %front.1 = (bf16[192,512]{1,0:T(8,128)(2,1)}, bf16[16,64,640]{2,1,0:T(8,128)(2,1)S(1)}, bf16[16,64,640]{2,1,0:T(8,128)(2,1)S(1)}, f32[192,512]{1,0:T(8,128)S(1)}...) custom-call(s32[1]{0:T(128)} %bitcast.core_ref, ...), custom_call_target="tpu_custom_call" | custom-call | flops 5000000000 | bytes 12000000 | tf_op jit(solution)/shard_map/front/pallas_call | solution.py:457
  17.9 2.5 %back.1 = (bf16[16,64,384]{2,1,0:T(8,128)(2,1)S(1)}, bf16[4,192,128]{2,1,0:T(8,128)(2,1)S(1)}, bf16[4,768,128]{2,1,0:T(8,128)(2,1)S(1)}, bf16[4,768,128]{2,1,0:T(8,128)(2,1)S(1)}) custom-call(s32[1]{0:T(128)} %bitcast.core_ref, bf16[192,512]{1,0:T(8,128)(2,1)S(1)} %get-tuple-element.47.query_ref, bf16[192,512]{1,0:T(8,128)(2,1)S(1)} %get-tuple-element.55.inv_q_ref, ...), custom_call_target="tpu_custom_call" | custom-call | flops 6000000000 | bytes 12000000 | tf_op jit(solution)/shard_map/back/pallas_call | solution.py:483
  20.4 0.6 collective-permute-start.7
  21.0 1.6 %push.1 = (bf16[16,64,384]{2,1,0:T(8,128)(2,1)S(1)}, bf16[2,192,512]{2,1,0:T(8,128)(2,1)S(1)}, bf16[192,512]{1,0:T(8,128)(2,1)S(1)}, f32[192,512]{1,0:T(8,128)S(1)}) custom-call(s32[1]{0:T(128)} %bitcast.core_ref, bf16[512,1536]{1,0:T(8,128)(2,1)S(1)} %copy-done.3, bf16[4,192,128]{2,1,0:T(8,128)(2,1)S(1)} %get-tuple-element.68.gq_ref, ...), custom_call_target="tpu_custom_call" | custom-call | flops 2000000000 | bytes 4000000 | tf_op jit(solution)/shard_map/push/pallas_call | solution.py:497
  23.0 0.5 join.1
  23.5 31.4 %all_to_all.10.parts_ref = bf16[16,64,1024]{2,1,0:T(8,128)(2,1)S(1)} all-to-all(bf16[16,64,1024]{2,1,0:T(8,128)(2,1)S(1)} %join.1), channel_id=1, replica_groups={{30,28,26,24,22,20,18,16,14,12,10,8,6,4,2,0},{31,29,27,25,23,21,19,17,1..., dimensions={0} | all-to-all | bytes 4194304 | tf_op jit(solution)/shard_map/all_to_all | solution.py:600
  54.9 0.9 %plane_sum.1 = bf16[64,1024]{1,0:T(8,128)(2,1)} custom-call(bf16[16,64,1024]{2,1,0:T(8,128)(2,1)S(1)} %all_to_all.10.parts_ref), custom_call_target="tpu_custom_call" | custom-call | flops 1000000 | bytes 4000000 | tf_op jit(solution)/shard_map/plane_sum/pallas_call | solution.py:509
  55.8 1.3 %collective-permute-start.8 = (bf16[2,192,512]{2,1,0:T(8,128)(2,1)S(1)}, bf16[2,192,512]{2,1,0:T(8,128)(2,1)S(1)}, u32[]{:S(2)}, u32[]{:S(2)}) collective-permute-start(bf16[2,192,512]{2,1,0:T(8,128)(2,1)S(1)} %get-tuple-element.78), channel_id=1, source_target_pairs={{0,1},{1,0},{2,3},{3,2},{4,5},{5,4},{6,7},{7,6},{8,9},{9,8},{10,11... | collective-permute-start | bytes 1179656 | tf_op jit(solution)/shard_map/ppermute | solution.py:562
  57.1 9.6 %all-to-all-start.1 = ((bf16[8,8,1024]{2,1,0:T(8,128)(2,1)}), bf16[8,8,1024]{2,1,0:T(8,128)(2,1)S(1)}, u32[]{:S(2)}, u32[]{:S(2)}) async-start(bf16[8,8,1024]{2,1,0:T(8,128)(2,1)} %bitcast.7), calls=%async_computation.1 | async-start | bytes 262144 | tf_op jit(solution)/shard_map/all_to_all | solution.py:605
  67.1 3.9 %all-to-all-done.1 = bf16[8,8,1024]{2,1,0:T(8,128)(2,1)S(1)} async-done(((bf16[8,8,1024]{2,1,0:T(8,128)(2,1)}), bf16[8,8,1024]{2,1,0:T(8,128)(2,1)S(1)}, u32[]{:S(2)}, u32[]{:S(2)}) %all-to-all-start.1) | async-done | bytes 131104 | tf_op jit(solution)/shard_map/all_to_all | solution.py:605
  71.0 0.8 %collective-permute-start.12 = (bf16[8,1024]{1,0:T(8,128)(2,1)S(1)}, bf16[8,1024]{1,0:T(8,128)(2,1)S(1)}, u32[]{:S(2)}, u32[]{:S(2)}) collective-permute-start(bf16[8,1024]{1,0:T(8,128)(2,1)S(1)} %reduce_sum.12.own_ref), channel_id=1, source_target_pairs={{0,3},{3,0},{1,2},{2,1},{4,7},{7,4},{5,6},{6,5},{8,11},{11,8},{9,1... | collective-permute-start | bytes 49160 | tf_op jit(solution)/shard_map/ppermute | solution.py:607
  71.9 1.1 %collective-permute-start.11 = (bf16[8,1024]{1,0:T(8,128)(2,1)S(1)}, bf16[8,1024]{1,0:T(8,128)(2,1)S(1)}, u32[]{:S(2)}, u32[]{:S(2)}) collective-permute-start(bf16[8,1024]{1,0:T(8,128)(2,1)S(1)} %reduce_sum.12.own_ref), channel_id=1, source_target_pairs={{0,2},{2,0},{1,3},{3,1},{4,6},{6,4},{5,7},{7,5},{8,10},{10,8},{9,1... | collective-permute-start | bytes 49160 | tf_op jit(solution)/shard_map/ppermute | solution.py:607
  73.3 1.0 %finish.1 = (bf16[192,512]{1,0:T(8,128)(2,1)}, f32[8,128]{1,0:T(8,128)S(1)}) custom-call(bf16[192,512]{1,0:T(8,128)(2,1)S(1)} %bitcast.12, f32[192,512]{1,0:T(8,128)S(1)} %get-tuple-element.71.own_ref, bf16[2,192,512]{2,1,0:T(8,128)(2,1)S(1)} %collective-permute-done.8.recv_core_ref, bf16[192,512]{1,0:T(8,128)(2,1)S(1)} %collective-permute-done.9.from_x_ref, ...), custom_call_target="tpu_custom_call" | custom-call | flops 1000000 | bytes 4000000 | tf_op jit(solution)/shard_map/finish/pallas_call | solution.py:509
  74.5 0.7 final.1
  (39 shorter events, 2.0 us)
Async XLA Ops:
  0.6 10.1 %collective-permute-start.1 = (s32[1,3]{1,0:T(1,128)}, s32[1,3]{1,0:T(1,128)S(1)}, u32[]{:S(2)}, u32[]{:S(2)}) collective-permute-start(s32[1,3]{1,0:T(1,128)} %bitcast.15), channel_id=1, source_target_pairs={{0,2},{2,0},{1,3},{3,1},{4,6},{6,4},{5,7},{7,5},{8,10},{10,8},{9,1... | collective-permute-start | bytes 44 | tf_op jit(solution)/shard_map/ppermute | solution.py:570
  2.8 10.0 %collective-permute-start = (s32[1,3]{1,0:T(1,128)}, s32[1,3]{1,0:T(1,128)S(1)}, u32[]{:S(2)}, u32[]{:S(2)}) collective-permute-start(s32[1,3]{1,0:T(1,128)} %bitcast.16), channel_id=1, source_target_pairs={{0,1},{1,0},{2,3},{3,2},{4,5},{5,4},{6,7},{7,6},{8,9},{9,8},{10,11... | collective-permute-start | bytes 44 | tf_op jit(solution)/shard_map/ppermute | solution.py:562
  4.1 7.7 %collective-permute-start.5 = (bf16[192,512]{1,0:T(8,128)(2,1)}, bf16[192,512]{1,0:T(8,128)(2,1)S(1)}, u32[]{:S(2)}, u32[]{:S(2)}) collective-permute-start(bf16[192,512]{1,0:T(8,128)(2,1)} %bitcast.8), channel_id=1, source_target_pairs={{0,1},{1,0},{2,3},{3,2},{4,5},{5,4},{6,7},{7,6},{8,9},{9,8},{10,11... | collective-permute-start | bytes 589832 | tf_op jit(solution)/shard_map/ppermute | solution.py:562
  4.2 7.5 %collective-permute-start.3 = (bf16[192,512]{1,0:T(8,128)(2,1)}, bf16[192,512]{1,0:T(8,128)(2,1)S(1)}, u32[]{:S(2)}, u32[]{:S(2)}) collective-permute-start(bf16[192,512]{1,0:T(8,128)(2,1)} %bitcast.9), channel_id=1, source_target_pairs={{0,2},{2,0},{1,3},{3,1},{4,6},{6,4},{5,7},{7,5},{8,10},{10,8},{9,1... | collective-permute-start | bytes 589832 | tf_op jit(solution)/shard_map/ppermute | solution.py:568
  5.7 1.0 %copy-start = (bf16[3,64,512]{2,1,0:T(8,128)(2,1)S(1)}, bf16[3,64,512]{2,1,0:T(8,128)(2,1)}, u32[]{:S(2)}) copy-start(bf16[3,64,512]{2,1,0:T(8,128)(2,1)} %param.7) | copy-start | bytes 589828
  6.7 1.4 %copy-start.2 = (bf16[512,1536]{1,0:T(8,128)(2,1)S(1)}, bf16[512,1536]{1,0:T(8,128)(2,1)}, u32[]{:S(2)}) copy-start(bf16[512,1536]{1,0:T(8,128)(2,1)} %w_qkv_ref.7) | copy-start | bytes 4718596
  8.1 1.5 %copy-start.5 = (bf16[1024,512]{1,0:T(8,128)(2,1)S(1)}, bf16[1024,512]{1,0:T(8,128)(2,1)}, u32[]{:S(2)}) copy-start(bf16[1024,512]{1,0:T(8,128)(2,1)} %w_down_ref.3) | copy-start | bytes 3145732
  8.1 1.5 %copy-start.7 = (bf16[3,64,512]{2,1,0:T(8,128)(2,1)S(1)}, bf16[3,64,512]{2,1,0:T(8,128)(2,1)}, u32[]{:S(2)}) copy-start(bf16[3,64,512]{2,1,0:T(8,128)(2,1)} %param.13) | copy-start | bytes 589828
  8.1 1.5 %copy-start.8 = (s32[3,1]{0,1:T(1,128)S(1)}, s32[3,1]{0,1:T(1,128)}, u32[]{:S(2)}) copy-start(s32[3,1]{0,1:T(1,128)} %param.8) | copy-start | bytes 40
  9.6 2.2 %copy-start.3 = (bf16[512,1536]{1,0:T(8,128)(2,1)S(1)}, bf16[512,1536]{1,0:T(8,128)(2,1)}, u32[]{:S(2)}) copy-start(bf16[512,1536]{1,0:T(8,128)(2,1)} %w_qkv_ref.7) | copy-start | bytes 4718596
  10.7 2.4 %copy-start.1 = (bf16[3,64,512]{2,1,0:T(8,128)(2,1)S(1)}, bf16[3,64,512]{2,1,0:T(8,128)(2,1)}, u32[]{:S(2)}) copy-start(bf16[3,64,512]{2,1,0:T(8,128)(2,1)} %param.7) | copy-start | bytes 589828
  10.7 2.4 %copy-start.4 = (bf16[512,1024]{1,0:T(8,128)(2,1)S(1)}, bf16[512,1024]{1,0:T(8,128)(2,1)}, u32[]{:S(2)}) copy-start(bf16[512,1024]{1,0:T(8,128)(2,1)} %w_up_ref.1) | copy-start | bytes 3145732
  10.7 2.4 %copy-start.6 = (bf16[512,512]{1,0:T(8,128)(2,1)S(1)}, bf16[512,512]{1,0:T(8,128)(2,1)}, u32[]{:S(2)}) copy-start(bf16[512,512]{1,0:T(8,128)(2,1)} %w_out_ref.1) | copy-start | bytes 1572868
  10.7 2.0 %collective-permute-start.2 = (s32[1,3]{1,0:T(1,128)S(1)}, s32[1,3]{1,0:T(1,128)S(1)}, u32[]{:S(2)}, u32[]{:S(2)}) collective-permute-start(s32[1,3]{1,0:T(1,128)S(1)} %collective-permute-done.1.count2_ref), channel_id=1, source_target_pairs={{0,1},{1,0},{2,3},{3,2},{4,5},{5,4},{6,7},{7,6},{8,9},{9,8},{10,11... | collective-permute-start | bytes 44 | tf_op jit(solution)/shard_map/ppermute | solution.py:562
  11.6 1.4 %collective-permute-start.4 = (bf16[192,512]{1,0:T(8,128)(2,1)S(1)}, bf16[192,512]{1,0:T(8,128)(2,1)S(1)}, u32[]{:S(2)}, u32[]{:S(2)}) collective-permute-start(bf16[192,512]{1,0:T(8,128)(2,1)S(1)} %collective-permute-done.3.tok2_ref), channel_id=1, source_target_pairs={{0,1},{1,0},{2,3},{3,2},{4,5},{5,4},{6,7},{7,6},{8,9},{9,8},{10,11... | collective-permute-start | bytes 589832 | tf_op jit(solution)/shard_map/ppermute | solution.py:562
  13.1 4.8 %copy-start.10 = (bf16[192,512]{1,0:T(8,128)(2,1)S(1)}, bf16[192,512]{1,0:T(8,128)(2,1)}, u32[]{:S(2)}) copy-start(bf16[192,512]{1,0:T(8,128)(2,1)} %copy-done.9) | copy-start | bytes 589828
  17.7 5.2 %collective-permute-start.6 = (bf16[16,64,640]{2,1,0:T(8,128)(2,1)S(1)}, bf16[16,64,640]{2,1,0:T(8,128)(2,1)S(1)}, u32[]{:S(2)}, u32[]{:S(2)}) collective-permute-start(bf16[16,64,640]{2,1,0:T(8,128)(2,1)S(1)} %get-tuple-element.73), channel_id=1, source_target_pairs={{0,1},{1,0},{2,3},{3,2},{4,5},{5,4},{6,7},{7,6},{8,9},{9,8},{10,11... | collective-permute-start | bytes 3932168 | tf_op jit(solution)/shard_map/ppermute | solution.py:562
  20.4 2.6 %collective-permute-start.7 = (bf16[16,64,384]{2,1,0:T(8,128)(2,1)S(1)}, bf16[16,64,384]{2,1,0:T(8,128)(2,1)S(1)}, u32[]{:S(2)}, u32[]{:S(2)}) collective-permute-start(bf16[16,64,384]{2,1,0:T(8,128)(2,1)S(1)} %get-tuple-element.75), channel_id=1, source_target_pairs={{0,1},{1,0},{2,3},{3,2},{4,5},{5,4},{6,7},{7,6},{8,9},{9,8},{10,11... | collective-permute-start | bytes 2359304 | tf_op jit(solution)/shard_map/ppermute | solution.py:562
  55.8 10.9 %collective-permute-start.8 = (bf16[2,192,512]{2,1,0:T(8,128)(2,1)S(1)}, bf16[2,192,512]{2,1,0:T(8,128)(2,1)S(1)}, u32[]{:S(2)}, u32[]{:S(2)}) collective-permute-start(bf16[2,192,512]{2,1,0:T(8,128)(2,1)S(1)} %get-tuple-element.78), channel_id=1, source_target_pairs={{0,1},{1,0},{2,3},{3,2},{4,5},{5,4},{6,7},{7,6},{8,9},{9,8},{10,11... | collective-permute-start | bytes 1179656 | tf_op jit(solution)/shard_map/ppermute | solution.py:562
  57.1 13.9 %all-to-all-start.1 = ((bf16[8,8,1024]{2,1,0:T(8,128)(2,1)}), bf16[8,8,1024]{2,1,0:T(8,128)(2,1)S(1)}, u32[]{:S(2)}, u32[]{:S(2)}) async-start(bf16[8,8,1024]{2,1,0:T(8,128)(2,1)} %bitcast.7), calls=%async_computation.1 | async-start | bytes 262144 | tf_op jit(solution)/shard_map/all_to_all | solution.py:605
  66.7 6.5 %collective-permute-start.9 = (bf16[192,512]{1,0:T(8,128)(2,1)S(1)}, bf16[192,512]{1,0:T(8,128)(2,1)S(1)}, u32[]{:S(2)}, u32[]{:S(2)}) collective-permute-start(bf16[192,512]{1,0:T(8,128)(2,1)S(1)} %add_x.1), channel_id=1, source_target_pairs={{0,2},{2,0},{1,3},{3,1},{4,6},{6,4},{5,7},{7,5},{8,10},{10,8},{9,1... | collective-permute-start | bytes 589832 | tf_op jit(solution)/shard_map/ppermute | solution.py:603
  71.0 3.4 %collective-permute-start.12 = (bf16[8,1024]{1,0:T(8,128)(2,1)S(1)}, bf16[8,1024]{1,0:T(8,128)(2,1)S(1)}, u32[]{:S(2)}, u32[]{:S(2)}) collective-permute-start(bf16[8,1024]{1,0:T(8,128)(2,1)S(1)} %reduce_sum.12.own_ref), channel_id=1, source_target_pairs={{0,3},{3,0},{1,2},{2,1},{4,7},{7,4},{5,6},{6,5},{8,11},{11,8},{9,1... | collective-permute-start | bytes 49160 | tf_op jit(solution)/shard_map/ppermute | solution.py:607
  71.9 2.6 %collective-permute-start.11 = (bf16[8,1024]{1,0:T(8,128)(2,1)S(1)}, bf16[8,1024]{1,0:T(8,128)(2,1)S(1)}, u32[]{:S(2)}, u32[]{:S(2)}) collective-permute-start(bf16[8,1024]{1,0:T(8,128)(2,1)S(1)} %reduce_sum.12.own_ref), channel_id=1, source_target_pairs={{0,2},{2,0},{1,3},{3,1},{4,6},{6,4},{5,7},{7,5},{8,10},{10,8},{9,1... | collective-permute-start | bytes 49160 | tf_op jit(solution)/shard_map/ppermute | solution.py:607
  73.0 1.5 %collective-permute-start.10 = (bf16[8,1024]{1,0:T(8,128)(2,1)S(1)}, bf16[8,1024]{1,0:T(8,128)(2,1)S(1)}, u32[]{:S(2)}, u32[]{:S(2)}) collective-permute-start(bf16[8,1024]{1,0:T(8,128)(2,1)S(1)} %reduce_sum.12.own_ref), channel_id=1, source_target_pairs={{0,1},{1,0},{2,3},{3,2},{4,5},{5,4},{6,7},{7,6},{8,9},{9,8},{10,11... | collective-permute-start | bytes 49160 | tf_op jit(solution)/shard_map/ppermute | solution.py:607
  (1 other events, 0.7 us)

commit v7 on v6

--- a/solution.py
+++ b/solution.py
@@ -34,13 +34,10 @@
 DIAGONAL = [(0, 3), (3, 0), (1, 2), (2, 1)]
 Z_ORDER = (4, 3, 5, 2, 6, 1, 7, 0)
 Z_GROUPS = [[lat_index(z, y, x) for z in Z_ORDER] for y in range(4) for x in range(2)]
+FOLDED = (2, 1, 3, 0)
+PLANE_ORDER = [y * 4 + x for y in FOLDED for x in FOLDED]
 PLANE_GROUPS = [
-    [
-        lat_index(z, y, x_hi) * 4 + x_lo * 2 + core
-        for y in reversed(range(4))
-        for x_hi in reversed(range(2))
-        for x_lo in reversed(range(2))
-    ]
+    [lat_index(z, at // 4, at % 4 // 2) * 4 + at % 2 * 2 + core for at in PLANE_ORDER]
     for z in range(8)
     for core in range(2)
 ]
@@ -104,7 +101,7 @@
     split = product.reshape(8, 8, 8, width)
     for place in range(8):
         piece = jnp.concatenate([split[z, place] for z in Z_ORDER], axis=0)
-        out_ref[15 - place * 2 - x_lo, :, column : column + width] = piece.astype(BF16)
+        out_ref[PLANE_ORDER.index(place * 2 + x_lo), :, column : column + width] = piece.astype(BF16)
 
 
 def rows_of(row, width=SECTOR):

time: 75.4 us -> 76 us (level)
  starting transfers between devices: 20.4 us -> 22.4 us
  blocking collectives: 31.4 us -> 30.2 us
    all_to_all x1, blocking collectives: 31.4 us -> 30.2 us  [local(): lax.all_to_all(joined, ('lat', 'lon'), 0, 0, axis_index_groups=PLANE_GROU...]
    ppermute x1, starting transfers between devices: 0.41 us -> 1.46 us  [local(): from_x = lax.ppermute(run_add_x(for_x, recv_core), 'lon', X_LO)]
    all_to_all x1, waiting for transfers between devices: 3.86 us -> 2.81 us  [local(): lax.all_to_all(plane.reshape(8, 8, 1024), 'lat', 0, 0, axis_index_groups=...]
    ppermute x3, waiting for transfers between devices: 0.23 us -> 1.07 us  [local(): lax.ppermute(column, 'lon', table)]
where the time goes in v7:
time: 76 us; the launch traced here: 75.7 us
  blocking collectives  30.2 us (40%)
  starting transfers between devices  22.4 us (29%)
  Pallas kernels  14.8 us (19%)
  waiting for transfers between devices  4.48 us (6%)
  local copies, waits for them, and re-layouts  3.08 us (4%)
  between operations  0.77 us (1%)
    all_to_all x1, blocking collectives, local(): lax.all_to_all(joined, ('lat', 'lon'), 0, 0, axis_index_groups=PLANE_GROU...  30.2 us
    all_to_all x1, starting transfers between devices, local(): lax.all_to_all(plane.reshape(8, 8, 1024), 'lat', 0, 0, axis_index_groups=...  10.2 us
    pallas_call x1, Pallas kernels, run_front(): pl.pallas_call(front_kernel, out_shape=outs, in_specs=smem(5) + vmem(7 +...  4.64 us
    ppermute x7, starting transfers between devices, swap(): return lax.ppermute(values, 'lon', CORE)  4.61 us
    unnamed x22, local copies, waits for them, and re-layouts  3.08 us
    all_to_all x1, waiting for transfers between devices, local(): lax.all_to_all(plane.reshape(8, 8, 1024), 'lat', 0, 0, axis_index_groups=...  2.81 us
    pallas_call x1, Pallas kernels, run_back(): pl.pallas_call(back_kernel, out_shape=outs, in_specs=smem(1) + vmem(len(s...  2.51 us
    ppermute x3, starting transfers between devices, local(): lax.ppermute(column, 'lon', table)  2.41 us
  transfers between devices with their start and end apart: 14, of which 4 were waited for; matrix products, arithmetic and copies ran while one was open for 0% of the time, Pallas kernels for 11%

profile of v7, /device:TPU:1, one launch (start us, length us, event | category | flops | bytes accessed | tf_op | source)
XLA Modules:
  0.0 75.7 jit_solution(11696820338034155085)
XLA Ops:
  0.6 2.1 %collective-permute-start.1 = (s32[1,3]{1,0:T(1,128)}, s32[1,3]{1,0:T(1,128)S(1)}, u32[]{:S(2)}, u32[]{:S(2)}) collective-permute-start(s32[1,3]{1,0:T(1,128)} %bitcast.15), channel_id=1, source_target_pairs={{0,2},{2,0},{1,3},{3,1},{4,6},{6,4},{5,7},{7,5},{8,10},{10,8},{9,1... | collective-permute-start | bytes 44 | tf_op jit(solution)/shard_map/ppermute | solution.py:567
  2.8 1.3 %collective-permute-start = (s32[1,3]{1,0:T(1,128)}, s32[1,3]{1,0:T(1,128)S(1)}, u32[]{:S(2)}, u32[]{:S(2)}) collective-permute-start(s32[1,3]{1,0:T(1,128)} %bitcast.16), channel_id=1, source_target_pairs={{0,1},{1,0},{2,3},{3,2},{4,5},{5,4},{6,7},{7,6},{8,9},{9,8},{10,11... | collective-permute-start | bytes 44 | tf_op jit(solution)/shard_map/ppermute | solution.py:559
  4.2 1.5 %collective-permute-start.3 = (bf16[192,512]{1,0:T(8,128)(2,1)}, bf16[192,512]{1,0:T(8,128)(2,1)S(1)}, u32[]{:S(2)}, u32[]{:S(2)}) collective-permute-start(bf16[192,512]{1,0:T(8,128)(2,1)} %bitcast.9), channel_id=1, source_target_pairs={{0,2},{2,0},{1,3},{3,1},{4,6},{6,4},{5,7},{7,5},{8,10},{10,8},{9,1... | collective-permute-start | bytes 589832 | tf_op jit(solution)/shard_map/ppermute | solution.py:565
  5.7 1.0 %copy-done = bf16[3,64,512]{2,1,0:T(8,128)(2,1)S(1)} copy-done((bf16[3,64,512]{2,1,0:T(8,128)(2,1)S(1)}, bf16[3,64,512]{2,1,0:T(8,128)(2,1)}, u32[]{:S(2)}) %copy-start) | copy-done | bytes 196632
  6.7 1.4 %copy-done.2 = bf16[512,1536]{1,0:T(8,128)(2,1)S(1)} copy-done((bf16[512,1536]{1,0:T(8,128)(2,1)S(1)}, bf16[512,1536]{1,0:T(8,128)(2,1)}, u32[]{:S(2)}) %copy-start.2) | copy-done | bytes 1572888
  8.1 0.8 %near.1 = (bf16[192,512]{1,0:T(8,128)(2,1)S(1)}, bf16[192,512]{1,0:T(8,128)(2,1)S(1)}, bf16[192,512]{1,0:T(8,128)(2,1)S(1)}, bf16[192,512]{1,0:T(8,128)(2,1)S(1)...) custom-call(bf16[192,512]{1,0:T(8,128)(2,1)S(1)} %bitcast.10, bf16[512,1536]{1,0:T(8,128)(2,1)S(1)} %copy-done.2), custom_call_target="tpu_custom_call" | custom-call | flops 2500000000 | bytes 4000000 | tf_op jit(solution)/shard_map/near/pallas_call | solution.py:405
  9.0 0.7 copy-done.9
  9.6 1.0 %active.1.grad_active_ref = bf16[192,1024]{1,0:T(8,128)(2,1)S(1)} custom-call(s32[1,3]{1,0:T(1,128)S(1)} %bitcast.17, bf16[1024,512]{1,0:T(8,128)(2,1)S(1)} %copy-done.5, bf16[192,512]{1,0:T(8,128)(2,1)S(1)} %bitcast.13), custom_call_target="tpu_custom_call" | custom-call | flops 2500000000 | bytes 2000000 | tf_op jit(solution)/shard_map/active/pallas_call | solution.py:417
  10.7 0.9 %collective-permute-start.2 = (s32[1,3]{1,0:T(1,128)S(1)}, s32[1,3]{1,0:T(1,128)S(1)}, u32[]{:S(2)}, u32[]{:S(2)}) collective-permute-start(s32[1,3]{1,0:T(1,128)S(1)} %collective-permute-done.1.count2_ref), channel_id=1, source_target_pairs={{0,1},{1,0},{2,3},{3,2},{4,5},{5,4},{6,7},{7,6},{8,9},{9,8},{10,11... | collective-permute-start | bytes 44 | tf_op jit(solution)/shard_map/ppermute | solution.py:559
  11.8 1.0 %pair.1 = (bf16[192,512]{1,0:T(8,128)(2,1)S(1)}, bf16[192,512]{1,0:T(8,128)(2,1)S(1)}, bf16[192,512]{1,0:T(8,128)(2,1)S(1)}, bf16[192,512]{1,0:T(8,128)(2,1)S(1)...) custom-call(bf16[192,512]{1,0:T(8,128)(2,1)S(1)} %collective-permute, ...), custom_call_target="tpu_custom_call" | custom-call | flops 20000000000 | bytes 2000000 | tf_op jit(solution)/shard_map/pair/pallas_call | solution.py:430
  13.1 4.6 %front.1 = (bf16[192,512]{1,0:T(8,128)(2,1)}, bf16[16,64,640]{2,1,0:T(8,128)(2,1)S(1)}, bf16[16,64,640]{2,1,0:T(8,128)(2,1)S(1)}, f32[192,512]{1,0:T(8,128)S(1)}...) custom-call(s32[1]{0:T(128)} %bitcast.core_ref, ...), custom_call_target="tpu_custom_call" | custom-call | flops 5000000000 | bytes 12000000 | tf_op jit(solution)/shard_map/front/pallas_call | solution.py:454
  17.9 2.5 %back.1 = (bf16[16,64,384]{2,1,0:T(8,128)(2,1)S(1)}, bf16[4,192,128]{2,1,0:T(8,128)(2,1)S(1)}, bf16[4,768,128]{2,1,0:T(8,128)(2,1)S(1)}, bf16[4,768,128]{2,1,0:T(8,128)(2,1)S(1)}) custom-call(s32[1]{0:T(128)} %bitcast.core_ref, bf16[192,512]{1,0:T(8,128)(2,1)S(1)} %get-tuple-element.47.query_ref, bf16[192,512]{1,0:T(8,128)(2,1)S(1)} %get-tuple-element.55.inv_q_ref, ...), custom_call_target="tpu_custom_call" | custom-call | flops 6000000000 | bytes 12000000 | tf_op jit(solution)/shard_map/back/pallas_call | solution.py:480
  20.4 0.6 collective-permute-start.7
  21.0 1.6 %push.1 = (bf16[16,64,384]{2,1,0:T(8,128)(2,1)S(1)}, bf16[2,192,512]{2,1,0:T(8,128)(2,1)S(1)}, bf16[192,512]{1,0:T(8,128)(2,1)S(1)}, f32[192,512]{1,0:T(8,128)S(1)}) custom-call(s32[1]{0:T(128)} %bitcast.core_ref, bf16[512,1536]{1,0:T(8,128)(2,1)S(1)} %copy-done.3, bf16[4,192,128]{2,1,0:T(8,128)(2,1)S(1)} %get-tuple-element.68.gq_ref, ...), custom_call_target="tpu_custom_call" | custom-call | flops 2000000000 | bytes 4000000 | tf_op jit(solution)/shard_map/push/pallas_call | solution.py:494
  23.5 30.2 %all_to_all.10.parts_ref = bf16[16,64,1024]{2,1,0:T(8,128)(2,1)S(1)} all-to-all(bf16[16,64,1024]{2,1,0:T(8,128)(2,1)S(1)} %join.1), channel_id=1, replica_groups={{20,18,22,16,12,10,14,8,28,26,30,24,4,2,6,0},{21,19,23,17,13,11,15,9,29..., dimensions={0} | all-to-all | bytes 4194304 | tf_op jit(solution)/shard_map/all_to_all | solution.py:597
  53.7 0.9 %plane_sum.1 = bf16[64,1024]{1,0:T(8,128)(2,1)} custom-call(bf16[16,64,1024]{2,1,0:T(8,128)(2,1)S(1)} %all_to_all.10.parts_ref), custom_call_target="tpu_custom_call" | custom-call | flops 1000000 | bytes 4000000 | tf_op jit(solution)/shard_map/plane_sum/pallas_call | solution.py:506
  54.6 1.4 %collective-permute-start.8 = (bf16[2,192,512]{2,1,0:T(8,128)(2,1)S(1)}, bf16[2,192,512]{2,1,0:T(8,128)(2,1)S(1)}, u32[]{:S(2)}, u32[]{:S(2)}) collective-permute-start(bf16[2,192,512]{2,1,0:T(8,128)(2,1)S(1)} %get-tuple-element.78), channel_id=1, source_target_pairs={{0,1},{1,0},{2,3},{3,2},{4,5},{5,4},{6,7},{7,6},{8,9},{9,8},{10,11... | collective-permute-start | bytes 1179656 | tf_op jit(solution)/shard_map/ppermute | solution.py:559
  56.0 10.2 %all-to-all-start.1 = ((bf16[8,8,1024]{2,1,0:T(8,128)(2,1)}), bf16[8,8,1024]{2,1,0:T(8,128)(2,1)S(1)}, u32[]{:S(2)}, u32[]{:S(2)}) async-start(bf16[8,8,1024]{2,1,0:T(8,128)(2,1)} %bitcast.7), calls=%async_computation.1 | async-start | bytes 262144 | tf_op jit(solution)/shard_map/all_to_all | solution.py:602
  66.3 1.5 %collective-permute-start.9 = (bf16[192,512]{1,0:T(8,128)(2,1)S(1)}, bf16[192,512]{1,0:T(8,128)(2,1)S(1)}, u32[]{:S(2)}, u32[]{:S(2)}) collective-permute-start(bf16[192,512]{1,0:T(8,128)(2,1)S(1)} %add_x.1), channel_id=1, source_target_pairs={{0,2},{2,0},{1,3},{3,1},{4,6},{6,4},{5,7},{7,5},{8,10},{10,8},{9,1... | collective-permute-start | bytes 589832 | tf_op jit(solution)/shard_map/ppermute | solution.py:600
  67.7 2.8 %all-to-all-done.1 = bf16[8,8,1024]{2,1,0:T(8,128)(2,1)S(1)} async-done(((bf16[8,8,1024]{2,1,0:T(8,128)(2,1)}), bf16[8,8,1024]{2,1,0:T(8,128)(2,1)S(1)}, u32[]{:S(2)}, u32[]{:S(2)}) %all-to-all-start.1) | async-done | bytes 131104 | tf_op jit(solution)/shard_map/all_to_all | solution.py:602
  70.6 1.9 %collective-permute-start.12 = (bf16[8,1024]{1,0:T(8,128)(2,1)S(1)}, bf16[8,1024]{1,0:T(8,128)(2,1)S(1)}, u32[]{:S(2)}, u32[]{:S(2)}) collective-permute-start(bf16[8,1024]{1,0:T(8,128)(2,1)S(1)} %reduce_sum.12.own_ref), channel_id=1, source_target_pairs={{0,3},{3,0},{1,2},{2,1},{4,7},{7,4},{5,6},{6,5},{8,11},{11,8},{9,1... | collective-permute-start | bytes 49160 | tf_op jit(solution)/shard_map/ppermute | solution.py:604
  73.0 1.0 %finish.1 = (bf16[192,512]{1,0:T(8,128)(2,1)}, f32[8,128]{1,0:T(8,128)S(1)}) custom-call(bf16[192,512]{1,0:T(8,128)(2,1)S(1)} %bitcast.12, f32[192,512]{1,0:T(8,128)S(1)} %get-tuple-element.71.own_ref, bf16[2,192,512]{2,1,0:T(8,128)(2,1)S(1)} %collective-permute-done.8.recv_core_ref, bf16[192,512]{1,0:T(8,128)(2,1)S(1)} %collective-permute-done.9.from_x_ref, ...), custom_call_target="tpu_custom_call" | custom-call | flops 1000000 | bytes 4000000 | tf_op jit(solution)/shard_map/finish/pallas_call | solution.py:506
  74.0 1.1 %collective-permute-done.11.x_ref = bf16[8,1024]{1,0:T(8,128)(2,1)S(1)} collective-permute-done((bf16[8,1024]{1,0:T(8,128)(2,1)S(1)}, bf16[8,1024]{1,0:T(8,128)(2,1)S(1)}, u32[]{:S(2)}, u32[]{:S(2)}) %collective-permute-start.11) | collective-permute-done | bytes 16416 | tf_op jit(solution)/shard_map/ppermute | solution.py:604
  75.0 0.7 final.1
  (39 shorter events, 2.2 us)
Async XLA Ops:
  0.6 10.1 %collective-permute-start.1 = (s32[1,3]{1,0:T(1,128)}, s32[1,3]{1,0:T(1,128)S(1)}, u32[]{:S(2)}, u32[]{:S(2)}) collective-permute-start(s32[1,3]{1,0:T(1,128)} %bitcast.15), channel_id=1, source_target_pairs={{0,2},{2,0},{1,3},{3,1},{4,6},{6,4},{5,7},{7,5},{8,10},{10,8},{9,1... | collective-permute-start | bytes 44 | tf_op jit(solution)/shard_map/ppermute | solution.py:567
  2.8 10.0 %collective-permute-start = (s32[1,3]{1,0:T(1,128)}, s32[1,3]{1,0:T(1,128)S(1)}, u32[]{:S(2)}, u32[]{:S(2)}) collective-permute-start(s32[1,3]{1,0:T(1,128)} %bitcast.16), channel_id=1, source_target_pairs={{0,1},{1,0},{2,3},{3,2},{4,5},{5,4},{6,7},{7,6},{8,9},{9,8},{10,11... | collective-permute-start | bytes 44 | tf_op jit(solution)/shard_map/ppermute | solution.py:559
  4.1 7.7 %collective-permute-start.5 = (bf16[192,512]{1,0:T(8,128)(2,1)}, bf16[192,512]{1,0:T(8,128)(2,1)S(1)}, u32[]{:S(2)}, u32[]{:S(2)}) collective-permute-start(bf16[192,512]{1,0:T(8,128)(2,1)} %bitcast.8), channel_id=1, source_target_pairs={{0,1},{1,0},{2,3},{3,2},{4,5},{5,4},{6,7},{7,6},{8,9},{9,8},{10,11... | collective-permute-start | bytes 589832 | tf_op jit(solution)/shard_map/ppermute | solution.py:559
  4.2 7.5 %collective-permute-start.3 = (bf16[192,512]{1,0:T(8,128)(2,1)}, bf16[192,512]{1,0:T(8,128)(2,1)S(1)}, u32[]{:S(2)}, u32[]{:S(2)}) collective-permute-start(bf16[192,512]{1,0:T(8,128)(2,1)} %bitcast.9), channel_id=1, source_target_pairs={{0,2},{2,0},{1,3},{3,1},{4,6},{6,4},{5,7},{7,5},{8,10},{10,8},{9,1... | collective-permute-start | bytes 589832 | tf_op jit(solution)/shard_map/ppermute | solution.py:565
  5.7 1.0 %copy-start = (bf16[3,64,512]{2,1,0:T(8,128)(2,1)S(1)}, bf16[3,64,512]{2,1,0:T(8,128)(2,1)}, u32[]{:S(2)}) copy-start(bf16[3,64,512]{2,1,0:T(8,128)(2,1)} %param.7) | copy-start | bytes 589828
  6.7 1.4 %copy-start.2 = (bf16[512,1536]{1,0:T(8,128)(2,1)S(1)}, bf16[512,1536]{1,0:T(8,128)(2,1)}, u32[]{:S(2)}) copy-start(bf16[512,1536]{1,0:T(8,128)(2,1)} %w_qkv_ref.7) | copy-start | bytes 4718596
  8.1 1.5 %copy-start.5 = (bf16[1024,512]{1,0:T(8,128)(2,1)S(1)}, bf16[1024,512]{1,0:T(8,128)(2,1)}, u32[]{:S(2)}) copy-start(bf16[1024,512]{1,0:T(8,128)(2,1)} %w_down_ref.3) | copy-start | bytes 3145732
  8.1 1.5 %copy-start.7 = (bf16[3,64,512]{2,1,0:T(8,128)(2,1)S(1)}, bf16[3,64,512]{2,1,0:T(8,128)(2,1)}, u32[]{:S(2)}) copy-start(bf16[3,64,512]{2,1,0:T(8,128)(2,1)} %param.13) | copy-start | bytes 589828
  8.1 1.5 %copy-start.8 = (s32[3,1]{0,1:T(1,128)S(1)}, s32[3,1]{0,1:T(1,128)}, u32[]{:S(2)}) copy-start(s32[3,1]{0,1:T(1,128)} %param.8) | copy-start | bytes 40
  9.6 2.2 %copy-start.3 = (bf16[512,1536]{1,0:T(8,128)(2,1)S(1)}, bf16[512,1536]{1,0:T(8,128)(2,1)}, u32[]{:S(2)}) copy-start(bf16[512,1536]{1,0:T(8,128)(2,1)} %w_qkv_ref.7) | copy-start | bytes 4718596
  10.7 2.4 %copy-start.1 = (bf16[3,64,512]{2,1,0:T(8,128)(2,1)S(1)}, bf16[3,64,512]{2,1,0:T(8,128)(2,1)}, u32[]{:S(2)}) copy-start(bf16[3,64,512]{2,1,0:T(8,128)(2,1)} %param.7) | copy-start | bytes 589828
  10.7 2.4 %copy-start.4 = (bf16[512,1024]{1,0:T(8,128)(2,1)S(1)}, bf16[512,1024]{1,0:T(8,128)(2,1)}, u32[]{:S(2)}) copy-start(bf16[512,1024]{1,0:T(8,128)(2,1)} %w_up_ref.1) | copy-start | bytes 3145732
  10.7 2.4 %copy-start.6 = (bf16[512,512]{1,0:T(8,128)(2,1)S(1)}, bf16[512,512]{1,0:T(8,128)(2,1)}, u32[]{:S(2)}) copy-start(bf16[512,512]{1,0:T(8,128)(2,1)} %w_out_ref.1) | copy-start | bytes 1572868
  10.7 2.0 %collective-permute-start.2 = (s32[1,3]{1,0:T(1,128)S(1)}, s32[1,3]{1,0:T(1,128)S(1)}, u32[]{:S(2)}, u32[]{:S(2)}) collective-permute-start(s32[1,3]{1,0:T(1,128)S(1)} %collective-permute-done.1.count2_ref), channel_id=1, source_target_pairs={{0,1},{1,0},{2,3},{3,2},{4,5},{5,4},{6,7},{7,6},{8,9},{9,8},{10,11... | collective-permute-start | bytes 44 | tf_op jit(solution)/shard_map/ppermute | solution.py:559
  11.6 1.4 %collective-permute-start.4 = (bf16[192,512]{1,0:T(8,128)(2,1)S(1)}, bf16[192,512]{1,0:T(8,128)(2,1)S(1)}, u32[]{:S(2)}, u32[]{:S(2)}) collective-permute-start(bf16[192,512]{1,0:T(8,128)(2,1)S(1)} %collective-permute-done.3.tok2_ref), channel_id=1, source_target_pairs={{0,1},{1,0},{2,3},{3,2},{4,5},{5,4},{6,7},{7,6},{8,9},{9,8},{10,11... | collective-permute-start | bytes 589832 | tf_op jit(solution)/shard_map/ppermute | solution.py:559
  13.1 4.8 %copy-start.10 = (bf16[192,512]{1,0:T(8,128)(2,1)S(1)}, bf16[192,512]{1,0:T(8,128)(2,1)}, u32[]{:S(2)}) copy-start(bf16[192,512]{1,0:T(8,128)(2,1)} %copy-done.9) | copy-start | bytes 589828
  17.7 5.2 %collective-permute-start.6 = (bf16[16,64,640]{2,1,0:T(8,128)(2,1)S(1)}, bf16[16,64,640]{2,1,0:T(8,128)(2,1)S(1)}, u32[]{:S(2)}, u32[]{:S(2)}) collective-permute-start(bf16[16,64,640]{2,1,0:T(8,128)(2,1)S(1)} %get-tuple-element.73), channel_id=1, source_target_pairs={{0,1},{1,0},{2,3},{3,2},{4,5},{5,4},{6,7},{7,6},{8,9},{9,8},{10,11... | collective-permute-start | bytes 3932168 | tf_op jit(solution)/shard_map/ppermute | solution.py:559
  20.4 2.6 %collective-permute-start.7 = (bf16[16,64,384]{2,1,0:T(8,128)(2,1)S(1)}, bf16[16,64,384]{2,1,0:T(8,128)(2,1)S(1)}, u32[]{:S(2)}, u32[]{:S(2)}) collective-permute-start(bf16[16,64,384]{2,1,0:T(8,128)(2,1)S(1)} %get-tuple-element.75), channel_id=1, source_target_pairs={{0,1},{1,0},{2,3},{3,2},{4,5},{5,4},{6,7},{7,6},{8,9},{9,8},{10,11... | collective-permute-start | bytes 2359304 | tf_op jit(solution)/shard_map/ppermute | solution.py:559
  54.6 11.6 %collective-permute-start.8 = (bf16[2,192,512]{2,1,0:T(8,128)(2,1)S(1)}, bf16[2,192,512]{2,1,0:T(8,128)(2,1)S(1)}, u32[]{:S(2)}, u32[]{:S(2)}) collective-permute-start(bf16[2,192,512]{2,1,0:T(8,128)(2,1)S(1)} %get-tuple-element.78), channel_id=1, source_target_pairs={{0,1},{1,0},{2,3},{3,2},{4,5},{5,4},{6,7},{7,6},{8,9},{9,8},{10,11... | collective-permute-start | bytes 1179656 | tf_op jit(solution)/shard_map/ppermute | solution.py:559
  56.0 14.6 %all-to-all-start.1 = ((bf16[8,8,1024]{2,1,0:T(8,128)(2,1)}), bf16[8,8,1024]{2,1,0:T(8,128)(2,1)S(1)}, u32[]{:S(2)}, u32[]{:S(2)}) async-start(bf16[8,8,1024]{2,1,0:T(8,128)(2,1)} %bitcast.7), calls=%async_computation.1 | async-start | bytes 262144 | tf_op jit(solution)/shard_map/all_to_all | solution.py:602
  66.3 6.7 %collective-permute-start.9 = (bf16[192,512]{1,0:T(8,128)(2,1)S(1)}, bf16[192,512]{1,0:T(8,128)(2,1)S(1)}, u32[]{:S(2)}, u32[]{:S(2)}) collective-permute-start(bf16[192,512]{1,0:T(8,128)(2,1)S(1)} %add_x.1), channel_id=1, source_target_pairs={{0,2},{2,0},{1,3},{3,1},{4,6},{6,4},{5,7},{7,5},{8,10},{10,8},{9,1... | collective-permute-start | bytes 589832 | tf_op jit(solution)/shard_map/ppermute | solution.py:600
  70.6 3.4 %collective-permute-start.12 = (bf16[8,1024]{1,0:T(8,128)(2,1)S(1)}, bf16[8,1024]{1,0:T(8,128)(2,1)S(1)}, u32[]{:S(2)}, u32[]{:S(2)}) collective-permute-start(bf16[8,1024]{1,0:T(8,128)(2,1)S(1)} %reduce_sum.12.own_ref), channel_id=1, source_target_pairs={{0,3},{3,0},{1,2},{2,1},{4,7},{7,4},{5,6},{6,5},{8,11},{11,8},{9,1... | collective-permute-start | bytes 49160 | tf_op jit(solution)/shard_map/ppermute | solution.py:604
  72.5 2.6 %collective-permute-start.11 = (bf16[8,1024]{1,0:T(8,128)(2,1)S(1)}, bf16[8,1024]{1,0:T(8,128)(2,1)S(1)}, u32[]{:S(2)}, u32[]{:S(2)}) collective-permute-start(bf16[8,1024]{1,0:T(8,128)(2,1)S(1)} %reduce_sum.12.own_ref), channel_id=1, source_target_pairs={{0,2},{2,0},{1,3},{3,1},{4,6},{6,4},{5,7},{7,5},{8,10},{10,8},{9,1... | collective-permute-start | bytes 49160 | tf_op jit(solution)/shard_map/ppermute | solution.py:604
  72.5 2.5 %collective-permute-start.10 = (bf16[8,1024]{1,0:T(8,128)(2,1)S(1)}, bf16[8,1024]{1,0:T(8,128)(2,1)S(1)}, u32[]{:S(2)}, u32[]{:S(2)}) collective-permute-start(bf16[8,1024]{1,0:T(8,128)(2,1)S(1)} %reduce_sum.12.own_ref), channel_id=1, source_target_pairs={{0,1},{1,0},{2,3},{3,2},{4,5},{5,4},{6,7},{7,6},{8,9},{9,8},{10,11... | collective-permute-start | bytes 49160 | tf_op jit(solution)/shard_map/ppermute | solution.py:604
  (1 other events, 0.7 us)
